TPU v7x, 32 devices: a whole 2x2x4 slice. The times are simulated.
32 devices in a mesh: dom: 32 (over z, y, x, core).
Axes of the slice: x: 2, y: 2, z: 4, core: 2. Of those that a mesh axis runs over, the one named last changes fastest.
Arguments:
- features: bfloat16 [8192, 256], P('dom'), may hold values from -48 to 48
- w_query: bfloat16 [256, 256], replicated, may hold values from -0.375 to 0.375
- w_key: bfloat16 [256, 256], replicated, may hold values from -0.375 to 0.375
- w_value: bfloat16 [256, 256], replicated, may hold values from -0.375 to 0.375
- w_out: bfloat16 [256, 256], replicated, may hold values from -0.375 to 0.375
- local_blocks: int32 [64, 4], P('dom'), may hold values from 0 to 3, as said below
- local_count: int32 [64], P('dom'), may hold values from 1 to 4, as said below
- expander_blocks: int32 [4, 64, 2], P(None, 'dom'), may hold values from 0 to 1, as said below
- expander_count: int32 [4, 64], P(None, 'dom'), may hold values from 1 to 2, as said below
Outputs:
- updated: bfloat16 [8192, 256], P('dom')
Inputs may be any that keep to these rules, and one draw needn't show every extreme that they name: `local_blocks`: each row names 4 different positions of the extended range; the row of each partition's first block begins with position 0 and that of its last block with position 3. `local_count`: loads differ from partition to partition; block 0 of every partition uses its partition's largest count. `expander_blocks`: each row names 2 different blocks. `expander_count`: loads differ from partition to partition; block 0 of every partition uses its partition's largest count.
All inputs are finite; a program needn't handle non-finite values.
Results may differ from a plain program's by a relative error of at most 0.0065.
Values may be sent and summed in bfloat16 or wider, within the bound.
No kernel may reach another device: no remote copies, remote signals or barrier semaphores. Data moves between devices by JAX's collectives and lax.ppermute only.
A program may use at most 64 MiB of HBM per device.

v0:
```python
import jax
import jax.numpy as jnp
from jax import lax
from jax.sharding import PartitionSpec as P

HEADS = 8


epsilon = 1e-06


def extended_2(array, sides, width):
    for axis, dim in sides:
        peers, length = (lax.axis_size(axis), array.shape[dim])
        up = [(i, (i + 1) % peers) for i in range(peers)]
        down = [(j, i) for i, j in up]
        last = lax.slice_in_dim(array, length - width, length, axis=dim)
        leading = lax.slice_in_dim(array, 0, width, axis=dim)
        before = lax.ppermute(last, axis, up)
        after = lax.ppermute(leading, axis, down)
        array = jnp.concatenate([before, array, after], axis=dim)
    return array


def partner_2(block, axis, apart):
    count = lax.axis_size(axis)
    route = []
    for low in range(count):
        high = low | 1 << apart
        if high != low and high < count:
            route += [(low, high), (high, low)]
    return lax.ppermute(block, axis, route)


def part_state(queries, kv_blocks, chosen, live_count):
    picked = kv_blocks[chosen]
    slot_count = chosen.shape[0]
    block_rows = kv_blocks.shape[1]
    head_size = queries.shape[-1]
    picked = picked.reshape(slot_count * block_rows, 2, HEADS, head_size)
    key_rows = picked[:, 0]
    values = picked[:, 1]
    scores = jnp.einsum("qhd,khd->hqk", queries, key_rows, preferred_element_type=jnp.float32)
    usable = jnp.arange(slot_count * block_rows, dtype=jnp.int32) // block_rows < live_count
    scores = jnp.where(usable[None, None, :], scores, jnp.float32(-1e30))
    row_max = jnp.max(scores, axis=-1)
    weights = jnp.where(
        usable[None, None, :], jnp.exp(scores - row_max[..., None]), jnp.float32(0.0)
    )
    weights = weights.astype(jnp.bfloat16)
    weight_sum = jnp.sum(weights.astype(jnp.float32), axis=-1)
    context = jnp.einsum("hqk,khd->hqd", weights, values, preferred_element_type=jnp.float32)
    return (row_max, weight_sum, context)


def block_states(queries, kv_blocks, chosen, live_count):
    return jax.vmap(part_state, in_axes=(0, None, 0, 0))(queries, kv_blocks, chosen, live_count)


def combine(states):
    tops = jnp.stack([s[0] for s in states])
    sums = jnp.stack([s[1] for s in states])
    outs = jnp.stack([s[2] for s in states])
    highest = jnp.max(tops, axis=0)
    factor = jnp.exp(tops - highest[None])
    total = jnp.sum(factor * sums, axis=0)
    merged = jnp.sum(factor[..., None] * outs, axis=0)
    return merged / total[..., None]


def shards(
    features,
    w_query,
    w_key,
    w_value,
    w_out,
    local_blocks,
    local_count,
    expander_blocks,
    expander_count,
):
    row_count, feature_width = features.shape
    group_count = local_blocks.shape[0]
    block_rows = row_count // group_count
    head_size = feature_width // HEADS
    scaling = float(head_size) ** (-0.5)
    queries = (jnp.dot(features, w_query, preferred_element_type=jnp.float32) * scaling).astype(
        jnp.bfloat16
    )
    queries = queries.reshape(group_count, block_rows, HEADS, head_size)
    w_pair = jnp.concatenate([w_key, w_value], axis=1)
    pairs = jnp.dot(features, w_pair, preferred_element_type=jnp.float32).astype(jnp.bfloat16)
    padded = extended_2(pairs, (("dom", 0),), block_rows)
    extended = padded.reshape(group_count + 2, block_rows, 2 * feature_width)
    states = [block_states(queries, extended, local_blocks, local_count)]
    levels = lax.axis_size("dom").bit_length() - 1
    match_total = expander_blocks.shape[0]
    for matching in range(match_total):
        swap_bit = matching * levels // match_total
        partner = partner_2(pairs, "dom", swap_bit)
        partner_blocks = partner.reshape(group_count, block_rows, 2 * feature_width)
        states.append(
            block_states(
                queries, partner_blocks, expander_blocks[matching], expander_count[matching]
            )
        )
    merged = combine(states)
    context = (
        jnp.transpose(merged, (0, 2, 1, 3)).reshape(row_count, feature_width).astype(jnp.bfloat16)
    )
    mixed = jnp.dot(context, w_out, preferred_element_type=jnp.float32)
    normed = mixed / jnp.sqrt(jnp.mean(mixed * mixed, axis=-1, keepdims=True) + epsilon)
    return (features.astype(jnp.float32) + normed).astype(jnp.bfloat16)


def solution(mesh):
    in_specs = (
        P("dom", None),
        P(),
        P(),
        P(),
        P(),
        P("dom", None),
        P("dom"),
        P(None, "dom", None),
        P(None, "dom"),
    )
    out_specs = P("dom", None)
    return jax.shard_map(shards, mesh=mesh, in_specs=in_specs, out_specs=out_specs, check_vma=False)
```

profile of v0, /device:TPU:0, one launch (start us, length us, event | category | flops | bytes accessed | tf_op | source)
XLA Modules:
  0.0 52.5 jit_solution(1798220626940901801)
XLA Ops:
  0.0 2.0 %fusion = bf16[256,512]{1,0:T(8,128)(2,1)} fusion(bf16[256,256]{1,0:T(8,128)(2,1)} %param.9, bf16[256,256]{1,0:T(8,128)(2,1)} %param.12, bf16[256,256]{1,0:T(8,128)(2,1)} %param.11), kind=kOutput, calls=%fused_computation.22 | convolution fusion | flops 67764224 | bytes 655360 | tf_op jit(solution)/shard_map/dot_general | solution.py:92
  2.0 0.5 collective-permute-start.2
  2.4 2.5 %collective-permute-start.3 = (bf16[256,512]{1,0:T(8,128)(2,1)}, bf16[256,512]{1,0:T(8,128)(2,1)}, u32[]{:S(2)}, u32[]{:S(2)}) collective-permute-start(bf16[256,512]{1,0:T(8,128)(2,1)} %fusion), channel_id=1, source_target_pairs={{0,2},{2,0},{1,3},{3,1},{4,6},{6,4},{5,7},{7,5},{8,10},{10,8},{9,1... | collective-permute-start | bytes 786440 | tf_op jit(solution)/shard_map/ppermute | solution.py:32
  4.9 1.5 %collective-permute-start.4 = (bf16[256,512]{1,0:T(8,128)(2,1)}, bf16[256,512]{1,0:T(8,128)(2,1)}, u32[]{:S(2)}, u32[]{:S(2)}) collective-permute-start(bf16[256,512]{1,0:T(8,128)(2,1)} %fusion), channel_id=1, source_target_pairs={{0,4},{4,0},{1,5},{5,1},{2,6},{6,2},{3,7},{7,3},{8,12},{12,8},{9,1... | collective-permute-start | bytes 786440 | tf_op jit(solution)/shard_map/ppermute | solution.py:32
  6.5 1.0 %fusion.43 = (bf16[128,512]{1,0:T(8,128)(2,1)S(1)}, bf16[128,512]{1,0:T(8,128)(2,1)S(1)}) fusion(bf16[256,512]{1,0:T(8,128)(2,1)} %fusion), kind=kLoop, calls=%fused_computation.130 | loop fusion | bytes 524288 | tf_op jit(solution)/shard_map/slice | solution.py:17
  7.4 3.1 %collective-permute-start.1 = (bf16[128,512]{1,0:T(8,128)(2,1)S(1)}, bf16[128,512]{1,0:T(8,128)(2,1)S(1)}, u32[]{:S(2)}, u32[]{:S(2)}) collective-permute-start(bf16[128,512]{1,0:T(8,128)(2,1)S(1)} %get-tuple-element.26), channel_id=1, source_target_pairs={{1,0},{2,1},{3,2},{4,3},{5,4},{6,5},{7,6},{8,7},{9,8},{10,9},{11,1... | collective-permute-start | bytes 393224 | tf_op jit(solution)/shard_map/ppermute | solution.py:20
  10.6 0.7 %compare_select_fusion.4 = s32[2,4]{1,0:T(2,128)S(1)} fusion(s32[2,4]{1,0:T(2,128)} %param.14), kind=kLoop, calls=%fused_computation.91 | loop fusion | flops 24 | bytes 64 | tf_op jit(solution)/shard_map/vmap()/select_n | solution.py:36
  11.4 1.2 %fusion.6 = bf16[256,256]{1,0:T(8,128)(2,1)S(1)} fusion(bf16[256,256]{1,0:T(8,128)(2,1)} %param.9, bf16[256,256]{1,0:T(8,128)(2,1)} %param.10), kind=kOutput, calls=%fused_computation.34 | convolution fusion | flops 33685504 | bytes 393216 | tf_op jit(solution)/shard_map/dot_general | solution.py:87
  12.5 1.1 %slice_reduce_fusion = (s32[2,2]{1,0:T(2,128)S(1)}, s32[2,2]{1,0:T(2,128)S(1)}, s32[2,2]{1,0:T(2,128)S(1)}, s32[2,2]{1,0:T(2,128)S(1)}) fusion(s32[4,2,2]{0,2,1:T(2,128)} %param.16), kind=kLoop, calls=%fused_computation.95 | loop fusion | bytes 128 | tf_op jit(solution)/shard_map/slice | solution.py:104
  13.7 0.6 %pad_clamp_fusion.3 = s32[1024]{0:T(1024)} fusion(s32[4]{0:T(128)S(1)} %reshape.401), kind=kLoop, calls=%fused_computation.82 | loop fusion | flops 1024 | bytes 4112 | tf_op jit(solution)/shard_map/vmap()/gather | solution.py:36
  14.3 1.0 %slice_reduce_fusion.4 = (s32[2]{0:T(128)S(1)}, s32[2]{0:T(128)S(1)}, s32[2]{0:T(128)S(1)}, s32[2]{0:T(128)S(1)}) fusion(s32[4,2]{0,1:T(2,128)} %param.17), kind=kLoop, calls=%fused_computation.106 | loop fusion | bytes 64 | tf_op jit(solution)/shard_map/slice | solution.py:104
  15.5 0.6 %pad_clamp_fusion.2 = s32[1024]{0:T(1024)} fusion(s32[4]{0:T(128)S(1)} %reshape.409), kind=kLoop, calls=%fused_computation.81 | loop fusion | flops 1024 | bytes 4112 | tf_op jit(solution)/shard_map/vmap()/gather | solution.py:36
  16.1 0.7 %broadcast_compare_fusion = pred[2,512]{1,0:T(4,128)(4,1)S(1)} fusion(s32[512]{0:T(512)S(1)} %add_select_fusion, s32[2]{0:T(128)} %param.15), kind=kLoop, calls=%fused_computation.102 | loop fusion | flops 1024 | bytes 3080 | tf_op jit(solution)/shard_map/vmap()/lt | solution.py:44
  16.9 0.7 %broadcast_compare_fusion.1 = (pred[2,256]{1,0:T(4,128)(4,1)S(1)}, pred[2,256]{1,0:T(4,128)(4,1)}, pred[2,256]{1,0:T(4,128)(4,1)}, pred[2,256]{1,0:T(4,128)(4,1)}) fusion(s32[256]{0:T(256)S(1)} %and_select_fusion, s32[2]{0:T(128)S(1)} %get-tuple-element.9, s32[2]{0:T(128)S(1)} %get-tuple-element.10, s32[2]{0:T(128)S(1)} %get-tuple-element.12, ...), kind=kLoop, calls=%fused_computation.110 | loop fusion | flops 2048 | bytes 3104 | tf_op jit(solution)/shard_map/vmap()/lt | solution.py:44
  17.5 0.6 %pad_clamp_fusion.1 = s32[1024]{0:T(1024)} fusion(s32[4]{0:T(128)S(1)} %reshape.417), kind=kLoop, calls=%fused_computation.80 | loop fusion | flops 1024 | bytes 4112 | tf_op jit(solution)/shard_map/vmap()/gather | solution.py:36
  18.1 1.0 %copy.58 = bf16[256,256]{0,1:T(8,128)(2,1)S(1)} copy(bf16[256,256]{1,0:T(8,128)(2,1)} %param.9) | data formatting | bytes 262144 | tf_op args[0]
  19.4 0.6 %pad_clamp_fusion = s32[1024]{0:T(1024)} fusion(s32[4]{0:T(128)S(1)} %reshape.425), kind=kLoop, calls=%fused_computation.79 | loop fusion | flops 1024 | bytes 4112 | tf_op jit(solution)/shard_map/vmap()/gather | solution.py:36
  20.0 1.0 %pad_maximum_fusion = bf16[512,512]{1,0:T(8,128)(2,1)S(1)} fusion(bf16[128,512]{1,0:T(8,128)(2,1)S(1)} %collective-permute-done.1, bf16[256,512]{1,0:T(8,128)(2,1)} %fusion, bf16[128,512]{1,0:T(8,128)(2,1)S(1)} %collective-permute-done), kind=kLoop, calls=%fused_computation.35 | loop fusion | flops 1572864 | bytes 1048576 | tf_op jit(solution)/shard_map/concatenate | solution.py:21
  21.0 0.6 %gather_fusion = bf16[8,128,512]{2,1,0:T(8,128)(2,1)S(1)} fusion(bf16[4,128,512]{2,1,0:T(8,128)(2,1)S(1)} %bitcast.133, s32[1024]{0:T(1024)S(1)} %pad_clamp_fusion.4), kind=kCustom, calls=%fused_computation | custom fusion | bytes 2097184 | tf_op jit(solution)/shard_map/vmap()/gather | solution.py:36
  21.6 0.8 %copy.60 = bf16[8,128,512]{1,0,2:T(8,128)(2,1)S(1)} copy(bf16[8,128,512]{2,1,0:T(8,128)(2,1)S(1)} %gather_fusion) | data formatting | bytes 2097152 | tf_op jit(solution)/shard_map/vmap()/gather | solution.py:36
  22.4 0.4 reshape.382
  22.8 0.7 %fusion.38 = (bf16[2,512,1,8,32]{1,0,4,3,2:T(2,128)(2,1)S(1)}, bf16[2,512,1,8,32]{1,0,4,3,2:T(2,128)(2,1)S(1)}) fusion(bf16[2,512,2,8,32]{1,0,4,3,2:T(2,128)(2,1)S(1)} %reshape.382), kind=kLoop, calls=%fused_computation.125 | loop fusion | bytes 2097152 | tf_op jit(solution)/shard_map/vmap()/slice | solution.py:41
  23.6 0.8 %select_reduce_fusion = (f32[2,8,128]{2,1,0:T(8,128)S(1)}, f32[2,8,128,512]{3,2,1,0:T(8,128)S(1)}) fusion(pred[2,512]{1,0:T(4,128)(4,1)S(1)} %broadcast_compare_fusion, bf16[2,512,1,8,32]{1,0,4,3,2:T(2,128)(2,1)S(1)} %get-tuple-element.15, bf16[2,128,8,32]{1,0,3,2:T(2,128)(2,1)S(1)} %reshape.380), kind=kOutput, calls=%fused_computation.7 | convolution fusion | flops 69203968 | bytes 4858880 | tf_op jit(solution)/shard_map/vmap(qhd,khd->hqk)/dot_general | solution.py:43
  24.4 1.2 %convert_reduce_fusion = f32[2,8,128]{2,1,0:T(8,128)S(1)} fusion(f32[2,8,128]{2,1,0:T(8,128)S(1)} %get-tuple-element.31, f32[2,8,128,512]{3,2,1,0:T(8,128)S(1)} %get-tuple-element.32, pred[2,512]{1,0:T(4,128)(4,1)S(1)} %broadcast_compare_fusion), kind=kLoop, calls=%fused_computation.5 | loop fusion | flops 6289408 | bytes 4211712 | tf_op jit(solution)/shard_map/vmap()/reduce_sum | solution.py:51
  25.6 1.3 %fusion.1 = f32[5,2,8,128,32]{3,4,2,1,0:T(8,128)S(1)} fusion(bf16[2,512,1,8,32]{1,0,4,3,2:T(2,128)(2,1)S(1)} %get-tuple-element.16, f32[2,8,128,512]{3,2,1,0:T(8,128)S(1)} %get-tuple-element.32, f32[2,8,128]{2,1,0:T(8,128)S(1)} %get-tuple-element.31, pred[2,512]{1,0:T(4,128)(4,1)S(1)} %broadcast_compare_fusion), kind=kOutput, calls=%fused_computation.24 | convolution fusion | flops 71303168 | bytes 4989952 | tf_op jit(solution)/shard_map/vmap(hqk,khd->hqd)/dot_general | solution.py:52
  26.8 0.6 %constant_dynamic-update-slice_fusion.4 = f32[5,2,8,128]{3,2,1,0:T(8,128)} fusion(f32[2,8,128]{2,1,0:T(8,128)S(1)} %get-tuple-element.31), kind=kLoop, calls=%fused_computation.72 | loop fusion | bytes 16384
  27.4 0.6 %constant_dynamic-update-slice_fusion.9 = f32[5,2,8,128]{3,2,1,0:T(8,128)} fusion(f32[2,8,128]{2,1,0:T(8,128)S(1)} %convert_reduce_fusion), kind=kLoop, calls=%fused_computation.77 | loop fusion | bytes 16384
  28.0 1.7 %gather_fusion.1 = bf16[4,128,512]{2,1,0:T(8,128)(2,1)S(1)} fusion(bf16[2,128,512]{2,1,0:T(8,128)(2,1)} %bitcast.4, s32[1024]{0:T(1024)} %pad_clamp_fusion.3), kind=kCustom, calls=%fused_computation.1 | custom fusion | bytes 1048592 | tf_op jit(solution)/shard_map/vmap()/gather | solution.py:36
  30.3 1.2 %fusion.42 = (bf16[2,256,1,8,32]{1,0,4,3,2:T(2,128)(2,1)S(1)}, bf16[2,256,1,8,32]{1,0,4,3,2:T(2,128)(2,1)}) fusion(bf16[2,256,2,8,32]{1,0,4,3,2:T(2,128)(2,1)S(1)} %reshape.384), kind=kLoop, calls=%fused_computation.129 | loop fusion | bytes 1048576 | tf_op jit(solution)/shard_map/vmap()/slice | solution.py:41
  31.5 1.7 %gather_fusion.2 = bf16[4,128,512]{2,1,0:T(8,128)(2,1)S(1)} fusion(bf16[2,128,512]{2,1,0:T(8,128)(2,1)} %bitcast.7, s32[1024]{0:T(1024)} %pad_clamp_fusion.2), kind=kCustom, calls=%fused_computation.2 | custom fusion | bytes 1048592 | tf_op jit(solution)/shard_map/vmap()/gather | solution.py:36
  33.8 1.2 %fusion.41 = (bf16[2,256,1,8,32]{1,0,4,3,2:T(2,128)(2,1)S(1)}, bf16[2,256,1,8,32]{1,0,4,3,2:T(2,128)(2,1)}) fusion(bf16[2,256,2,8,32]{1,0,4,3,2:T(2,128)(2,1)S(1)} %reshape.386), kind=kLoop, calls=%fused_computation.128 | loop fusion | bytes 1048576 | tf_op jit(solution)/shard_map/vmap()/slice | solution.py:41
  35.0 1.7 %gather_fusion.3 = bf16[4,128,512]{2,1,0:T(8,128)(2,1)S(1)} fusion(bf16[2,128,512]{2,1,0:T(8,128)(2,1)} %bitcast.10, s32[1024]{0:T(1024)} %pad_clamp_fusion.1), kind=kCustom, calls=%fused_computation.3 | custom fusion | bytes 1048592 | tf_op jit(solution)/shard_map/vmap()/gather | solution.py:36
  37.3 1.2 %fusion.40 = (bf16[2,256,1,8,32]{1,0,4,3,2:T(2,128)(2,1)S(1)}, bf16[2,256,1,8,32]{1,0,4,3,2:T(2,128)(2,1)}) fusion(bf16[2,256,2,8,32]{1,0,4,3,2:T(2,128)(2,1)S(1)} %reshape.388), kind=kLoop, calls=%fused_computation.127 | loop fusion | bytes 1048576 | tf_op jit(solution)/shard_map/vmap()/slice | solution.py:41
  38.5 1.7 %gather_fusion.4 = bf16[4,128,512]{2,1,0:T(8,128)(2,1)S(1)} fusion(bf16[2,128,512]{2,1,0:T(8,128)(2,1)} %bitcast.13, s32[1024]{0:T(1024)} %pad_clamp_fusion), kind=kCustom, calls=%fused_computation.4 | custom fusion | bytes 1048592 | tf_op jit(solution)/shard_map/vmap()/gather | solution.py:36
  40.8 0.4 fusion.39
  41.3 1.2 %select_reduce_fusion.4 = (f32[2,8,128]{2,1,0:T(8,128)S(1)}, f32[2,8,128,256]{3,2,1,0:T(8,128)S(1)}) fusion(pred[2,256]{1,0:T(4,128)(4,1)} %get-tuple-element.30, bf16[2,256,1,8,32]{1,0,4,3,2:T(2,128)(2,1)S(1)} %get-tuple-element.23, bf16[2,128,8,32]{1,0,3,2:T(2,128)(2,1)S(1)} %reshape.380), kind=kOutput, calls=%fused_computation.19 | convolution fusion | flops 34600960 | bytes 2499072 | tf_op jit(solution)/shard_map/vmap(qhd,khd->hqk)/dot_general | solution.py:43
  42.5 0.6 %select_reduce_fusion.3 = (f32[2,8,128]{2,1,0:T(8,128)S(1)}, f32[2,8,128,256]{3,2,1,0:T(8,128)S(1)}) fusion(pred[2,256]{1,0:T(4,128)(4,1)S(1)} %copy-done.7, bf16[2,256,1,8,32]{1,0,4,3,2:T(2,128)(2,1)S(1)} %get-tuple-element.21, bf16[2,128,8,32]{1,0,3,2:T(2,128)(2,1)S(1)} %reshape.380), kind=kOutput, calls=%fused_computation.18 | convolution fusion | flops 34600960 | bytes 2499072 | tf_op jit(solution)/shard_map/vmap(qhd,khd->hqk)/dot_general | solution.py:43
  43.1 0.6 %select_reduce_fusion.2 = (f32[2,8,128]{2,1,0:T(8,128)S(1)}, f32[2,8,128,256]{3,2,1,0:T(8,128)S(1)}) fusion(pred[2,256]{1,0:T(4,128)(4,1)S(1)} %copy-done.6, bf16[2,256,1,8,32]{1,0,4,3,2:T(2,128)(2,1)S(1)} %get-tuple-element.19, bf16[2,128,8,32]{1,0,3,2:T(2,128)(2,1)S(1)} %reshape.380), kind=kOutput, calls=%fused_computation.17 | convolution fusion | flops 34600960 | bytes 2499072 | tf_op jit(solution)/shard_map/vmap(qhd,khd->hqk)/dot_general | solution.py:43
  43.7 0.6 %select_reduce_fusion.1 = (f32[2,8,128]{2,1,0:T(8,128)S(1)}, f32[2,8,128,256]{3,2,1,0:T(8,128)S(1)}) fusion(pred[2,256]{1,0:T(4,128)(4,1)S(1)} %get-tuple-element.27, bf16[2,256,1,8,32]{1,0,4,3,2:T(2,128)(2,1)S(1)} %get-tuple-element.17, bf16[2,128,8,32]{1,0,3,2:T(2,128)(2,1)S(1)} %reshape.380), kind=kOutput, calls=%fused_computation.16 | convolution fusion | flops 34600960 | bytes 2499072 | tf_op jit(solution)/shard_map/vmap(qhd,khd->hqk)/dot_general | solution.py:43
  44.2 0.8 %convert_reduce_fusion.4 = f32[2,8,128]{2,1,0:T(8,128)S(1)} fusion(f32[2,8,128]{2,1,0:T(8,128)S(1)} %get-tuple-element.33, f32[2,8,128,256]{3,2,1,0:T(8,128)S(1)} %get-tuple-element.34, pred[2,256]{1,0:T(4,128)(4,1)S(1)} %copy-done.8), kind=kLoop, calls=%fused_computation.11 | loop fusion | flops 3143680 | bytes 2114048 | tf_op jit(solution)/shard_map/vmap()/reduce_sum | solution.py:51
  45.1 0.8 %convert_reduce_fusion.3 = f32[2,8,128]{2,1,0:T(8,128)S(1)} fusion(f32[2,8,128]{2,1,0:T(8,128)S(1)} %get-tuple-element.35, f32[2,8,128,256]{3,2,1,0:T(8,128)S(1)} %get-tuple-element.36, pred[2,256]{1,0:T(4,128)(4,1)S(1)} %copy-done.7), kind=kLoop, calls=%fused_computation.10 | loop fusion | flops 3143680 | bytes 2114048 | tf_op jit(solution)/shard_map/vmap()/reduce_sum | solution.py:51
  45.9 0.8 %convert_reduce_fusion.2 = f32[2,8,128]{2,1,0:T(8,128)S(1)} fusion(f32[2,8,128]{2,1,0:T(8,128)S(1)} %get-tuple-element.37, f32[2,8,128,256]{3,2,1,0:T(8,128)S(1)} %get-tuple-element.38, pred[2,256]{1,0:T(4,128)(4,1)S(1)} %copy-done.6), kind=kLoop, calls=%fused_computation.9 | loop fusion | flops 3143680 | bytes 2114048 | tf_op jit(solution)/shard_map/vmap()/reduce_sum | solution.py:51
  46.8 0.8 %convert_reduce_fusion.1 = f32[2,8,128]{2,1,0:T(8,128)S(1)} fusion(f32[2,8,128]{2,1,0:T(8,128)S(1)} %get-tuple-element.39, f32[2,8,128,256]{3,2,1,0:T(8,128)S(1)} %get-tuple-element.40, pred[2,256]{1,0:T(4,128)(4,1)S(1)} %get-tuple-element.27), kind=kLoop, calls=%fused_computation.8 | loop fusion | flops 3143680 | bytes 2114048 | tf_op jit(solution)/shard_map/vmap()/reduce_sum | solution.py:51
  47.7 0.8 %fusion.5 = f32[5,2,8,128,32]{3,4,2,1,0:T(8,128)S(1)} fusion(f32[5,2,8,128,32]{3,4,2,1,0:T(8,128)S(1)} %fusion.1, bf16[2,256,1,8,32]{1,0,4,3,2:T(2,128)(2,1)S(1)} %copy-done.1, f32[2,8,128,256]{3,2,1,0:T(8,128)S(1)} %get-tuple-element.34, f32[2,8,128]{2,1,0:T(8,128)S(1)} %get-tuple-element.33, pred[2,256]{1,0:T(4,128)(4,1)S(1)} %copy-done.8), kind=kOutput, calls=%fused_computation.33 | convolution fusion | flops 35651584 | bytes 2630656 | tf_op jit(solution)/shard_map/vmap(hqk,khd->hqd)/dot_general | solution.py:52
  48.6 0.8 %fusion.4 = f32[5,2,8,128,32]{3,4,2,1,0:T(8,128)S(1)} fusion(f32[5,2,8,128,32]{3,4,2,1,0:T(8,128)S(1)} %fusion.5, bf16[2,256,1,8,32]{1,0,4,3,2:T(2,128)(2,1)S(1)} %copy-done.2, f32[2,8,128,256]{3,2,1,0:T(8,128)S(1)} %get-tuple-element.36, f32[2,8,128]{2,1,0:T(8,128)S(1)} %get-tuple-element.35, pred[2,256]{1,0:T(4,128)(4,1)S(1)} %copy-done.7), kind=kOutput, calls=%fused_computation.31 | convolution fusion | flops 35651584 | bytes 2630656 | tf_op jit(solution)/shard_map/vmap(hqk,khd->hqd)/dot_general | solution.py:52
  49.5 0.8 %fusion.3 = f32[5,2,8,128,32]{3,4,2,1,0:T(8,128)S(1)} fusion(f32[5,2,8,128,32]{3,4,2,1,0:T(8,128)S(1)} %fusion.4, bf16[2,256,1,8,32]{1,0,4,3,2:T(2,128)(2,1)S(1)} %copy-done.3, f32[2,8,128,256]{3,2,1,0:T(8,128)S(1)} %get-tuple-element.38, f32[2,8,128]{2,1,0:T(8,128)S(1)} %get-tuple-element.37, pred[2,256]{1,0:T(4,128)(4,1)S(1)} %copy-done.6), kind=kOutput, calls=%fused_computation.29 | convolution fusion | flops 35651584 | bytes 2630656 | tf_op jit(solution)/shard_map/vmap(hqk,khd->hqd)/dot_general | solution.py:52
  50.2 0.8 %fusion.2 = f32[5,2,8,128,32]{3,4,2,1,0:T(8,128)S(1)} fusion(f32[5,2,8,128,32]{3,4,2,1,0:T(8,128)S(1)} %fusion.3, bf16[2,256,1,8,32]{1,0,4,3,2:T(2,128)(2,1)S(1)} %get-tuple-element.18, f32[2,8,128,256]{3,2,1,0:T(8,128)S(1)} %get-tuple-element.40, f32[2,8,128]{2,1,0:T(8,128)S(1)} %get-tuple-element.39, pred[2,256]{1,0:T(4,128)(4,1)S(1)} %get-tuple-element.27), kind=kOutput, calls=%fused_computation.27 | convolution fusion | flops 35651584 | bytes 2630656 | tf_op jit(solution)/shard_map/vmap(hqk,khd->hqd)/dot_general | solution.py:52
  51.8 0.8 %copy.81 = bf16[256,256]{1,0:T(8,128)(2,1)} copy(bf16[256,256]{0,1:T(8,128)(2,1)S(1)} %add_convert_fusion) | data formatting | bytes 262144 | tf_op jit(solution)/shard_map/convert_element_type | solution.py:113
  (62 shorter events, 4.2 us)
Async XLA Ops:
  0.0 51.4 %copy-start = (bf16[256,256]{1,0:T(8,128)(2,1)S(1)}, bf16[256,256]{1,0:T(8,128)(2,1)}, u32[]{:S(2)}) copy-start(bf16[256,256]{1,0:T(8,128)(2,1)} %param.13) | copy-start | bytes 393220
  2.0 26.0 %collective-permute-start.2 = (bf16[256,512]{1,0:T(8,128)(2,1)}, bf16[256,512]{1,0:T(8,128)(2,1)}, u32[]{:S(2)}, u32[]{:S(2)}) collective-permute-start(bf16[256,512]{1,0:T(8,128)(2,1)} %fusion), channel_id=1, source_target_pairs={{0,1},{1,0},{2,3},{3,2},{4,5},{5,4},{6,7},{7,6},{8,9},{9,8},{10,11... | collective-permute-start | bytes 786440 | tf_op jit(solution)/shard_map/ppermute | solution.py:32
  2.4 29.1 %collective-permute-start.3 = (bf16[256,512]{1,0:T(8,128)(2,1)}, bf16[256,512]{1,0:T(8,128)(2,1)}, u32[]{:S(2)}, u32[]{:S(2)}) collective-permute-start(bf16[256,512]{1,0:T(8,128)(2,1)} %fusion), channel_id=1, source_target_pairs={{0,2},{2,0},{1,3},{3,1},{4,6},{6,4},{5,7},{7,5},{8,10},{10,8},{9,1... | collective-permute-start | bytes 786440 | tf_op jit(solution)/shard_map/ppermute | solution.py:32
  4.9 30.1 %collective-permute-start.4 = (bf16[256,512]{1,0:T(8,128)(2,1)}, bf16[256,512]{1,0:T(8,128)(2,1)}, u32[]{:S(2)}, u32[]{:S(2)}) collective-permute-start(bf16[256,512]{1,0:T(8,128)(2,1)} %fusion), channel_id=1, source_target_pairs={{0,4},{4,0},{1,5},{5,1},{2,6},{6,2},{3,7},{7,3},{8,12},{12,8},{9,1... | collective-permute-start | bytes 786440 | tf_op jit(solution)/shard_map/ppermute | solution.py:32
  7.4 12.5 %collective-permute-start.1 = (bf16[128,512]{1,0:T(8,128)(2,1)S(1)}, bf16[128,512]{1,0:T(8,128)(2,1)S(1)}, u32[]{:S(2)}, u32[]{:S(2)}) collective-permute-start(bf16[128,512]{1,0:T(8,128)(2,1)S(1)} %get-tuple-element.26), channel_id=1, source_target_pairs={{1,0},{2,1},{3,2},{4,3},{5,4},{6,5},{7,6},{8,7},{9,8},{10,9},{11,1... | collective-permute-start | bytes 393224 | tf_op jit(solution)/shard_map/ppermute | solution.py:20
  10.6 9.4 %collective-permute-start = (bf16[128,512]{1,0:T(8,128)(2,1)S(1)}, bf16[128,512]{1,0:T(8,128)(2,1)S(1)}, u32[]{:S(2)}, u32[]{:S(2)}) collective-permute-start(bf16[128,512]{1,0:T(8,128)(2,1)S(1)} %get-tuple-element.25), channel_id=1, source_target_pairs={{0,1},{1,2},{2,3},{3,4},{4,5},{5,6},{6,7},{7,8},{8,9},{9,10},{10,1... | collective-permute-start | bytes 393224 | tf_op jit(solution)/shard_map/ppermute | solution.py:19
  20.0 18.6 %collective-permute-start.5 = (bf16[256,512]{1,0:T(8,128)(2,1)}, bf16[256,512]{1,0:T(8,128)(2,1)}, u32[]{:S(2)}, u32[]{:S(2)}) collective-permute-start(bf16[256,512]{1,0:T(8,128)(2,1)} %fusion), channel_id=1, source_target_pairs={{0,8},{8,0},{1,9},{9,1},{2,10},{10,2},{3,11},{11,3},{4,12},{12,4},... | collective-permute-start | bytes 786440 | tf_op jit(solution)/shard_map/ppermute | solution.py:32
  40.8 1.7 %copy-start.7 = (pred[2,256]{1,0:T(4,128)(4,1)S(1)}, pred[2,256]{1,0:T(4,128)(4,1)}, u32[]{:S(2)}) copy-start(pred[2,256]{1,0:T(4,128)(4,1)} %get-tuple-element.28) | copy-start | bytes 1540
  41.2 1.8 %copy-start.6 = (pred[2,256]{1,0:T(4,128)(4,1)S(1)}, pred[2,256]{1,0:T(4,128)(4,1)}, u32[]{:S(2)}) copy-start(pred[2,256]{1,0:T(4,128)(4,1)} %get-tuple-element.29) | copy-start | bytes 1540
  43.1 1.1 %copy-start.8 = (pred[2,256]{1,0:T(4,128)(4,1)S(1)}, pred[2,256]{1,0:T(4,128)(4,1)}, u32[]{:S(2)}) copy-start(pred[2,256]{1,0:T(4,128)(4,1)} %get-tuple-element.30) | copy-start | bytes 1540
  45.9 1.7 %copy-start.5 = (f32[5,2,8,128]{3,2,1,0:T(8,128)S(1)}, f32[5,2,8,128]{3,2,1,0:T(8,128)}, u32[]{:S(2)}) copy-start(f32[5,2,8,128]{3,2,1,0:T(8,128)} %constant_dynamic-update-slice_fusion.4) | copy-start | bytes 122884
  45.9 1.8 %copy-start.1 = (bf16[2,256,1,8,32]{1,0,4,3,2:T(2,128)(2,1)S(1)}, bf16[2,256,1,8,32]{1,0,4,3,2:T(2,128)(2,1)}, u32[]{:S(2)}) copy-start(bf16[2,256,1,8,32]{1,0,4,3,2:T(2,128)(2,1)} %get-tuple-element.24) | copy-start | bytes 786436
  47.6 1.0 %copy-start.2 = (bf16[2,256,1,8,32]{1,0,4,3,2:T(2,128)(2,1)S(1)}, bf16[2,256,1,8,32]{1,0,4,3,2:T(2,128)(2,1)}, u32[]{:S(2)}) copy-start(bf16[2,256,1,8,32]{1,0,4,3,2:T(2,128)(2,1)} %get-tuple-element.22) | copy-start | bytes 786436
  48.5 1.0 %copy-start.3 = (bf16[2,256,1,8,32]{1,0,4,3,2:T(2,128)(2,1)S(1)}, bf16[2,256,1,8,32]{1,0,4,3,2:T(2,128)(2,1)}, u32[]{:S(2)}) copy-start(bf16[2,256,1,8,32]{1,0,4,3,2:T(2,128)(2,1)} %get-tuple-element.20) | copy-start | bytes 786436
  50.2 0.8 %copy-start.4 = (f32[5,2,8,128]{3,2,1,0:T(8,128)S(1)}, f32[5,2,8,128]{3,2,1,0:T(8,128)}, u32[]{:S(2)}) copy-start(f32[5,2,8,128]{3,2,1,0:T(8,128)} %constant_dynamic-update-slice_fusion.9) | copy-start | bytes 122884
where the time goes:
time: 53.4 us; the launch traced here: 52.5 us
  local copies, waits for them, and re-layouts  22.7 us (43%)
  matrix products  11.5 us (22%)
  other arithmetic  10.3 us (19%)
  starting transfers between devices  7.58 us (14%)
    gather x10, local copies, waits for them, and re-layouts, part_state(): picked = kv_blocks[chosen]  9.22 us
    slice x5, local copies, waits for them, and re-layouts, part_state(): key_rows = picked[:, 0]  4.65 us
    reduce_sum x5, other arithmetic, part_state(): weight_sum = jnp.sum(weights.astype(jnp.float32), axis=-1)  4.5 us
    ppermute x4, starting transfers between devices, partner_2(): return lax.ppermute(block, axis, route)  4.46 us
    dot_general x5, matrix products, part_state(): jnp.einsum('hqk,khd->hqd', weights, values, preferred_element_type=jnp.fl...  4.31 us
    dot_general x5, matrix products, part_state(): jnp.einsum('qhd,khd->hqk', queries, key_rows, preferred_element_type=jnp....  3.77 us
    ppermute x1, starting transfers between devices, extended_2(): after = lax.ppermute(leading, axis, down)  3.12 us
    unnamed x27, local copies, waits for them, and re-layouts  2.49 us
  transfers between devices with their start and end apart: 6, of which 0 were waited for; matrix products, arithmetic and copies ran while one was open for 55% of the time, Pallas kernels for 0%

commit v1 on v0

v1 whole, which is shorter than its diff:
```python
import functools

import jax
import jax.numpy as jnp
from jax import lax
from jax.experimental import pallas as pl
from jax.experimental.pallas import tpu as pltpu
from jax.sharding import PartitionSpec as P

HEADS = 8
EPSILON = 1e-06
LOW = -1e30
HIGH = 1e30

VMEM = pl.BlockSpec(memory_space=pltpu.VMEM)
SMEM = pl.BlockSpec(memory_space=pltpu.SMEM)


def matmul(a, b):
    return jnp.dot(a, b, preferred_element_type=jnp.float32)


def matmul_nt(a, b):
    return lax.dot_general(a, b, (((1,), (1,)), ((), ())), preferred_element_type=jnp.float32)


def head_of(queries_t, head):
    rows, columns = queries_t.shape
    size = rows // HEADS
    parts = []
    if head:
        parts.append(jnp.zeros((head * size, columns), queries_t.dtype))
    parts.append(queries_t[head * size : (head + 1) * size])
    if head < HEADS - 1:
        parts.append(jnp.zeros(((HEADS - 1 - head) * size, columns), queries_t.dtype))
    return jnp.concatenate(parts, axis=0)


def lanes_of_blocks(values, block_rows):
    return jnp.concatenate([jnp.full((1, block_rows), v, jnp.float32) for v in values], axis=1)


def key_value(features, w_key, w_value_t):
    keys = matmul(features, w_key).astype(jnp.bfloat16)
    values_t = matmul_nt(w_value_t, features).astype(jnp.bfloat16)
    return keys, values_t


def part_states(queries_t, parts, block_rows):
    size = queries_t.shape[0] // HEADS
    states = []
    for head in range(HEADS):
        own = head_of(queries_t, head)
        scores = []
        top = None
        for keys, values_t, uses in parts:
            part_scores = matmul(keys, own)
            for b, use in enumerate(uses):
                block = part_scores[b * block_rows : (b + 1) * block_rows]
                scores.append((block, use))
                block_top = jnp.where(use > 0, jnp.max(block, axis=0, keepdims=True), LOW)
                top = block_top if top is None else jnp.maximum(top, block_top)
        i = 0
        out = None
        for keys, values_t, uses in parts:
            weights = []
            for use in uses:
                block, use = scores[i]
                i += 1
                shift = jnp.where(use > 0, top, HIGH)
                weights.append((jnp.exp(block - shift) * use).astype(jnp.bfloat16))
            weights = jnp.concatenate(weights, axis=0)
            left = jnp.concatenate(
                [values_t[head * size : (head + 1) * size], jnp.ones((16, values_t.shape[1]), jnp.bfloat16)], axis=0
            )
            term = matmul(left, weights)
            out = term if out is None else out + term
        states.append((top, out[size : size + 1], out[:size]))
    return states


def uses_of(blocks_ref, count_ref, position, group_count, most, block_rows, lead=()):
    values = []
    for g in range(group_count):
        total = jnp.int32(0)
        for j in range(most):
            hit = (blocks_ref[(*lead, g, j)] == position) & (j < count_ref[(*lead, g)])
            total = total + hit.astype(jnp.int32)
        values.append(total.astype(jnp.float32))
    return lanes_of_blocks(values, block_rows)


def own_kernel(
    features, w_query, w_key, w_value, w_out, local_blocks, local_count,
    queries_t, w_value_t, w_out_t, tops, sums, outs,
):
    group_count, most = local_blocks.shape
    block_rows = features.shape[0] // group_count
    size = features.shape[1] // HEADS
    scaling = float(size) ** (-0.5)
    x = features[...]
    queries = (matmul(x, w_query[...]) * scaling).astype(jnp.bfloat16)
    q_t = queries.T
    v_t = w_value[...].T
    queries_t[...] = q_t
    w_value_t[...] = v_t
    w_out_t[...] = w_out[...].T
    keys, values_t = key_value(x, w_key[...], v_t)
    uses = [
        uses_of(local_blocks, local_count, 1 + b, group_count, most, block_rows)
        for b in range(group_count)
    ]
    for head, (top, total, out) in enumerate(part_states(q_t, [(keys, values_t, uses)], block_rows)):
        tops[head : head + 1] = top
        sums[head : head + 1] = total
        outs[head * size : (head + 1) * size] = out


def rest_kernel(
    features, by_core, by_1, by_2, by_3, ring,
    w_key, queries_t, w_value_t, w_out_t, tops, sums, outs,
    local_blocks, local_count, expander_blocks, expander_count, odd,
    result,
):
    group_count, most = local_blocks.shape
    most_far = expander_blocks.shape[2]
    block_rows = features.shape[0] // group_count
    size = features.shape[1] // HEADS
    w_k, v_t, q_t = w_key[...], w_value_t[...], queries_t[...]
    is_odd = odd[0]
    far = functools.partial(
        uses_of, expander_blocks, expander_count, group_count=group_count, most=most_far, block_rows=block_rows
    )
    near = functools.partial(
        uses_of, local_blocks, local_count, group_count=group_count, most=most, block_rows=block_rows
    )
    before = near(0)
    after = near(group_count + 1)
    parts = []
    for m, ref in enumerate((by_core, by_1, by_2, by_3)):
        keys, values_t = key_value(ref[...], w_k, v_t)
        uses = [far(b, lead=(m,)) for b in range(group_count)]
        if m == 0:
            uses[0] = uses[0] + jnp.where(is_odd == 0, after, 0.0)
            uses[-1] = uses[-1] + jnp.where(is_odd == 0, 0.0, before)
        parts.append((keys, values_t, uses))
    keys, values_t = key_value(ring[...], w_k, v_t)
    parts.append((keys, values_t, [jnp.where(is_odd == 0, before, after)]))
    context = []
    for head, (top, total, out) in enumerate(part_states(q_t, parts, block_rows)):
        first_top = tops[head : head + 1]
        highest = jnp.maximum(first_top, top)
        first = jnp.exp(first_top - highest)
        second = jnp.exp(top - highest)
        total = first * sums[head : head + 1] + second * total
        out = first * outs[head * size : (head + 1) * size] + second * out
        context.append((out / total).astype(jnp.bfloat16))
    context = jnp.concatenate(context, axis=0)
    mixed = matmul(w_out_t[...], context)
    normed = mixed * lax.rsqrt(jnp.mean(mixed * mixed, axis=0, keepdims=True) + EPSILON)
    result[...] = (features[...].astype(jnp.float32) + normed.T).astype(result.dtype)


def shards(
    features,
    w_query,
    w_key,
    w_value,
    w_out,
    local_blocks,
    local_count,
    expander_blocks,
    expander_count,
):
    rows, width = features.shape
    group_count = local_blocks.shape[0]
    block_rows = rows // group_count
    peers = lax.axis_size("dom")
    levels = peers.bit_length() - 1
    match_total = expander_blocks.shape[0]
    odd = lax.axis_index("dom") % 2
    arrived = []
    for matching in range(match_total):
        apart = 1 << (matching * levels // match_total)
        arrived.append(lax.ppermute(features, "dom", [(i, i ^ apart) for i in range(peers)]))
    edge = lax.dynamic_slice_in_dim(features, odd * (rows - block_rows), block_rows, axis=0)
    ring = lax.ppermute(
        edge, "dom", [(i, (i + 1) % peers if i % 2 else (i - 1) % peers) for i in range(peers)]
    )
    wide = jax.ShapeDtypeStruct((width, width), jnp.bfloat16)
    rows8 = jax.ShapeDtypeStruct((HEADS, rows), jnp.float32)
    queries_t, w_value_t, w_out_t, tops, sums, outs = pl.pallas_call(
        own_kernel,
        out_shape=(
            jax.ShapeDtypeStruct((width, rows), jnp.bfloat16),
            wide,
            wide,
            rows8,
            rows8,
            jax.ShapeDtypeStruct((width, rows), jnp.float32),
        ),
        in_specs=[VMEM] * 5 + [SMEM] * 2,
        out_specs=(VMEM,) * 6,
        compiler_params=pltpu.CompilerParams(vmem_limit_bytes=32 * 2**20),
        name="own",
    )(features, w_query, w_key, w_value, w_out, local_blocks, local_count)
    return pl.pallas_call(
        rest_kernel,
        out_shape=jax.ShapeDtypeStruct((rows, width), features.dtype),
        in_specs=[VMEM] * 13 + [SMEM] * 5,
        out_specs=VMEM,
        compiler_params=pltpu.CompilerParams(vmem_limit_bytes=32 * 2**20),
        name="rest",
    )(
        features, *arrived, ring, w_key, queries_t, w_value_t, w_out_t, tops, sums, outs,
        local_blocks, local_count, expander_blocks, expander_count, odd.reshape(1),
    )


def solution(mesh):
    in_specs = (
        P("dom", None),
        P(),
        P(),
        P(),
        P(),
        P("dom", None),
        P("dom"),
        P(None, "dom", None),
        P(None, "dom"),
    )
    out_specs = P("dom", None)
    return jax.shard_map(shards, mesh=mesh, in_specs=in_specs, out_specs=out_specs, check_vma=False)
```

time: 53.4 us -> 22.9 us (0.43); the launches traced: 52.5 us -> 22.7 us
  local copies, waits for them, and re-layouts: 22.7 us -> 5.27 us
  matrix products: 11.5 us -> 0 us
  other arithmetic: 10.3 us -> 0 us
  Pallas kernels: 0 us -> 8.82 us
  starting transfers between devices: 7.58 us -> 8.52 us
    dot_general x13 -> x0, matrix products: 11.5 us -> none  [the longest x5 4.31 us: part_state(): jnp.einsum('hqk,khd->hqd', weights, values, preferred_element_type=jnp.fl...]
    gather x10 -> x0, local copies, waits for them, and re-layouts: 9.22 us -> none  [part_state(): picked = kv_blocks[chosen]]
    pallas_call x0 -> x2, Pallas kernels: none -> 8.82 us  [the longest x1 5.84 us: shards(): pl.pallas_call(rest_kernel, out_shape=jax.ShapeDtypeStruct((rows, width),...]
    slice x8 -> x0, local copies, waits for them, and re-layouts: 7.8 us -> none  [the longest x5 4.65 us: part_state(): key_rows = picked[:, 0]]
    reduce_sum x7 -> x0, other arithmetic: 4.69 us -> none  [the longest x5 4.5 us: part_state(): weight_sum = jnp.sum(weights.astype(jnp.float32), axis=-1)]
    gather x5 -> x0, other arithmetic: 2.41 us -> none  [part_state(): picked = kv_blocks[chosen]]
    unnamed x27 -> x20, local copies, waits for them, and re-layouts: 2.49 us -> 4.4 us
    reshape x6 -> x0, local copies, waits for them, and re-layouts: 1.81 us -> none  [the longest x5 1.77 us: part_state(): picked = picked.reshape(slot_count * block_rows, 2, HEADS, head_size)]
  transfers between devices with their start and end apart: 6 -> 5, of which waited for: 0 -> 0; matrix products, arithmetic and copies ran while one was open for 55% -> 5% of each run, Pallas kernels for 0% -> 13%
where the time goes in v1:
time: 22.9 us; the launch traced here: 22.7 us
  Pallas kernels  8.82 us (39%)
  starting transfers between devices  8.52 us (37%)
  local copies, waits for them, and re-layouts  5.27 us (23%)
    ppermute x4, starting transfers between devices, shards(): lax.ppermute(features, 'dom', [(i, i ^ apart) for i in range(peers)])  6.04 us
    pallas_call x1, Pallas kernels, shards(): pl.pallas_call(rest_kernel, out_shape=jax.ShapeDtypeStruct((rows, width),...  5.84 us
    unnamed x20, local copies, waits for them, and re-layouts  4.4 us
    pallas_call x1, Pallas kernels, shards(): pl.pallas_call(own_kernel, out_shape=(jax.ShapeDtypeStruct((width, rows),...  2.98 us
    ppermute x1, starting transfers between devices, shards(): lax.ppermute(edge, 'dom', [(i, (i + 1) % peers if i % 2 else (i - 1) % pe...  2.49 us
    dynamic_slice x1, local copies, waits for them, and re-layouts, shards(): lax.dynamic_slice_in_dim(features, odd * (rows - block_rows), block_rows,...  0.87 us
  transfers between devices with their start and end apart: 5, of which 0 were waited for; matrix products, arithmetic and copies ran while one was open for 5% of the time, Pallas kernels for 13%

profile of v1, /device:TPU:0, one launch (start us, length us, event | category | flops | bytes accessed | tf_op | source)
XLA Modules:
  0.0 22.7 jit_solution(18185848360411707201)
XLA Ops:
  0.0 0.0 copy-start
  0.0 3.0 %collective-permute-start.3 = (bf16[256,256]{1,0:T(8,128)(2,1)}, bf16[256,256]{1,0:T(8,128)(2,1)S(1)}, u32[]{:S(2)}, u32[]{:S(2)}) collective-permute-start(bf16[256,256]{1,0:T(8,128)(2,1)} %features.3), channel_id=1, source_target_pairs={{0,8},{1,9},{2,10},{3,11},{4,12},{5,13},{6,14},{7,15},{8,0},{9,1},... | collective-permute-start | bytes 393224 | tf_op jit(solution)/shard_map/ppermute | solution.py:185
  3.0 1.5 %collective-permute-start.2 = (bf16[256,256]{1,0:T(8,128)(2,1)}, bf16[256,256]{1,0:T(8,128)(2,1)S(1)}, u32[]{:S(2)}, u32[]{:S(2)}) collective-permute-start(bf16[256,256]{1,0:T(8,128)(2,1)} %features.3), channel_id=1, source_target_pairs={{0,4},{1,5},{2,6},{3,7},{4,0},{5,1},{6,2},{7,3},{8,12},{9,13},{10,... | collective-permute-start | bytes 393224 | tf_op jit(solution)/shard_map/ppermute | solution.py:185
  4.5 1.5 %collective-permute-start.1 = (bf16[256,256]{1,0:T(8,128)(2,1)}, bf16[256,256]{1,0:T(8,128)(2,1)S(1)}, u32[]{:S(2)}, u32[]{:S(2)}) collective-permute-start(bf16[256,256]{1,0:T(8,128)(2,1)} %features.3), channel_id=1, source_target_pairs={{0,2},{1,3},{2,0},{3,1},{4,6},{5,7},{6,4},{7,5},{8,10},{9,11},{10,... | collective-permute-start | bytes 393224 | tf_op jit(solution)/shard_map/ppermute | solution.py:185
  6.0 0.0 collective-permute-start
  6.0 0.0 copy-start.8
  6.0 0.9 %constant_dynamic-slice_fusion = bf16[128,256]{1,0:T(8,128)(2,1)S(1)} fusion(bf16[256,256]{1,0:T(8,128)(2,1)} %features.3, s32[]{:T(128)S(6)} %select_n.11), kind=kLoop, calls=%fused_computation | loop fusion | bytes 131076 | tf_op jit(solution)/shard_map/dynamic_slice | solution.py:186
  6.9 0.0 copy-start.7
  6.9 2.5 %collective-permute-start.4 = (bf16[128,256]{1,0:T(8,128)(2,1)S(1)}, bf16[128,256]{1,0:T(8,128)(2,1)S(1)}, u32[]{:S(2)}, u32[]{:S(2)}) collective-permute-start(bf16[128,256]{1,0:T(8,128)(2,1)S(1)} %constant_dynamic-slice_fusion), channel_id=1, source_target_pairs={{0,31},{1,2},{2,1},{3,4},{4,3},{5,6},{6,5},{7,8},{8,7},{9,10},{10,... | collective-permute-start | bytes 196616 | tf_op jit(solution)/shard_map/ppermute | solution.py:187
  9.4 0.0 copy-done.8
  9.4 0.1 copy.11.expander_count
  9.5 0.0 copy-done.7
  9.5 0.0 copy-start.5
  9.5 0.0 copy-start.6
  9.5 0.1 copy.10.expander_blocks
  9.6 0.0 copy-done
  9.6 0.6 %copy-done.5 = s32[2,4]{1,0:T(2,128)S(1)} copy-done((s32[2,4]{1,0:T(2,128)S(1)}, s32[2,4]{1,0:T(2,128)}, u32[]{:S(2)}) %copy-start.5) | copy-done | bytes 56
  10.2 0.0 copy-done.6
  10.2 0.0 copy-start.1
  10.2 0.9 %copy-done.1 = bf16[256,256]{1,0:T(8,128)(2,1)S(1)} copy-done((bf16[256,256]{1,0:T(8,128)(2,1)S(1)}, bf16[256,256]{1,0:T(8,128)(2,1)}, u32[]{:S(2)}) %copy-start.1) | copy-done | bytes 131096
  11.1 0.0 copy-start.2
  11.1 0.9 %copy-done.2 = bf16[256,256]{1,0:T(8,128)(2,1)S(1)} copy-done((bf16[256,256]{1,0:T(8,128)(2,1)S(1)}, bf16[256,256]{1,0:T(8,128)(2,1)}, u32[]{:S(2)}) %copy-start.2) | copy-done | bytes 131096
  12.0 0.0 copy-start.3
  12.0 0.9 %copy-done.3 = bf16[256,256]{1,0:T(8,128)(2,1)S(1)} copy-done((bf16[256,256]{1,0:T(8,128)(2,1)S(1)}, bf16[256,256]{1,0:T(8,128)(2,1)}, u32[]{:S(2)}) %copy-start.3) | copy-done | bytes 131096
  12.9 0.0 copy-start.4
  12.9 0.9 %copy-done.4 = bf16[256,256]{1,0:T(8,128)(2,1)S(1)} copy-done((bf16[256,256]{1,0:T(8,128)(2,1)S(1)}, bf16[256,256]{1,0:T(8,128)(2,1)}, u32[]{:S(2)}) %copy-start.4) | copy-done | bytes 131096
  13.8 3.0 %own.1 = (bf16[256,256]{1,0:T(8,128)(2,1)S(1)}, bf16[256,256]{1,0:T(8,128)(2,1)S(1)}, bf16[256,256]{1,0:T(8,128)(2,1)S(1)}, f32[8,256]{1,0:T(8,128)S(1)}, f32[8,256]{1,0:T(8,128)S(1)}, /*index=5*/f32[256,256]{1,0:T(8,128)S(1)}) custom-call(bf16[256,256]{1,0:T(8,128)(2,1)S(1)} %copy-done, bf16[256,256]{1,0:T(8,128)(2,1)S(1)} %copy-done.2, ...), custom_call_target="tpu_custom_call" | custom-call | tf_op jit(solution)/shard_map/own/pallas_call | solution.py:192
  16.8 0.0 collective-permute-done.4.ring
  16.8 0.0 collective-permute-done.3.by_3
  16.8 0.0 collective-permute-done.2.by_2
  16.8 0.0 collective-permute-done.1.by_1
  16.8 0.0 collective-permute-done.by_core
  16.8 5.8 %rest.1 = bf16[256,256]{1,0:T(8,128)(2,1)} custom-call(bf16[256,256]{1,0:T(8,128)(2,1)S(1)} %copy-done, bf16[256,256]{1,0:T(8,128)(2,1)S(1)} %collective-permute-done.by_core, bf16[256,256]{1,0:T(8,128)(2,1)S(1)} %collective-permute-done.1.by_1, bf16[256,256]{1,0:T(8,128)(2,1)S(1)} %collective-permute-done.2.by_2, ...), custom_call_target="tpu_custom_call" | custom-call | tf_op jit(solution)/shard_map/rest/pallas_call | solution.py:207
Async XLA Ops:
  0.0 9.6 %copy-start = (bf16[256,256]{1,0:T(8,128)(2,1)S(1)}, bf16[256,256]{1,0:T(8,128)(2,1)}, u32[]{:S(2)}) copy-start(bf16[256,256]{1,0:T(8,128)(2,1)} %features.3) | copy-start | bytes 393220
  0.0 16.8 %collective-permute-start.3 = (bf16[256,256]{1,0:T(8,128)(2,1)}, bf16[256,256]{1,0:T(8,128)(2,1)S(1)}, u32[]{:S(2)}, u32[]{:S(2)}) collective-permute-start(bf16[256,256]{1,0:T(8,128)(2,1)} %features.3), channel_id=1, source_target_pairs={{0,8},{1,9},{2,10},{3,11},{4,12},{5,13},{6,14},{7,15},{8,0},{9,1},... | collective-permute-start | bytes 393224 | tf_op jit(solution)/shard_map/ppermute | solution.py:185
  3.0 13.8 %collective-permute-start.2 = (bf16[256,256]{1,0:T(8,128)(2,1)}, bf16[256,256]{1,0:T(8,128)(2,1)S(1)}, u32[]{:S(2)}, u32[]{:S(2)}) collective-permute-start(bf16[256,256]{1,0:T(8,128)(2,1)} %features.3), channel_id=1, source_target_pairs={{0,4},{1,5},{2,6},{3,7},{4,0},{5,1},{6,2},{7,3},{8,12},{9,13},{10,... | collective-permute-start | bytes 393224 | tf_op jit(solution)/shard_map/ppermute | solution.py:185
  4.5 12.3 %collective-permute-start.1 = (bf16[256,256]{1,0:T(8,128)(2,1)}, bf16[256,256]{1,0:T(8,128)(2,1)S(1)}, u32[]{:S(2)}, u32[]{:S(2)}) collective-permute-start(bf16[256,256]{1,0:T(8,128)(2,1)} %features.3), channel_id=1, source_target_pairs={{0,2},{1,3},{2,0},{3,1},{4,6},{5,7},{6,4},{7,5},{8,10},{9,11},{10,... | collective-permute-start | bytes 393224 | tf_op jit(solution)/shard_map/ppermute | solution.py:185
  6.0 10.8 %collective-permute-start = (bf16[256,256]{1,0:T(8,128)(2,1)}, bf16[256,256]{1,0:T(8,128)(2,1)S(1)}, u32[]{:S(2)}, u32[]{:S(2)}) collective-permute-start(bf16[256,256]{1,0:T(8,128)(2,1)} %features.3), channel_id=1, source_target_pairs={{0,1},{1,0},{2,3},{3,2},{4,5},{5,4},{6,7},{7,6},{8,9},{9,8},{10,11... | collective-permute-start | bytes 393224 | tf_op jit(solution)/shard_map/ppermute | solution.py:185
  6.0 3.4 %copy-start.8 = (s32[4,2]{0,1:T(2,128)S(1)}, s32[4,2]{0,1:T(2,128)}, u32[]{:S(2)}) copy-start(s32[4,2]{0,1:T(2,128)} %param.17) | copy-start | bytes 100
  6.9 2.6 %copy-start.7 = (s32[4,2,2]{0,2,1:T(2,128)S(1)}, s32[4,2,2]{0,2,1:T(2,128)}, u32[]{:S(2)}) copy-start(s32[4,2,2]{0,2,1:T(2,128)} %param.16) | copy-start | bytes 196
  6.9 9.9 %collective-permute-start.4 = (bf16[128,256]{1,0:T(8,128)(2,1)S(1)}, bf16[128,256]{1,0:T(8,128)(2,1)S(1)}, u32[]{:S(2)}, u32[]{:S(2)}) collective-permute-start(bf16[128,256]{1,0:T(8,128)(2,1)S(1)} %constant_dynamic-slice_fusion), channel_id=1, source_target_pairs={{0,31},{1,2},{2,1},{3,4},{4,3},{5,6},{6,5},{7,8},{8,7},{9,10},{10,... | collective-permute-start | bytes 196616 | tf_op jit(solution)/shard_map/ppermute | solution.py:187
  9.5 0.7 %copy-start.5 = (s32[2,4]{1,0:T(2,128)S(1)}, s32[2,4]{1,0:T(2,128)}, u32[]{:S(2)}) copy-start(s32[2,4]{1,0:T(2,128)} %local_blocks.3) | copy-start | bytes 100
  9.5 0.7 %copy-start.6 = (s32[2]{0:T(128)S(1)}, s32[2]{0:T(128)}, u32[]{:S(2)}) copy-start(s32[2]{0:T(128)} %local_count.3) | copy-start | bytes 28
  10.2 0.9 %copy-start.1 = (bf16[256,256]{1,0:T(8,128)(2,1)S(1)}, bf16[256,256]{1,0:T(8,128)(2,1)}, u32[]{:S(2)}) copy-start(bf16[256,256]{1,0:T(8,128)(2,1)} %w_key.3) | copy-start | bytes 393220
  11.1 0.9 %copy-start.2 = (bf16[256,256]{1,0:T(8,128)(2,1)S(1)}, bf16[256,256]{1,0:T(8,128)(2,1)}, u32[]{:S(2)}) copy-start(bf16[256,256]{1,0:T(8,128)(2,1)} %w_query.1) | copy-start | bytes 393220
  12.0 0.9 %copy-start.3 = (bf16[256,256]{1,0:T(8,128)(2,1)S(1)}, bf16[256,256]{1,0:T(8,128)(2,1)}, u32[]{:S(2)}) copy-start(bf16[256,256]{1,0:T(8,128)(2,1)} %w_value.1) | copy-start | bytes 393220
  12.9 0.9 %copy-start.4 = (bf16[256,256]{1,0:T(8,128)(2,1)S(1)}, bf16[256,256]{1,0:T(8,128)(2,1)}, u32[]{:S(2)}) copy-start(bf16[256,256]{1,0:T(8,128)(2,1)} %w_out.1) | copy-start | bytes 393220

commit v2 on v0

v2 whole, which is shorter than its diff:
```python
import jax
import jax.numpy as jnp
from jax import lax
from jax.experimental import pallas as pl
from jax.experimental.pallas import tpu as pltpu
from jax.sharding import PartitionSpec as P

HEADS = 8
EPSILON = 1e-06
LOW = -1e30

VMEM = pl.BlockSpec(memory_space=pltpu.VMEM)
ANY = pl.BlockSpec(memory_space=pl.ANY)

ORDER = tuple(range(0, HEADS, 2)) + tuple(range(1, HEADS, 2))


def matmul(a, b):
    return jnp.dot(a, b, preferred_element_type=jnp.float32)


def matmul_nt(a, b):
    return lax.dot_general(a, b, (((1,), (1,)), ((), ())), preferred_element_type=jnp.float32)


def lane_heads(width):
    return lax.broadcasted_iota(jnp.int32, (1, width), 1) // (width // HEADS)


def used(blocks, count, position, most):
    total = jnp.int32(0)
    for j in range(most):
        total = total + ((blocks(j) == position) & (j < count)).astype(jnp.int32)
    return total


def along_keys(values, block_rows):
    return jnp.concatenate([jnp.full((1, block_rows), v, jnp.float32) for v in values], axis=1)


def attend(queries, parts, groups):
    rows, width = queries.shape
    heads = lane_heads(width)
    zero = jnp.zeros((), queries.dtype)
    one = jnp.ones((), queries.dtype)
    masked = jnp.concatenate([jnp.where(heads == h, queries, zero) for h in ORDER], axis=0)

    def by_group(array):
        return array.reshape(HEADS, groups, rows // groups, array.shape[-1])

    scores = []
    top = None
    for keys, _, bias, _ in parts:
        part = by_group(matmul_nt(masked, keys)) + bias[None, :, None, :]
        part = part.reshape(HEADS * rows, keys.shape[0])
        scores.append(part)
        part_top = jnp.max(part, axis=1, keepdims=True)
        top = part_top if top is None else jnp.maximum(top, part_top)
    half = HEADS * rows // 2
    first = second = None
    for part, (keys, values, _, times) in zip(scores, parts):
        weights = jnp.exp(part - top)
        if times is not None:
            weights = (by_group(weights) * times[None, :, None, :]).reshape(HEADS * rows, keys.shape[0])
        weights = weights.astype(jnp.bfloat16)
        even = matmul(weights[:half], jnp.where(heads % 2 == 0, values, one))
        odd = matmul(weights[half:], jnp.where(heads % 2 == 1, values, one))
        first = even if first is None else first + even
        second = odd if second is None else second + odd
    tops = out = sums = jnp.zeros((rows, width), jnp.float32)
    for i, h in enumerate(ORDER):
        source, at = (first, i) if i < HEADS // 2 else (second, i - HEADS // 2)
        block = source[at * rows : (at + 1) * rows]
        out = jnp.where(heads == h, block, out)
        sums = jnp.where(heads == (h ^ 1), block, sums)
        tops = jnp.where(heads == h, top[i * rows : (i + 1) * rows], tops)
    size = width // HEADS
    sums = jnp.where(heads % 2 == 0, pltpu.roll(sums, width - size, axis=1), pltpu.roll(sums, size, axis=1))
    return tops, out, sums


def merge(one, other):
    top = jnp.maximum(one[0], other[0])
    left, right = jnp.exp(one[0] - top), jnp.exp(other[0] - top)
    return top, left * one[1] + right * other[1], left * one[2] + right * other[2]


def key_value(features, w_key, w_value):
    return matmul(features, w_key).astype(jnp.bfloat16), matmul(features, w_value).astype(jnp.bfloat16)


def own_kernel(
    features, w_query, w_key, w_value, w_out, local_blocks, local_count, expander_blocks, expander_count,
    x, key_copy, value_copy, out_copy, queries, bias, times, tops, outs, sums,
    query_copy, blocks, count, far_blocks, far_count, sems,
):
    pairs = (
        (features, x), (w_query, query_copy), (w_key, key_copy), (w_value, value_copy), (local_blocks, blocks),
        (local_count, count), (expander_blocks, far_blocks), (expander_count, far_count), (w_out, out_copy),
    )
    copies = [pltpu.make_async_copy(a, b, sems.at[i]) for i, (a, b) in enumerate(pairs)]
    for copy in copies:
        copy.start()
    groups, most = blocks.shape
    most_far, matchings = far_blocks.shape[1:]
    block_rows = x.shape[0] // groups
    size = x.shape[1] // HEADS
    is_odd = lax.rem(lax.axis_index("dom"), 2) == 1
    for copy in copies[4:8]:
        copy.wait()
    for g in range(groups):
        near = [used(lambda j: blocks[g, j], count[g], position, most) for position in range(groups + 2)]
        takes = [near[1:-1]]
        for m in range(matchings):
            takes.append(
                [used(lambda j: far_blocks[g, j, m], far_count[g, m], b, most_far) for b in range(groups)]
            )
        takes[1][0] = takes[1][0] + jnp.where(is_odd, 0, near[-1])
        takes[1][-1] = takes[1][-1] + jnp.where(is_odd, near[0], 0)
        takes.append([jnp.where(is_odd, near[-1], near[0])] * groups)
        for p, take in enumerate(takes):
            bias[p, g : g + 1, :] = along_keys([jnp.where(t > 0, 0.0, LOW) for t in take], block_rows)
        times[g : g + 1, :] = along_keys([t.astype(jnp.float32) for t in takes[1]], block_rows)
    for copy in copies[:4]:
        copy.wait()
    own = x[...]
    q = (matmul(own, query_copy[...]) * (float(size) ** -0.5)).astype(jnp.bfloat16)
    queries[...] = q
    keys, values = key_value(own, key_copy[...], value_copy[...])
    tops[...], outs[...], sums[...] = attend(q, [(keys, values, bias[0], None)], groups)
    copies[8].wait()


def middle_kernel(
    by_core, by_1, by_2, w_key, w_value, queries, bias, times, tops, outs, sums,
    new_tops, new_outs, new_sums,
):
    groups = times.shape[0]
    parts = []
    for m, ref in enumerate((by_core, by_1, by_2)):
        keys, values = key_value(ref[...], w_key[...], w_value[...])
        parts.append((keys, values, bias[1 + m], times[...] if m == 0 else None))
    state = attend(queries[...], parts, groups)
    new_tops[...], new_outs[...], new_sums[...] = merge((tops[...], outs[...], sums[...]), state)


def last_kernel(
    features, by_3, ring, w_key, w_value, w_out, queries, bias, tops, outs, sums,
    result,
):
    groups = bias.shape[1]
    block_rows = features.shape[0] // groups
    odd = lax.rem(lax.axis_index("dom"), 2)
    keys, values = key_value(by_3[...], w_key[...], w_value[...])
    parts = [(keys, values, bias[4], None)]
    edge = ring[pl.ds(pl.multiple_of((1 - odd) * ((groups - 1) * block_rows), block_rows), block_rows), :]
    keys, values = key_value(edge, w_key[...], w_value[...])
    parts.append((keys, values, bias[5][:, :block_rows], None))
    _, out, total = merge((tops[...], outs[...], sums[...]), attend(queries[...], parts, groups))
    context = (out / total).astype(jnp.bfloat16)
    mixed = matmul(context, w_out[...])
    normed = mixed * lax.rsqrt(jnp.mean(mixed * mixed, axis=1, keepdims=True) + EPSILON)
    result[...] = (features[...].astype(jnp.float32) + normed).astype(result.dtype)


def shards(
    features,
    w_query,
    w_key,
    w_value,
    w_out,
    local_blocks,
    local_count,
    expander_blocks,
    expander_count,
):
    rows, width = features.shape
    peers = lax.axis_size("dom")
    levels = peers.bit_length() - 1
    match_total = expander_blocks.shape[0]
    arrived = []
    for matching in range(match_total):
        apart = 1 << (matching * levels // match_total)
        arrived.append(lax.ppermute(features, "dom", [(i, i ^ apart) for i in range(peers)]))
    by_core, by_1, by_2, by_3 = arrived
    ring = lax.ppermute(
        features, "dom", [(i, (i + 1) % peers if i % 2 else (i - 1) % peers) for i in range(peers)]
    )
    params = pltpu.CompilerParams(vmem_limit_bytes=48 * 2**20)
    groups = local_blocks.shape[0]
    wide = jax.ShapeDtypeStruct((width, width), jnp.bfloat16)
    small = jax.ShapeDtypeStruct((rows, width), jnp.bfloat16)
    state = jax.ShapeDtypeStruct((rows, width), jnp.float32)
    far_blocks, far_count = jnp.transpose(expander_blocks, (1, 2, 0)), jnp.transpose(expander_count)
    tables = (local_blocks, local_count, far_blocks, far_count)
    inputs = (features, w_query, w_key, w_value, w_out, *tables)
    x, w_key, w_value, w_out, queries, bias, times, *states = pl.pallas_call(
        own_kernel,
        out_shape=(
            small, wide, wide, wide, small,
            jax.ShapeDtypeStruct((match_total + 2, groups, rows), jnp.float32),
            jax.ShapeDtypeStruct((groups, rows), jnp.float32),
            state, state, state,
        ),
        in_specs=[ANY] * len(inputs),
        out_specs=(VMEM,) * 10,
        scratch_shapes=[
            pltpu.VMEM((width, width), jnp.bfloat16),
            *(pltpu.SMEM(t.shape, jnp.int32) for t in tables),
            pltpu.SemaphoreType.DMA((len(inputs),)),
        ],
        compiler_params=params,
        name="own",
    )(*(pltpu.with_memory_space_constraint(a, pltpu.HBM) for a in inputs))
    states = pl.pallas_call(
        middle_kernel,
        out_shape=(state,) * 3,
        in_specs=[VMEM] * 11,
        out_specs=(VMEM,) * 3,
        compiler_params=params,
        name="middle",
    )(by_core, by_1, by_2, w_key, w_value, queries, bias, times, *states)
    return pl.pallas_call(
        last_kernel,
        out_shape=jax.ShapeDtypeStruct((rows, width), features.dtype),
        in_specs=[VMEM] * 11,
        out_specs=VMEM,
        compiler_params=params,
        name="last",
    )(x, by_3, ring, w_key, w_value, w_out, queries, bias, *states)


def solution(mesh):
    in_specs = (
        P("dom", None),
        P(),
        P(),
        P(),
        P(),
        P("dom", None),
        P("dom"),
        P(None, "dom", None),
        P(None, "dom"),
    )
    out_specs = P("dom", None)
    return jax.shard_map(shards, mesh=mesh, in_specs=in_specs, out_specs=out_specs, check_vma=False)
```

time: 53.4 us -> 17.1 us (0.32); the launches traced: 52.5 us -> 17 us
  local copies, waits for them, and re-layouts: 22.7 us -> 0 us
  matrix products: 11.5 us -> 0 us
  other arithmetic: 10.3 us -> 0 us
  Pallas kernels: 0 us -> 8.73 us
    dot_general x13 -> x0, matrix products: 11.5 us -> none  [the longest x5 4.31 us: part_state(): jnp.einsum('hqk,khd->hqd', weights, values, preferred_element_type=jnp.fl...]
    gather x10 -> x0, local copies, waits for them, and re-layouts: 9.22 us -> none  [part_state(): picked = kv_blocks[chosen]]
    pallas_call x0 -> x3, Pallas kernels: none -> 8.73 us  [the longest x1 3.53 us: shards(): pl.pallas_call(middle_kernel, out_shape=(state,) * 3, in_specs=[VMEM] * 1...]
    slice x8 -> x0, local copies, waits for them, and re-layouts: 7.8 us -> none  [the longest x5 4.65 us: part_state(): key_rows = picked[:, 0]]
    reduce_sum x7 -> x0, other arithmetic: 4.69 us -> none  [the longest x5 4.5 us: part_state(): weight_sum = jnp.sum(weights.astype(jnp.float32), axis=-1)]
    unnamed x27 -> x0, local copies, waits for them, and re-layouts: 2.49 us -> none
    gather x5 -> x0, other arithmetic: 2.41 us -> none  [part_state(): picked = kv_blocks[chosen]]
    reshape x6 -> x0, local copies, waits for them, and re-layouts: 1.81 us -> none  [the longest x5 1.77 us: part_state(): picked = picked.reshape(slot_count * block_rows, 2, HEADS, head_size)]
  transfers between devices with their start and end apart: 6 -> 5, of which waited for: 0 -> 1; matrix products, arithmetic and copies ran while one was open for 55% -> 0% of each run, Pallas kernels for 0% -> 35%
where the time goes in v2:
time: 17.1 us; the launch traced here: 17 us
  Pallas kernels  8.73 us (51%)
  starting transfers between devices  7.7 us (45%)
  waiting for transfers between devices  0.5 us (3%)
    ppermute x4, starting transfers between devices, shards(): lax.ppermute(features, 'dom', [(i, i ^ apart) for i in range(peers)])  6.04 us
    pallas_call x1, Pallas kernels, shards(): pl.pallas_call(middle_kernel, out_shape=(state,) * 3, in_specs=[VMEM] * 1...  3.53 us
    pallas_call x1, Pallas kernels, shards(): pl.pallas_call(last_kernel, out_shape=jax.ShapeDtypeStruct((rows, width),...  2.74 us
    pallas_call x1, Pallas kernels, shards(): pl.pallas_call(own_kernel, out_shape=(small, wide, wide, wide, small, jax...  2.46 us
    ppermute x1, starting transfers between devices, shards(): lax.ppermute(features, 'dom', [(i, (i + 1) % peers if i % 2 else (i - 1)...  1.66 us
    ppermute x1, waiting for transfers between devices, shards(): lax.ppermute(features, 'dom', [(i, (i + 1) % peers if i % 2 else (i - 1)...  0.49 us
  transfers between devices with their start and end apart: 5, of which 1 were waited for; matrix products, arithmetic and copies ran while one was open for 0% of the time, Pallas kernels for 35%

profile of v2, /device:TPU:0, one launch (start us, length us, event | category | flops | bytes accessed | tf_op | source)
XLA Modules:
  0.0 17.0 jit_solution(13611687964372954096)
XLA Ops:
  0.0 0.5 %collective-permute-start.2 = (bf16[256,256]{1,0:T(8,128)(2,1)}, bf16[256,256]{1,0:T(8,128)(2,1)S(1)}, u32[]{:S(2)}, u32[]{:S(2)}) collective-permute-start(bf16[256,256]{1,0:T(8,128)(2,1)} %features.1), channel_id=1, source_target_pairs={{0,1},{1,0},{2,3},{3,2},{4,5},{5,4},{6,7},{7,6},{8,9},{9,8},{10,11... | collective-permute-start | bytes 393224 | tf_op jit(solution)/shard_map/ppermute | solution.py:184
  0.5 2.5 %collective-permute-start.3 = (bf16[256,256]{1,0:T(8,128)(2,1)}, bf16[256,256]{1,0:T(8,128)(2,1)S(1)}, u32[]{:S(2)}, u32[]{:S(2)}) collective-permute-start(bf16[256,256]{1,0:T(8,128)(2,1)} %features.1), channel_id=1, source_target_pairs={{0,2},{1,3},{2,0},{3,1},{4,6},{5,7},{6,4},{7,5},{8,10},{9,11},{10,... | collective-permute-start | bytes 393224 | tf_op jit(solution)/shard_map/ppermute | solution.py:184
  2.9 1.5 %collective-permute-start.4 = (bf16[256,256]{1,0:T(8,128)(2,1)}, bf16[256,256]{1,0:T(8,128)(2,1)S(1)}, u32[]{:S(2)}, u32[]{:S(2)}) collective-permute-start(bf16[256,256]{1,0:T(8,128)(2,1)} %features.1), channel_id=1, source_target_pairs={{0,4},{1,5},{2,6},{3,7},{4,0},{5,1},{6,2},{7,3},{8,12},{9,13},{10,... | collective-permute-start | bytes 393224 | tf_op jit(solution)/shard_map/ppermute | solution.py:184
  4.5 1.6 %collective-permute-start = (bf16[256,256]{1,0:T(8,128)(2,1)}, bf16[256,256]{1,0:T(8,128)(2,1)S(1)}, u32[]{:S(2)}, u32[]{:S(2)}) collective-permute-start(bf16[256,256]{1,0:T(8,128)(2,1)} %features.1), channel_id=1, source_target_pairs={{0,8},{1,9},{2,10},{3,11},{4,12},{5,13},{6,14},{7,15},{8,0},{9,1},... | collective-permute-start | bytes 393224 | tf_op jit(solution)/shard_map/ppermute | solution.py:184
  6.0 1.7 %collective-permute-start.1 = (bf16[256,256]{1,0:T(8,128)(2,1)}, bf16[256,256]{1,0:T(8,128)(2,1)S(1)}, u32[]{:S(2)}, u32[]{:S(2)}) collective-permute-start(bf16[256,256]{1,0:T(8,128)(2,1)} %features.1), channel_id=1, source_target_pairs={{0,31},{1,2},{2,1},{3,4},{4,3},{5,6},{6,5},{7,8},{8,7},{9,10},{10,... | collective-permute-start | bytes 393224 | tf_op jit(solution)/shard_map/ppermute | solution.py:186
  7.7 2.5 %own.1 = (bf16[256,256]{1,0:T(8,128)(2,1)S(1)}, bf16[256,256]{1,0:T(8,128)(2,1)S(1)}, bf16[256,256]{1,0:T(8,128)(2,1)S(1)}, bf16[256,256]{1,0:T(8,128)(2,1)S(1)}...) custom-call(bf16[256,256]{1,0:T(8,128)(2,1)} %features.1, ...), custom_call_target="tpu_custom_call" | custom-call | tf_op jit(solution)/shard_map/own/pallas_call | solution.py:197
  10.2 0.0 collective-permute-done.2.by_core
  10.2 0.0 collective-permute-done.3.by_1
  10.2 0.0 collective-permute-done.4.by_2
  10.2 3.5 %middle.1 = (f32[256,256]{1,0:T(8,128)S(1)}, f32[256,256]{1,0:T(8,128)S(1)}, f32[256,256]{1,0:T(8,128)S(1)}) custom-call(bf16[256,256]{1,0:T(8,128)(2,1)S(1)} %collective-permute-done.2.by_core, bf16[256,256]{1,0:T(8,128)(2,1)S(1)} %collective-permute-done.3.by_1, bf16[256,256]{1,0:T(8,128)(2,1)S(1)} %collective-permute-done.4.by_2, ...), custom_call_target="tpu_custom_call" | custom-call | tf_op jit(solution)/shard_map/middle/pallas_call | solution.py:215
  13.7 0.0 collective-permute-done.by_3
  13.7 0.5 %collective-permute-done.1.ring = bf16[256,256]{1,0:T(8,128)(2,1)S(1)} collective-permute-done((bf16[256,256]{1,0:T(8,128)(2,1)}, bf16[256,256]{1,0:T(8,128)(2,1)S(1)}, u32[]{:S(2)}, u32[]{:S(2)}) %collective-permute-start.1) | collective-permute-done | bytes 131104 | tf_op jit(solution)/shard_map/ppermute | solution.py:186
  14.2 2.7 %last.1 = bf16[256,256]{1,0:T(8,128)(2,1)} custom-call(bf16[256,256]{1,0:T(8,128)(2,1)S(1)} %get-tuple-element.18.features, bf16[256,256]{1,0:T(8,128)(2,1)S(1)} %collective-permute-done.by_3, bf16[256,256]{1,0:T(8,128)(2,1)S(1)} %collective-permute-done.1.ring, bf16[256,256]{1,0:T(8,128)(2,1)S(1)} %get-tuple-element.19.w_key, ...), custom_call_target="tpu_custom_call" | custom-call | tf_op jit(solution)/shard_map/last/pallas_call | solution.py:223
Async XLA Ops:
  0.0 10.2 %collective-permute-start.2 = (bf16[256,256]{1,0:T(8,128)(2,1)}, bf16[256,256]{1,0:T(8,128)(2,1)S(1)}, u32[]{:S(2)}, u32[]{:S(2)}) collective-permute-start(bf16[256,256]{1,0:T(8,128)(2,1)} %features.1), channel_id=1, source_target_pairs={{0,1},{1,0},{2,3},{3,2},{4,5},{5,4},{6,7},{7,6},{8,9},{9,8},{10,11... | collective-permute-start | bytes 393224 | tf_op jit(solution)/shard_map/ppermute | solution.py:184
  0.5 9.7 %collective-permute-start.3 = (bf16[256,256]{1,0:T(8,128)(2,1)}, bf16[256,256]{1,0:T(8,128)(2,1)S(1)}, u32[]{:S(2)}, u32[]{:S(2)}) collective-permute-start(bf16[256,256]{1,0:T(8,128)(2,1)} %features.1), channel_id=1, source_target_pairs={{0,2},{1,3},{2,0},{3,1},{4,6},{5,7},{6,4},{7,5},{8,10},{9,11},{10,... | collective-permute-start | bytes 393224 | tf_op jit(solution)/shard_map/ppermute | solution.py:184
  2.9 7.2 %collective-permute-start.4 = (bf16[256,256]{1,0:T(8,128)(2,1)}, bf16[256,256]{1,0:T(8,128)(2,1)S(1)}, u32[]{:S(2)}, u32[]{:S(2)}) collective-permute-start(bf16[256,256]{1,0:T(8,128)(2,1)} %features.1), channel_id=1, source_target_pairs={{0,4},{1,5},{2,6},{3,7},{4,0},{5,1},{6,2},{7,3},{8,12},{9,13},{10,... | collective-permute-start | bytes 393224 | tf_op jit(solution)/shard_map/ppermute | solution.py:184
  4.5 9.3 %collective-permute-start = (bf16[256,256]{1,0:T(8,128)(2,1)}, bf16[256,256]{1,0:T(8,128)(2,1)S(1)}, u32[]{:S(2)}, u32[]{:S(2)}) collective-permute-start(bf16[256,256]{1,0:T(8,128)(2,1)} %features.1), channel_id=1, source_target_pairs={{0,8},{1,9},{2,10},{3,11},{4,12},{5,13},{6,14},{7,15},{8,0},{9,1},... | collective-permute-start | bytes 393224 | tf_op jit(solution)/shard_map/ppermute | solution.py:184
  6.0 8.2 %collective-permute-start.1 = (bf16[256,256]{1,0:T(8,128)(2,1)}, bf16[256,256]{1,0:T(8,128)(2,1)S(1)}, u32[]{:S(2)}, u32[]{:S(2)}) collective-permute-start(bf16[256,256]{1,0:T(8,128)(2,1)} %features.1), channel_id=1, source_target_pairs={{0,31},{1,2},{2,1},{3,4},{4,3},{5,6},{6,5},{7,8},{8,7},{9,10},{10,... | collective-permute-start | bytes 393224 | tf_op jit(solution)/shard_map/ppermute | solution.py:186

commit v3 on v2

--- a/solution.py
+++ b/solution.py
@@ -51,20 +51,20 @@
     scores = []
     top = None
     for keys, _, bias, _ in parts:
-        part = by_group(matmul_nt(masked, keys)) + bias[None, :, None, :]
-        part = part.reshape(HEADS * rows, keys.shape[0])
+        part = by_group(matmul_nt(masked, keys())) + bias()[None, :, None, :]
+        part = part.reshape(HEADS * rows, part.shape[-1])
         scores.append(part)
         part_top = jnp.max(part, axis=1, keepdims=True)
         top = part_top if top is None else jnp.maximum(top, part_top)
     half = HEADS * rows // 2
     first = second = None
-    for part, (keys, values, _, times) in zip(scores, parts):
+    for part, (_, values, _, times) in zip(scores, parts):
         weights = jnp.exp(part - top)
         if times is not None:
-            weights = (by_group(weights) * times[None, :, None, :]).reshape(HEADS * rows, keys.shape[0])
+            weights = (by_group(weights) * times()[None, :, None, :]).reshape(part.shape)
         weights = weights.astype(jnp.bfloat16)
-        even = matmul(weights[:half], jnp.where(heads % 2 == 0, values, one))
-        odd = matmul(weights[half:], jnp.where(heads % 2 == 1, values, one))
+        even = matmul(weights[:half], jnp.where(heads % 2 == 0, values(), one))
+        odd = matmul(weights[half:], jnp.where(heads % 2 == 1, values(), one))
         first = even if first is None else first + even
         second = odd if second is None else second + odd
     tops = out = sums = jnp.zeros((rows, width), jnp.float32)
@@ -85,14 +85,21 @@
     return top, left * one[1] + right * other[1], left * one[2] + right * other[2]
 
 
-def key_value(features, w_key, w_value):
-    return matmul(features, w_key).astype(jnp.bfloat16), matmul(features, w_value).astype(jnp.bfloat16)
+def project(features, w_key, w_value, keys, values, start):
+    rows = pl.ds(start, features.shape[0])
+    keys[rows, :] = matmul(features, w_key[...]).astype(keys.dtype)
+    values[rows, :] = matmul(features, w_value[...]).astype(values.dtype)
+
+
+def part_at(keys, values, start, rows, bias, times=None):
+    where = pl.ds(start, rows)
+    return lambda: keys[where, :], lambda: values[where, :], bias, times
 
 
 def own_kernel(
     features, w_query, w_key, w_value, w_out, local_blocks, local_count, expander_blocks, expander_count,
     x, key_copy, value_copy, out_copy, queries, bias, times, tops, outs, sums,
-    query_copy, blocks, count, far_blocks, far_count, sems,
+    query_copy, keys, values, blocks, count, far_blocks, far_count, sems,
 ):
     pairs = (
         (features, x), (w_query, query_copy), (w_key, key_copy), (w_value, value_copy), (local_blocks, blocks),
@@ -126,20 +133,25 @@
     own = x[...]
     q = (matmul(own, query_copy[...]) * (float(size) ** -0.5)).astype(jnp.bfloat16)
     queries[...] = q
-    keys, values = key_value(own, key_copy[...], value_copy[...])
-    tops[...], outs[...], sums[...] = attend(q, [(keys, values, bias[0], None)], groups)
+    project(own, key_copy, value_copy, keys, values, 0)
+    parts = [part_at(keys, values, 0, own.shape[0], lambda: bias[0])]
+    tops[...], outs[...], sums[...] = attend(q, parts, groups)
     copies[8].wait()
 
 
 def middle_kernel(
     by_core, by_1, by_2, w_key, w_value, queries, bias, times, tops, outs, sums,
     new_tops, new_outs, new_sums,
+    keys, values,
 ):
     groups = times.shape[0]
+    rows = by_core.shape[0]
     parts = []
     for m, ref in enumerate((by_core, by_1, by_2)):
-        keys, values = key_value(ref[...], w_key[...], w_value[...])
-        parts.append((keys, values, bias[1 + m], times[...] if m == 0 else None))
+        project(ref[...], w_key, w_value, keys, values, m * rows)
+        parts.append(
+            part_at(keys, values, m * rows, rows, lambda m=m: bias[1 + m], (lambda: times[...]) if m == 0 else None)
+        )
     state = attend(queries[...], parts, groups)
     new_tops[...], new_outs[...], new_sums[...] = merge((tops[...], outs[...], sums[...]), state)
 
@@ -147,15 +159,19 @@
 def last_kernel(
     features, by_3, ring, w_key, w_value, w_out, queries, bias, tops, outs, sums,
     result,
+    keys, values,
 ):
     groups = bias.shape[1]
-    block_rows = features.shape[0] // groups
+    rows = features.shape[0]
+    block_rows = rows // groups
     odd = lax.rem(lax.axis_index("dom"), 2)
-    keys, values = key_value(by_3[...], w_key[...], w_value[...])
-    parts = [(keys, values, bias[4], None)]
+    project(by_3[...], w_key, w_value, keys, values, 0)
     edge = ring[pl.ds(pl.multiple_of((1 - odd) * ((groups - 1) * block_rows), block_rows), block_rows), :]
-    keys, values = key_value(edge, w_key[...], w_value[...])
-    parts.append((keys, values, bias[5][:, :block_rows], None))
+    project(edge, w_key, w_value, keys, values, rows)
+    parts = [
+        part_at(keys, values, 0, rows, lambda: bias[4]),
+        part_at(keys, values, rows, block_rows, lambda: bias[5, :, :block_rows]),
+    ]
     _, out, total = merge((tops[...], outs[...], sums[...]), attend(queries[...], parts, groups))
     context = (out / total).astype(jnp.bfloat16)
     mixed = matmul(context, w_out[...])
@@ -191,6 +207,10 @@
     wide = jax.ShapeDtypeStruct((width, width), jnp.bfloat16)
     small = jax.ShapeDtypeStruct((rows, width), jnp.bfloat16)
     state = jax.ShapeDtypeStruct((rows, width), jnp.float32)
+
+    def pairs_of(total):
+        return [pltpu.VMEM((total, width), jnp.bfloat16)] * 2
+
     far_blocks, far_count = jnp.transpose(expander_blocks, (1, 2, 0)), jnp.transpose(expander_count)
     tables = (local_blocks, local_count, far_blocks, far_count)
     inputs = (features, w_query, w_key, w_value, w_out, *tables)
@@ -206,6 +226,7 @@
         out_specs=(VMEM,) * 10,
         scratch_shapes=[
             pltpu.VMEM((width, width), jnp.bfloat16),
+            *pairs_of(rows),
             *(pltpu.SMEM(t.shape, jnp.int32) for t in tables),
             pltpu.SemaphoreType.DMA((len(inputs),)),
         ],
@@ -217,6 +238,7 @@
         out_shape=(state,) * 3,
         in_specs=[VMEM] * 11,
         out_specs=(VMEM,) * 3,
+        scratch_shapes=pairs_of(3 * rows),
         compiler_params=params,
         name="middle",
     )(by_core, by_1, by_2, w_key, w_value, queries, bias, times, *states)
@@ -225,6 +247,7 @@
         out_shape=jax.ShapeDtypeStruct((rows, width), features.dtype),
         in_specs=[VMEM] * 11,
         out_specs=VMEM,
+        scratch_shapes=pairs_of(rows + rows // groups),
         compiler_params=params,
         name="last",
     )(x, by_3, ring, w_key, w_value, w_out, queries, bias, *states)

time: 17.1 us -> 17.1 us (level)
  no operation moved by 1% of the time
where the time goes in v3:
time: 17.1 us; the launch traced here: 17 us
  Pallas kernels  8.73 us (51%)
  starting transfers between devices  7.7 us (45%)
  waiting for transfers between devices  0.49 us (3%)
    ppermute x4, starting transfers between devices, shards(): lax.ppermute(features, 'dom', [(i, i ^ apart) for i in range(peers)])  6.04 us
    pallas_call x1, Pallas kernels, shards(): pl.pallas_call(middle_kernel, out_shape=(state,) * 3, in_specs=[VMEM] * 1...  3.54 us
    pallas_call x1, Pallas kernels, shards(): pl.pallas_call(last_kernel, out_shape=jax.ShapeDtypeStruct((rows, width),...  2.73 us
    pallas_call x1, Pallas kernels, shards(): pl.pallas_call(own_kernel, out_shape=(small, wide, wide, wide, small, jax...  2.46 us
    ppermute x1, starting transfers between devices, shards(): lax.ppermute(features, 'dom', [(i, (i + 1) % peers if i % 2 else (i - 1)...  1.66 us
    ppermute x1, waiting for transfers between devices, shards(): lax.ppermute(features, 'dom', [(i, (i + 1) % peers if i % 2 else (i - 1)...  0.48 us
  transfers between devices with their start and end apart: 5, of which 1 were waited for; matrix products, arithmetic and copies ran while one was open for 0% of the time, Pallas kernels for 35%

profile of v3, /device:TPU:0, one launch (start us, length us, event | category | flops | bytes accessed | tf_op | source)
XLA Modules:
  0.0 17.0 jit_solution(11675815742392551649)
XLA Ops:
  0.0 0.5 %collective-permute-start.2 = (bf16[256,256]{1,0:T(8,128)(2,1)}, bf16[256,256]{1,0:T(8,128)(2,1)S(1)}, u32[]{:S(2)}, u32[]{:S(2)}) collective-permute-start(bf16[256,256]{1,0:T(8,128)(2,1)} %features.1), channel_id=1, source_target_pairs={{0,1},{1,0},{2,3},{3,2},{4,5},{5,4},{6,7},{7,6},{8,9},{9,8},{10,11... | collective-permute-start | bytes 393224 | tf_op jit(solution)/shard_map/ppermute | solution.py:200
  0.5 2.5 %collective-permute-start.3 = (bf16[256,256]{1,0:T(8,128)(2,1)}, bf16[256,256]{1,0:T(8,128)(2,1)S(1)}, u32[]{:S(2)}, u32[]{:S(2)}) collective-permute-start(bf16[256,256]{1,0:T(8,128)(2,1)} %features.1), channel_id=1, source_target_pairs={{0,2},{1,3},{2,0},{3,1},{4,6},{5,7},{6,4},{7,5},{8,10},{9,11},{10,... | collective-permute-start | bytes 393224 | tf_op jit(solution)/shard_map/ppermute | solution.py:200
  2.9 1.5 %collective-permute-start.4 = (bf16[256,256]{1,0:T(8,128)(2,1)}, bf16[256,256]{1,0:T(8,128)(2,1)S(1)}, u32[]{:S(2)}, u32[]{:S(2)}) collective-permute-start(bf16[256,256]{1,0:T(8,128)(2,1)} %features.1), channel_id=1, source_target_pairs={{0,4},{1,5},{2,6},{3,7},{4,0},{5,1},{6,2},{7,3},{8,12},{9,13},{10,... | collective-permute-start | bytes 393224 | tf_op jit(solution)/shard_map/ppermute | solution.py:200
  4.5 1.6 %collective-permute-start = (bf16[256,256]{1,0:T(8,128)(2,1)}, bf16[256,256]{1,0:T(8,128)(2,1)S(1)}, u32[]{:S(2)}, u32[]{:S(2)}) collective-permute-start(bf16[256,256]{1,0:T(8,128)(2,1)} %features.1), channel_id=1, source_target_pairs={{0,8},{1,9},{2,10},{3,11},{4,12},{5,13},{6,14},{7,15},{8,0},{9,1},... | collective-permute-start | bytes 393224 | tf_op jit(solution)/shard_map/ppermute | solution.py:200
  6.0 1.7 %collective-permute-start.1 = (bf16[256,256]{1,0:T(8,128)(2,1)}, bf16[256,256]{1,0:T(8,128)(2,1)S(1)}, u32[]{:S(2)}, u32[]{:S(2)}) collective-permute-start(bf16[256,256]{1,0:T(8,128)(2,1)} %features.1), channel_id=1, source_target_pairs={{0,31},{1,2},{2,1},{3,4},{4,3},{5,6},{6,5},{7,8},{8,7},{9,10},{10,... | collective-permute-start | bytes 393224 | tf_op jit(solution)/shard_map/ppermute | solution.py:202
  7.7 2.5 %own.1 = (bf16[256,256]{1,0:T(8,128)(2,1)S(1)}, bf16[256,256]{1,0:T(8,128)(2,1)S(1)}, bf16[256,256]{1,0:T(8,128)(2,1)S(1)}, bf16[256,256]{1,0:T(8,128)(2,1)S(1)}...) custom-call(bf16[256,256]{1,0:T(8,128)(2,1)} %features.1, ...), custom_call_target="tpu_custom_call" | custom-call | tf_op jit(solution)/shard_map/own/pallas_call | solution.py:217
  10.2 0.0 collective-permute-done.2.by_core
  10.2 0.0 collective-permute-done.3.by_1
  10.2 0.0 collective-permute-done.4.by_2
  10.2 3.5 %middle.1 = (f32[256,256]{1,0:T(8,128)S(1)}, f32[256,256]{1,0:T(8,128)S(1)}, f32[256,256]{1,0:T(8,128)S(1)}) custom-call(bf16[256,256]{1,0:T(8,128)(2,1)S(1)} %collective-permute-done.2.by_core, bf16[256,256]{1,0:T(8,128)(2,1)S(1)} %collective-permute-done.3.by_1, bf16[256,256]{1,0:T(8,128)(2,1)S(1)} %collective-permute-done.4.by_2, ...), custom_call_target="tpu_custom_call" | custom-call | tf_op jit(solution)/shard_map/middle/pallas_call | solution.py:236
  13.7 0.0 collective-permute-done.by_3
  13.8 0.5 %collective-permute-done.1.ring = bf16[256,256]{1,0:T(8,128)(2,1)S(1)} collective-permute-done((bf16[256,256]{1,0:T(8,128)(2,1)}, bf16[256,256]{1,0:T(8,128)(2,1)S(1)}, u32[]{:S(2)}, u32[]{:S(2)}) %collective-permute-start.1) | collective-permute-done | bytes 131104 | tf_op jit(solution)/shard_map/ppermute | solution.py:202
  14.2 2.7 %last.1 = bf16[256,256]{1,0:T(8,128)(2,1)} custom-call(bf16[256,256]{1,0:T(8,128)(2,1)S(1)} %get-tuple-element.18.features, bf16[256,256]{1,0:T(8,128)(2,1)S(1)} %collective-permute-done.by_3, bf16[256,256]{1,0:T(8,128)(2,1)S(1)} %collective-permute-done.1.ring, bf16[256,256]{1,0:T(8,128)(2,1)S(1)} %get-tuple-element.19.w_key, ...), custom_call_target="tpu_custom_call" | custom-call | tf_op jit(solution)/shard_map/last/pallas_call | solution.py:245
Async XLA Ops:
  0.0 10.2 %collective-permute-start.2 = (bf16[256,256]{1,0:T(8,128)(2,1)}, bf16[256,256]{1,0:T(8,128)(2,1)S(1)}, u32[]{:S(2)}, u32[]{:S(2)}) collective-permute-start(bf16[256,256]{1,0:T(8,128)(2,1)} %features.1), channel_id=1, source_target_pairs={{0,1},{1,0},{2,3},{3,2},{4,5},{5,4},{6,7},{7,6},{8,9},{9,8},{10,11... | collective-permute-start | bytes 393224 | tf_op jit(solution)/shard_map/ppermute | solution.py:200
  0.5 9.7 %collective-permute-start.3 = (bf16[256,256]{1,0:T(8,128)(2,1)}, bf16[256,256]{1,0:T(8,128)(2,1)S(1)}, u32[]{:S(2)}, u32[]{:S(2)}) collective-permute-start(bf16[256,256]{1,0:T(8,128)(2,1)} %features.1), channel_id=1, source_target_pairs={{0,2},{1,3},{2,0},{3,1},{4,6},{5,7},{6,4},{7,5},{8,10},{9,11},{10,... | collective-permute-start | bytes 393224 | tf_op jit(solution)/shard_map/ppermute | solution.py:200
  2.9 7.3 %collective-permute-start.4 = (bf16[256,256]{1,0:T(8,128)(2,1)}, bf16[256,256]{1,0:T(8,128)(2,1)S(1)}, u32[]{:S(2)}, u32[]{:S(2)}) collective-permute-start(bf16[256,256]{1,0:T(8,128)(2,1)} %features.1), channel_id=1, source_target_pairs={{0,4},{1,5},{2,6},{3,7},{4,0},{5,1},{6,2},{7,3},{8,12},{9,13},{10,... | collective-permute-start | bytes 393224 | tf_op jit(solution)/shard_map/ppermute | solution.py:200
  4.5 9.3 %collective-permute-start = (bf16[256,256]{1,0:T(8,128)(2,1)}, bf16[256,256]{1,0:T(8,128)(2,1)S(1)}, u32[]{:S(2)}, u32[]{:S(2)}) collective-permute-start(bf16[256,256]{1,0:T(8,128)(2,1)} %features.1), channel_id=1, source_target_pairs={{0,8},{1,9},{2,10},{3,11},{4,12},{5,13},{6,14},{7,15},{8,0},{9,1},... | collective-permute-start | bytes 393224 | tf_op jit(solution)/shard_map/ppermute | solution.py:200
  6.0 8.2 %collective-permute-start.1 = (bf16[256,256]{1,0:T(8,128)(2,1)}, bf16[256,256]{1,0:T(8,128)(2,1)S(1)}, u32[]{:S(2)}, u32[]{:S(2)}) collective-permute-start(bf16[256,256]{1,0:T(8,128)(2,1)} %features.1), channel_id=1, source_target_pairs={{0,31},{1,2},{2,1},{3,4},{4,3},{5,6},{6,5},{7,8},{8,7},{9,10},{10,... | collective-permute-start | bytes 393224 | tf_op jit(solution)/shard_map/ppermute | solution.py:202

commit v4 on v3

--- a/solution.py
+++ b/solution.py
@@ -63,10 +63,10 @@
         if times is not None:
             weights = (by_group(weights) * times()[None, :, None, :]).reshape(part.shape)
         weights = weights.astype(jnp.bfloat16)
-        even = matmul(weights[:half], jnp.where(heads % 2 == 0, values(), one))
-        odd = matmul(weights[half:], jnp.where(heads % 2 == 1, values(), one))
-        first = even if first is None else first + even
-        second = odd if second is None else second + odd
+        even = jnp.where(heads % 2 == 0, values(), one)
+        first = matmul(weights[:half], even) if first is None else first + matmul(weights[:half], even)
+        odd = jnp.where(heads % 2 == 1, values(), one)
+        second = matmul(weights[half:], odd) if second is None else second + matmul(weights[half:], odd)
     tops = out = sums = jnp.zeros((rows, width), jnp.float32)
     for i, h in enumerate(ORDER):
         source, at = (first, i) if i < HEADS // 2 else (second, i - HEADS // 2)

time: 17.1 us -> 17.1 us (level)
  waiting for transfers between devices: 0.49 us -> 1.65 us
  Pallas kernels: 8.73 us -> 7.58 us
    pallas_call x1, Pallas kernels: 3.54 us -> 2.39 us  [shards(): pl.pallas_call(middle_kernel, out_shape=(state,) * 3, in_specs=[VMEM] * 1...]
    ppermute x1, waiting for transfers between devices: 0.48 us -> 1.64 us  [shards(): lax.ppermute(features, 'dom', [(i, (i + 1) % peers if i % 2 else (i - 1)...]
  transfers between devices with their start and end apart: 5 -> 5, of which waited for: 1 -> 1; matrix products, arithmetic and copies ran while one was open for 0% -> 0% of each run, Pallas kernels for 35% -> 29%
where the time goes in v4:
time: 17.1 us; the launch traced here: 17 us
  starting transfers between devices  7.7 us (45%)
  Pallas kernels  7.58 us (44%)
  waiting for transfers between devices  1.65 us (10%)
    ppermute x4, starting transfers between devices, shards(): lax.ppermute(features, 'dom', [(i, i ^ apart) for i in range(peers)])  6.04 us
    pallas_call x1, Pallas kernels, shards(): pl.pallas_call(last_kernel, out_shape=jax.ShapeDtypeStruct((rows, width),...  2.73 us
    pallas_call x1, Pallas kernels, shards(): pl.pallas_call(own_kernel, out_shape=(small, wide, wide, wide, small, jax...  2.46 us
    pallas_call x1, Pallas kernels, shards(): pl.pallas_call(middle_kernel, out_shape=(state,) * 3, in_specs=[VMEM] * 1...  2.39 us
    ppermute x1, starting transfers between devices, shards(): lax.ppermute(features, 'dom', [(i, (i + 1) % peers if i % 2 else (i - 1)...  1.66 us
    ppermute x1, waiting for transfers between devices, shards(): lax.ppermute(features, 'dom', [(i, (i + 1) % peers if i % 2 else (i - 1)...  1.64 us
  transfers between devices with their start and end apart: 5, of which 1 were waited for; matrix products, arithmetic and copies ran while one was open for 0% of the time, Pallas kernels for 29%

profile of v4, /device:TPU:0, one launch (start us, length us, event | category | flops | bytes accessed | tf_op | source)
XLA Modules:
  0.0 17.0 jit_solution(10814953362214157948)
XLA Ops:
  0.0 0.5 %collective-permute-start.2 = (bf16[256,256]{1,0:T(8,128)(2,1)}, bf16[256,256]{1,0:T(8,128)(2,1)S(1)}, u32[]{:S(2)}, u32[]{:S(2)}) collective-permute-start(bf16[256,256]{1,0:T(8,128)(2,1)} %features.1), channel_id=1, source_target_pairs={{0,1},{1,0},{2,3},{3,2},{4,5},{5,4},{6,7},{7,6},{8,9},{9,8},{10,11... | collective-permute-start | bytes 393224 | tf_op jit(solution)/shard_map/ppermute | solution.py:200
  0.5 2.5 %collective-permute-start.3 = (bf16[256,256]{1,0:T(8,128)(2,1)}, bf16[256,256]{1,0:T(8,128)(2,1)S(1)}, u32[]{:S(2)}, u32[]{:S(2)}) collective-permute-start(bf16[256,256]{1,0:T(8,128)(2,1)} %features.1), channel_id=1, source_target_pairs={{0,2},{1,3},{2,0},{3,1},{4,6},{5,7},{6,4},{7,5},{8,10},{9,11},{10,... | collective-permute-start | bytes 393224 | tf_op jit(solution)/shard_map/ppermute | solution.py:200
  2.9 1.5 %collective-permute-start.4 = (bf16[256,256]{1,0:T(8,128)(2,1)}, bf16[256,256]{1,0:T(8,128)(2,1)S(1)}, u32[]{:S(2)}, u32[]{:S(2)}) collective-permute-start(bf16[256,256]{1,0:T(8,128)(2,1)} %features.1), channel_id=1, source_target_pairs={{0,4},{1,5},{2,6},{3,7},{4,0},{5,1},{6,2},{7,3},{8,12},{9,13},{10,... | collective-permute-start | bytes 393224 | tf_op jit(solution)/shard_map/ppermute | solution.py:200
  4.5 1.6 %collective-permute-start = (bf16[256,256]{1,0:T(8,128)(2,1)}, bf16[256,256]{1,0:T(8,128)(2,1)S(1)}, u32[]{:S(2)}, u32[]{:S(2)}) collective-permute-start(bf16[256,256]{1,0:T(8,128)(2,1)} %features.1), channel_id=1, source_target_pairs={{0,8},{1,9},{2,10},{3,11},{4,12},{5,13},{6,14},{7,15},{8,0},{9,1},... | collective-permute-start | bytes 393224 | tf_op jit(solution)/shard_map/ppermute | solution.py:200
  6.0 1.7 %collective-permute-start.1 = (bf16[256,256]{1,0:T(8,128)(2,1)}, bf16[256,256]{1,0:T(8,128)(2,1)S(1)}, u32[]{:S(2)}, u32[]{:S(2)}) collective-permute-start(bf16[256,256]{1,0:T(8,128)(2,1)} %features.1), channel_id=1, source_target_pairs={{0,31},{1,2},{2,1},{3,4},{4,3},{5,6},{6,5},{7,8},{8,7},{9,10},{10,... | collective-permute-start | bytes 393224 | tf_op jit(solution)/shard_map/ppermute | solution.py:202
  7.7 2.5 %own.1 = (bf16[256,256]{1,0:T(8,128)(2,1)S(1)}, bf16[256,256]{1,0:T(8,128)(2,1)S(1)}, bf16[256,256]{1,0:T(8,128)(2,1)S(1)}, bf16[256,256]{1,0:T(8,128)(2,1)S(1)}...) custom-call(bf16[256,256]{1,0:T(8,128)(2,1)} %features.1, ...), custom_call_target="tpu_custom_call" | custom-call | tf_op jit(solution)/shard_map/own/pallas_call | solution.py:217
  10.2 0.0 collective-permute-done.2.by_core
  10.2 0.0 collective-permute-done.3.by_1
  10.2 0.0 collective-permute-done.4.by_2
  10.2 2.4 %middle.1 = (f32[256,256]{1,0:T(8,128)S(1)}, f32[256,256]{1,0:T(8,128)S(1)}, f32[256,256]{1,0:T(8,128)S(1)}) custom-call(bf16[256,256]{1,0:T(8,128)(2,1)S(1)} %collective-permute-done.2.by_core, bf16[256,256]{1,0:T(8,128)(2,1)S(1)} %collective-permute-done.3.by_1, bf16[256,256]{1,0:T(8,128)(2,1)S(1)} %collective-permute-done.4.by_2, ...), custom_call_target="tpu_custom_call" | custom-call | tf_op jit(solution)/shard_map/middle/pallas_call | solution.py:236
  12.6 0.0 collective-permute-done.by_3
  12.6 1.6 %collective-permute-done.1.ring = bf16[256,256]{1,0:T(8,128)(2,1)S(1)} collective-permute-done((bf16[256,256]{1,0:T(8,128)(2,1)}, bf16[256,256]{1,0:T(8,128)(2,1)S(1)}, u32[]{:S(2)}, u32[]{:S(2)}) %collective-permute-start.1) | collective-permute-done | bytes 131104 | tf_op jit(solution)/shard_map/ppermute | solution.py:202
  14.2 2.7 %last.1 = bf16[256,256]{1,0:T(8,128)(2,1)} custom-call(bf16[256,256]{1,0:T(8,128)(2,1)S(1)} %get-tuple-element.18.features, bf16[256,256]{1,0:T(8,128)(2,1)S(1)} %collective-permute-done.by_3, bf16[256,256]{1,0:T(8,128)(2,1)S(1)} %collective-permute-done.1.ring, bf16[256,256]{1,0:T(8,128)(2,1)S(1)} %get-tuple-element.19.w_key, ...), custom_call_target="tpu_custom_call" | custom-call | tf_op jit(solution)/shard_map/last/pallas_call | solution.py:245
Async XLA Ops:
  0.0 10.2 %collective-permute-start.2 = (bf16[256,256]{1,0:T(8,128)(2,1)}, bf16[256,256]{1,0:T(8,128)(2,1)S(1)}, u32[]{:S(2)}, u32[]{:S(2)}) collective-permute-start(bf16[256,256]{1,0:T(8,128)(2,1)} %features.1), channel_id=1, source_target_pairs={{0,1},{1,0},{2,3},{3,2},{4,5},{5,4},{6,7},{7,6},{8,9},{9,8},{10,11... | collective-permute-start | bytes 393224 | tf_op jit(solution)/shard_map/ppermute | solution.py:200
  0.5 9.7 %collective-permute-start.3 = (bf16[256,256]{1,0:T(8,128)(2,1)}, bf16[256,256]{1,0:T(8,128)(2,1)S(1)}, u32[]{:S(2)}, u32[]{:S(2)}) collective-permute-start(bf16[256,256]{1,0:T(8,128)(2,1)} %features.1), channel_id=1, source_target_pairs={{0,2},{1,3},{2,0},{3,1},{4,6},{5,7},{6,4},{7,5},{8,10},{9,11},{10,... | collective-permute-start | bytes 393224 | tf_op jit(solution)/shard_map/ppermute | solution.py:200
  2.9 7.3 %collective-permute-start.4 = (bf16[256,256]{1,0:T(8,128)(2,1)}, bf16[256,256]{1,0:T(8,128)(2,1)S(1)}, u32[]{:S(2)}, u32[]{:S(2)}) collective-permute-start(bf16[256,256]{1,0:T(8,128)(2,1)} %features.1), channel_id=1, source_target_pairs={{0,4},{1,5},{2,6},{3,7},{4,0},{5,1},{6,2},{7,3},{8,12},{9,13},{10,... | collective-permute-start | bytes 393224 | tf_op jit(solution)/shard_map/ppermute | solution.py:200
  4.5 8.1 %collective-permute-start = (bf16[256,256]{1,0:T(8,128)(2,1)}, bf16[256,256]{1,0:T(8,128)(2,1)S(1)}, u32[]{:S(2)}, u32[]{:S(2)}) collective-permute-start(bf16[256,256]{1,0:T(8,128)(2,1)} %features.1), channel_id=1, source_target_pairs={{0,8},{1,9},{2,10},{3,11},{4,12},{5,13},{6,14},{7,15},{8,0},{9,1},... | collective-permute-start | bytes 393224 | tf_op jit(solution)/shard_map/ppermute | solution.py:200
  6.0 8.2 %collective-permute-start.1 = (bf16[256,256]{1,0:T(8,128)(2,1)}, bf16[256,256]{1,0:T(8,128)(2,1)S(1)}, u32[]{:S(2)}, u32[]{:S(2)}) collective-permute-start(bf16[256,256]{1,0:T(8,128)(2,1)} %features.1), channel_id=1, source_target_pairs={{0,31},{1,2},{2,1},{3,4},{4,3},{5,6},{6,5},{7,8},{8,7},{9,10},{10,... | collective-permute-start | bytes 393224 | tf_op jit(solution)/shard_map/ppermute | solution.py:202

commit v5 on v4

--- a/solution.py
+++ b/solution.py
@@ -96,10 +96,10 @@
     return lambda: keys[where, :], lambda: values[where, :], bias, times
 
 
-def own_kernel(
+def load_kernel(
     features, w_query, w_key, w_value, w_out, local_blocks, local_count, expander_blocks, expander_count,
-    x, key_copy, value_copy, out_copy, queries, bias, times, tops, outs, sums,
-    query_copy, keys, values, blocks, count, far_blocks, far_count, sems,
+    x, key_copy, value_copy, out_copy, queries, keys, values, bias, times, trailing, leading,
+    query_copy, blocks, count, far_blocks, far_count, sems,
 ):
     pairs = (
         (features, x), (w_query, query_copy), (w_key, key_copy), (w_value, value_copy), (local_blocks, blocks),
@@ -110,8 +110,9 @@
         copy.start()
     groups, most = blocks.shape
     most_far, matchings = far_blocks.shape[1:]
-    block_rows = x.shape[0] // groups
-    size = x.shape[1] // HEADS
+    rows, width = x.shape
+    block_rows = rows // groups
+    size = width // HEADS
     is_odd = lax.rem(lax.axis_index("dom"), 2) == 1
     for copy in copies[4:8]:
         copy.wait()
@@ -131,46 +132,48 @@
     for copy in copies[:4]:
         copy.wait()
     own = x[...]
-    q = (matmul(own, query_copy[...]) * (float(size) ** -0.5)).astype(jnp.bfloat16)
-    queries[...] = q
+    trailing[...] = x[rows - block_rows :, :]
+    leading[...] = x[:block_rows, :]
+    queries[...] = (matmul(own, query_copy[...]) * (float(size) ** -0.5)).astype(jnp.bfloat16)
     project(own, key_copy, value_copy, keys, values, 0)
-    parts = [part_at(keys, values, 0, own.shape[0], lambda: bias[0])]
-    tops[...], outs[...], sums[...] = attend(q, parts, groups)
     copies[8].wait()
 
 
-def middle_kernel(
-    by_core, by_1, by_2, w_key, w_value, queries, bias, times, tops, outs, sums,
-    new_tops, new_outs, new_sums,
+def near_kernel(
+    own_keys, own_values, by_core, by_1, leading, w_key, w_value, queries, bias, times,
+    tops, outs, sums, leading_copy,
     keys, values,
 ):
     groups = times.shape[0]
     rows = by_core.shape[0]
-    parts = []
-    for m, ref in enumerate((by_core, by_1, by_2)):
-        project(ref[...], w_key, w_value, keys, values, m * rows)
-        parts.append(
-            part_at(keys, values, m * rows, rows, lambda m=m: bias[1 + m], (lambda: times[...]) if m == 0 else None)
-        )
-    state = attend(queries[...], parts, groups)
-    new_tops[...], new_outs[...], new_sums[...] = merge((tops[...], outs[...], sums[...]), state)
+    leading_copy[...] = leading[...]
+    project(by_core[...], w_key, w_value, keys, values, 0)
+    project(by_1[...], w_key, w_value, keys, values, rows)
+    parts = [
+        part_at(own_keys, own_values, 0, rows, lambda: bias[0]),
+        part_at(keys, values, 0, rows, lambda: bias[1], lambda: times[...]),
+        part_at(keys, values, rows, rows, lambda: bias[2]),
+    ]
+    tops[...], outs[...], sums[...] = attend(queries[...], parts, groups)
 
 
 def last_kernel(
-    features, by_3, ring, w_key, w_value, w_out, queries, bias, tops, outs, sums,
+    features, by_2, by_3, before, after, w_key, w_value, w_out, queries, bias, tops, outs, sums,
     result,
     keys, values,
 ):
     groups = bias.shape[1]
     rows = features.shape[0]
     block_rows = rows // groups
-    odd = lax.rem(lax.axis_index("dom"), 2)
-    project(by_3[...], w_key, w_value, keys, values, 0)
-    edge = ring[pl.ds(pl.multiple_of((1 - odd) * ((groups - 1) * block_rows), block_rows), block_rows), :]
-    project(edge, w_key, w_value, keys, values, rows)
+    is_odd = lax.rem(lax.axis_index("dom"), 2) == 1
+    project(by_2[...], w_key, w_value, keys, values, 0)
+    project(by_3[...], w_key, w_value, keys, values, rows)
+    edge = jnp.where(is_odd, after[...], before[...])
+    project(edge, w_key, w_value, keys, values, 2 * rows)
     parts = [
-        part_at(keys, values, 0, rows, lambda: bias[4]),
-        part_at(keys, values, rows, block_rows, lambda: bias[5, :, :block_rows]),
+        part_at(keys, values, 0, rows, lambda: bias[3]),
+        part_at(keys, values, rows, rows, lambda: bias[4]),
+        part_at(keys, values, 2 * rows, block_rows, lambda: bias[5, :, :block_rows]),
     ]
     _, out, total = merge((tops[...], outs[...], sums[...]), attend(queries[...], parts, groups))
     context = (out / total).astype(jnp.bfloat16)
@@ -191,6 +194,8 @@
     expander_count,
 ):
     rows, width = features.shape
+    groups = local_blocks.shape[0]
+    block_rows = rows // groups
     peers = lax.axis_size("dom")
     levels = peers.bit_length() - 1
     match_total = expander_blocks.shape[0]
@@ -199,58 +204,55 @@
         apart = 1 << (matching * levels // match_total)
         arrived.append(lax.ppermute(features, "dom", [(i, i ^ apart) for i in range(peers)]))
     by_core, by_1, by_2, by_3 = arrived
-    ring = lax.ppermute(
-        features, "dom", [(i, (i + 1) % peers if i % 2 else (i - 1) % peers) for i in range(peers)]
-    )
     params = pltpu.CompilerParams(vmem_limit_bytes=48 * 2**20)
-    groups = local_blocks.shape[0]
-    wide = jax.ShapeDtypeStruct((width, width), jnp.bfloat16)
-    small = jax.ShapeDtypeStruct((rows, width), jnp.bfloat16)
-    state = jax.ShapeDtypeStruct((rows, width), jnp.float32)
+
+    def array(*shape, dtype=jnp.bfloat16):
+        return jax.ShapeDtypeStruct(shape, dtype)
 
     def pairs_of(total):
         return [pltpu.VMEM((total, width), jnp.bfloat16)] * 2
 
+    state = [array(rows, width, dtype=jnp.float32)] * 3
     far_blocks, far_count = jnp.transpose(expander_blocks, (1, 2, 0)), jnp.transpose(expander_count)
     tables = (local_blocks, local_count, far_blocks, far_count)
     inputs = (features, w_query, w_key, w_value, w_out, *tables)
-    x, w_key, w_value, w_out, queries, bias, times, *states = pl.pallas_call(
-        own_kernel,
+    x, w_key, w_value, w_out, queries, own_keys, own_values, bias, times, trailing, leading = pl.pallas_call(
+        load_kernel,
         out_shape=(
-            small, wide, wide, wide, small,
-            jax.ShapeDtypeStruct((match_total + 2, groups, rows), jnp.float32),
-            jax.ShapeDtypeStruct((groups, rows), jnp.float32),
-            state, state, state,
+            array(rows, width), *[array(width, width)] * 3, *[array(rows, width)] * 3,
+            array(match_total + 2, groups, rows, dtype=jnp.float32), array(groups, rows, dtype=jnp.float32),
+            array(block_rows, width), array(block_rows, width),
         ),
         in_specs=[ANY] * len(inputs),
-        out_specs=(VMEM,) * 10,
+        out_specs=(VMEM,) * 11,
         scratch_shapes=[
             pltpu.VMEM((width, width), jnp.bfloat16),
-            *pairs_of(rows),
             *(pltpu.SMEM(t.shape, jnp.int32) for t in tables),
             pltpu.SemaphoreType.DMA((len(inputs),)),
         ],
         compiler_params=params,
-        name="own",
+        name="load",
     )(*(pltpu.with_memory_space_constraint(a, pltpu.HBM) for a in inputs))
-    states = pl.pallas_call(
-        middle_kernel,
-        out_shape=(state,) * 3,
-        in_specs=[VMEM] * 11,
-        out_specs=(VMEM,) * 3,
-        scratch_shapes=pairs_of(3 * rows),
+    before = lax.ppermute(trailing, "dom", [(i, (i + 1) % peers) for i in range(peers)])
+    *states, leading = pl.pallas_call(
+        near_kernel,
+        out_shape=(*state, array(block_rows, width)),
+        in_specs=[VMEM] * 10,
+        out_specs=(VMEM,) * 4,
+        scratch_shapes=pairs_of(2 * rows),
         compiler_params=params,
-        name="middle",
-    )(by_core, by_1, by_2, w_key, w_value, queries, bias, times, *states)
+        name="near",
+    )(own_keys, own_values, by_core, by_1, leading, w_key, w_value, queries, bias, times)
+    after = lax.ppermute(leading, "dom", [(i, (i - 1) % peers) for i in range(peers)])
     return pl.pallas_call(
         last_kernel,
-        out_shape=jax.ShapeDtypeStruct((rows, width), features.dtype),
-        in_specs=[VMEM] * 11,
+        out_shape=array(rows, width, dtype=features.dtype),
+        in_specs=[VMEM] * 13,
         out_specs=VMEM,
-        scratch_shapes=pairs_of(rows + rows // groups),
+        scratch_shapes=pairs_of(2 * rows + block_rows),
         compiler_params=params,
         name="last",
-    )(x, by_3, ring, w_key, w_value, w_out, queries, bias, *states)
+    )(x, by_2, by_3, before, after, w_key, w_value, w_out, queries, bias, *states)
 
 
 def solution(mesh):

time: 17.1 us -> 20.6 us (1.20)
  starting transfers between devices: 7.7 us -> 11.5 us
  Pallas kernels: 7.58 us -> 7.06 us
  waiting for transfers between devices: 1.65 us -> 1.91 us
    ppermute x1 -> x2, starting transfers between devices: 1.66 us -> 5.42 us  [the longest x1 5.36 us: shards(): lax.ppermute(leading, 'dom', [(i, (i - 1) % peers) for i in range(peers)])]
    pallas_call x3, Pallas kernels: 7.58 us -> 7.06 us  [the longest x1 3.2 us: shards(): pl.pallas_call(last_kernel, out_shape=array(rows, width, dtype=features.d...]
    ppermute x1 -> x2, waiting for transfers between devices: 1.64 us -> 1.9 us  [the longest x1 1.89 us: shards(): lax.ppermute(leading, 'dom', [(i, (i - 1) % peers) for i in range(peers)])]
  transfers between devices with their start and end apart: 5 -> 6, of which waited for: 1 -> 1; matrix products, arithmetic and copies ran while one was open for 0% -> 0% of each run, Pallas kernels for 29% -> 19%
where the time goes in v5:
time: 20.6 us; the launch traced here: 20.5 us
  starting transfers between devices  11.5 us (56%)
  Pallas kernels  7.06 us (34%)
  waiting for transfers between devices  1.91 us (9%)
    ppermute x4, starting transfers between devices, shards(): lax.ppermute(features, 'dom', [(i, i ^ apart) for i in range(peers)])  6.04 us
    ppermute x1, starting transfers between devices, shards(): lax.ppermute(leading, 'dom', [(i, (i - 1) % peers) for i in range(peers)])  5.36 us
    pallas_call x1, Pallas kernels, shards(): pl.pallas_call(last_kernel, out_shape=array(rows, width, dtype=features.d...  3.2 us
    pallas_call x1, Pallas kernels, shards(): pl.pallas_call(near_kernel, out_shape=(*state, array(block_rows, width)),...  2.42 us
    ppermute x1, waiting for transfers between devices, shards(): lax.ppermute(leading, 'dom', [(i, (i - 1) % peers) for i in range(peers)])  1.89 us
    pallas_call x1, Pallas kernels, shards(): pl.pallas_call(load_kernel, out_shape=(array(rows, width), *[array(width,...  1.45 us
  transfers between devices with their start and end apart: 6, of which 1 were waited for; matrix products, arithmetic and copies ran while one was open for 0% of the time, Pallas kernels for 19%

profile of v5, /device:TPU:0, one launch (start us, length us, event | category | flops | bytes accessed | tf_op | source)
XLA Modules:
  0.0 20.5 jit_solution(263990120217950552)
XLA Ops:
  0.0 0.5 %collective-permute-start.3 = (bf16[256,256]{1,0:T(8,128)(2,1)}, bf16[256,256]{1,0:T(8,128)(2,1)S(1)}, u32[]{:S(2)}, u32[]{:S(2)}) collective-permute-start(bf16[256,256]{1,0:T(8,128)(2,1)} %features.1), channel_id=1, source_target_pairs={{0,1},{1,0},{2,3},{3,2},{4,5},{5,4},{6,7},{7,6},{8,9},{9,8},{10,11... | collective-permute-start | bytes 393224 | tf_op jit(solution)/shard_map/ppermute | solution.py:205
  0.5 2.5 %collective-permute-start.4 = (bf16[256,256]{1,0:T(8,128)(2,1)}, bf16[256,256]{1,0:T(8,128)(2,1)S(1)}, u32[]{:S(2)}, u32[]{:S(2)}) collective-permute-start(bf16[256,256]{1,0:T(8,128)(2,1)} %features.1), channel_id=1, source_target_pairs={{0,2},{1,3},{2,0},{3,1},{4,6},{5,7},{6,4},{7,5},{8,10},{9,11},{10,... | collective-permute-start | bytes 393224 | tf_op jit(solution)/shard_map/ppermute | solution.py:205
  2.9 1.5 %collective-permute-start = (bf16[256,256]{1,0:T(8,128)(2,1)}, bf16[256,256]{1,0:T(8,128)(2,1)S(1)}, u32[]{:S(2)}, u32[]{:S(2)}) collective-permute-start(bf16[256,256]{1,0:T(8,128)(2,1)} %features.1), channel_id=1, source_target_pairs={{0,4},{1,5},{2,6},{3,7},{4,0},{5,1},{6,2},{7,3},{8,12},{9,13},{10,... | collective-permute-start | bytes 393224 | tf_op jit(solution)/shard_map/ppermute | solution.py:205
  4.5 1.6 %collective-permute-start.1 = (bf16[256,256]{1,0:T(8,128)(2,1)}, bf16[256,256]{1,0:T(8,128)(2,1)S(1)}, u32[]{:S(2)}, u32[]{:S(2)}) collective-permute-start(bf16[256,256]{1,0:T(8,128)(2,1)} %features.1), channel_id=1, source_target_pairs={{0,8},{1,9},{2,10},{3,11},{4,12},{5,13},{6,14},{7,15},{8,0},{9,1},... | collective-permute-start | bytes 393224 | tf_op jit(solution)/shard_map/ppermute | solution.py:205
  6.0 1.4 %load.1 = (bf16[256,256]{1,0:T(8,128)(2,1)S(1)}, bf16[256,256]{1,0:T(8,128)(2,1)S(1)}, bf16[256,256]{1,0:T(8,128)(2,1)S(1)}, bf16[256,256]{1,0:T(8,128)(2,1)S(1)...) custom-call(bf16[256,256]{1,0:T(8,128)(2,1)} %features.1, ...), custom_call_target="tpu_custom_call" | custom-call | tf_op jit(solution)/shard_map/load/pallas_call | solution.py:219
  7.5 0.1 collective-permute-start.2
  7.6 0.0 collective-permute-done.3.by_core
  7.6 0.0 collective-permute-done.4.by_1
  7.6 2.4 %near.1 = (f32[256,256]{1,0:T(8,128)S(1)}, f32[256,256]{1,0:T(8,128)S(1)}, f32[256,256]{1,0:T(8,128)S(1)}, bf16[128,256]{1,0:T(8,128)(2,1)S(1)}) custom-call(bf16[256,256]{1,0:T(8,128)(2,1)S(1)} %get-tuple-element.22.own_keys, bf16[256,256]{1,0:T(8,128)(2,1)S(1)} %get-tuple-element.23.own_values, bf16[256,256]{1,0:T(8,128)(2,1)S(1)} %collective-permute-done.3.by_core, ...), custom_call_target="tpu_custom_call" | custom-call | tf_op jit(solution)/shard_map/near/pallas_call | solution.py:237
  10.0 5.4 %collective-permute-start.5 = (bf16[128,256]{1,0:T(8,128)(2,1)S(1)}, bf16[128,256]{1,0:T(8,128)(2,1)S(1)}, u32[]{:S(2)}, u32[]{:S(2)}) collective-permute-start(bf16[128,256]{1,0:T(8,128)(2,1)S(1)} %get-tuple-element.30), channel_id=1, source_target_pairs={{0,31},{1,0},{2,1},{3,2},{4,3},{5,4},{6,5},{7,6},{8,7},{9,8},{10,9... | collective-permute-start | bytes 196616 | tf_op jit(solution)/shard_map/ppermute | solution.py:246
  15.4 0.0 collective-permute-done.2.before
  15.4 0.0 collective-permute-done.by_2
  15.4 0.0 collective-permute-done.1.by_3
  15.4 1.9 %collective-permute-done.5.after = bf16[128,256]{1,0:T(8,128)(2,1)S(1)} collective-permute-done((bf16[128,256]{1,0:T(8,128)(2,1)S(1)}, bf16[128,256]{1,0:T(8,128)(2,1)S(1)}, u32[]{:S(2)}, u32[]{:S(2)}) %collective-permute-start.5) | collective-permute-done | bytes 65568 | tf_op jit(solution)/shard_map/ppermute | solution.py:246
  17.3 3.2 %last.1 = bf16[256,256]{1,0:T(8,128)(2,1)} custom-call(bf16[256,256]{1,0:T(8,128)(2,1)S(1)} %get-tuple-element.20.features, bf16[256,256]{1,0:T(8,128)(2,1)S(1)} %collective-permute-done.by_2, bf16[256,256]{1,0:T(8,128)(2,1)S(1)} %collective-permute-done.1.by_3, bf16[128,256]{1,0:T(8,128)(2,1)S(1)} %collective-permute-done.2.before, ...), custom_call_target="tpu_custom_call" | custom-call | tf_op jit(solution)/shard_map/last/pallas_call | solution.py:247
Async XLA Ops:
  0.0 7.6 %collective-permute-start.3 = (bf16[256,256]{1,0:T(8,128)(2,1)}, bf16[256,256]{1,0:T(8,128)(2,1)S(1)}, u32[]{:S(2)}, u32[]{:S(2)}) collective-permute-start(bf16[256,256]{1,0:T(8,128)(2,1)} %features.1), channel_id=1, source_target_pairs={{0,1},{1,0},{2,3},{3,2},{4,5},{5,4},{6,7},{7,6},{8,9},{9,8},{10,11... | collective-permute-start | bytes 393224 | tf_op jit(solution)/shard_map/ppermute | solution.py:205
  0.5 7.1 %collective-permute-start.4 = (bf16[256,256]{1,0:T(8,128)(2,1)}, bf16[256,256]{1,0:T(8,128)(2,1)S(1)}, u32[]{:S(2)}, u32[]{:S(2)}) collective-permute-start(bf16[256,256]{1,0:T(8,128)(2,1)} %features.1), channel_id=1, source_target_pairs={{0,2},{1,3},{2,0},{3,1},{4,6},{5,7},{6,4},{7,5},{8,10},{9,11},{10,... | collective-permute-start | bytes 393224 | tf_op jit(solution)/shard_map/ppermute | solution.py:205
  2.9 12.4 %collective-permute-start = (bf16[256,256]{1,0:T(8,128)(2,1)}, bf16[256,256]{1,0:T(8,128)(2,1)S(1)}, u32[]{:S(2)}, u32[]{:S(2)}) collective-permute-start(bf16[256,256]{1,0:T(8,128)(2,1)} %features.1), channel_id=1, source_target_pairs={{0,4},{1,5},{2,6},{3,7},{4,0},{5,1},{6,2},{7,3},{8,12},{9,13},{10,... | collective-permute-start | bytes 393224 | tf_op jit(solution)/shard_map/ppermute | solution.py:205
  4.5 10.9 %collective-permute-start.1 = (bf16[256,256]{1,0:T(8,128)(2,1)}, bf16[256,256]{1,0:T(8,128)(2,1)S(1)}, u32[]{:S(2)}, u32[]{:S(2)}) collective-permute-start(bf16[256,256]{1,0:T(8,128)(2,1)} %features.1), channel_id=1, source_target_pairs={{0,8},{1,9},{2,10},{3,11},{4,12},{5,13},{6,14},{7,15},{8,0},{9,1},... | collective-permute-start | bytes 393224 | tf_op jit(solution)/shard_map/ppermute | solution.py:205
  7.5 7.9 %collective-permute-start.2 = (bf16[128,256]{1,0:T(8,128)(2,1)S(1)}, bf16[128,256]{1,0:T(8,128)(2,1)S(1)}, u32[]{:S(2)}, u32[]{:S(2)}) collective-permute-start(bf16[128,256]{1,0:T(8,128)(2,1)S(1)} %get-tuple-element.21), channel_id=1, source_target_pairs={{0,1},{1,2},{2,3},{3,4},{4,5},{5,6},{6,7},{7,8},{8,9},{9,10},{10,1... | collective-permute-start | bytes 196616 | tf_op jit(solution)/shard_map/ppermute | solution.py:236
  10.0 7.3 %collective-permute-start.5 = (bf16[128,256]{1,0:T(8,128)(2,1)S(1)}, bf16[128,256]{1,0:T(8,128)(2,1)S(1)}, u32[]{:S(2)}, u32[]{:S(2)}) collective-permute-start(bf16[128,256]{1,0:T(8,128)(2,1)S(1)} %get-tuple-element.30), channel_id=1, source_target_pairs={{0,31},{1,0},{2,1},{3,2},{4,3},{5,4},{6,5},{7,6},{8,7},{9,8},{10,9... | collective-permute-start | bytes 196616 | tf_op jit(solution)/shard_map/ppermute | solution.py:246

commit v6 on v4

--- a/solution.py
+++ b/solution.py
@@ -110,8 +110,9 @@
         copy.start()
     groups, most = blocks.shape
     most_far, matchings = far_blocks.shape[1:]
-    block_rows = x.shape[0] // groups
-    size = x.shape[1] // HEADS
+    rows, width = x.shape
+    block_rows = rows // groups
+    size = width // HEADS
     is_odd = lax.rem(lax.axis_index("dom"), 2) == 1
     for copy in copies[4:8]:
         copy.wait()
@@ -134,44 +135,29 @@
     q = (matmul(own, query_copy[...]) * (float(size) ** -0.5)).astype(jnp.bfloat16)
     queries[...] = q
     project(own, key_copy, value_copy, keys, values, 0)
-    parts = [part_at(keys, values, 0, own.shape[0], lambda: bias[0])]
+    parts = [part_at(keys, values, 0, rows, lambda: bias[0])]
     tops[...], outs[...], sums[...] = attend(q, parts, groups)
     copies[8].wait()
 
 
-def middle_kernel(
-    by_core, by_1, by_2, w_key, w_value, queries, bias, times, tops, outs, sums,
-    new_tops, new_outs, new_sums,
+def rest_kernel(
+    features, before, by_1, by_2, by_3, after, w_key, w_value, w_out, queries, bias, times, tops, outs, sums,
+    result,
     keys, values,
 ):
     groups = times.shape[0]
-    rows = by_core.shape[0]
-    parts = []
-    for m, ref in enumerate((by_core, by_1, by_2)):
-        project(ref[...], w_key, w_value, keys, values, m * rows)
-        parts.append(
-            part_at(keys, values, m * rows, rows, lambda m=m: bias[1 + m], (lambda: times[...]) if m == 0 else None)
-        )
-    state = attend(queries[...], parts, groups)
-    new_tops[...], new_outs[...], new_sums[...] = merge((tops[...], outs[...], sums[...]), state)
-
-
-def last_kernel(
-    features, by_3, ring, w_key, w_value, w_out, queries, bias, tops, outs, sums,
-    result,
-    keys, values,
-):
-    groups = bias.shape[1]
     rows = features.shape[0]
     block_rows = rows // groups
-    odd = lax.rem(lax.axis_index("dom"), 2)
-    project(by_3[...], w_key, w_value, keys, values, 0)
-    edge = ring[pl.ds(pl.multiple_of((1 - odd) * ((groups - 1) * block_rows), block_rows), block_rows), :]
-    project(edge, w_key, w_value, keys, values, rows)
-    parts = [
-        part_at(keys, values, 0, rows, lambda: bias[4]),
-        part_at(keys, values, rows, block_rows, lambda: bias[5, :, :block_rows]),
-    ]
+    is_odd = lax.rem(lax.axis_index("dom"), 2) == 1
+    project(by_1[...], w_key, w_value, keys, values, 0)
+    project(by_2[...], w_key, w_value, keys, values, rows)
+    project(by_3[...], w_key, w_value, keys, values, 2 * rows)
+    project(jnp.where(is_odd, before[...], after[...]), w_key, w_value, keys, values, 3 * rows)
+    edge = jnp.where(is_odd, after[:block_rows, :], before[rows - block_rows :, :])
+    project(edge, w_key, w_value, keys, values, 4 * rows)
+    parts = [part_at(keys, values, m * rows, rows, lambda m=m: bias[2 + m]) for m in range(3)]
+    parts.append(part_at(keys, values, 3 * rows, rows, lambda: bias[1], lambda: times[...]))
+    parts.append(part_at(keys, values, 4 * rows, block_rows, lambda: bias[5, :, :block_rows]))
     _, out, total = merge((tops[...], outs[...], sums[...]), attend(queries[...], parts, groups))
     context = (out / total).astype(jnp.bfloat16)
     mixed = matmul(context, w_out[...])
@@ -191,36 +177,36 @@
     expander_count,
 ):
     rows, width = features.shape
+    groups = local_blocks.shape[0]
+    block_rows = rows // groups
     peers = lax.axis_size("dom")
     levels = peers.bit_length() - 1
     match_total = expander_blocks.shape[0]
-    arrived = []
-    for matching in range(match_total):
-        apart = 1 << (matching * levels // match_total)
-        arrived.append(lax.ppermute(features, "dom", [(i, i ^ apart) for i in range(peers)]))
-    by_core, by_1, by_2, by_3 = arrived
-    ring = lax.ppermute(
-        features, "dom", [(i, (i + 1) % peers if i % 2 else (i - 1) % peers) for i in range(peers)]
-    )
     params = pltpu.CompilerParams(vmem_limit_bytes=48 * 2**20)
-    groups = local_blocks.shape[0]
-    wide = jax.ShapeDtypeStruct((width, width), jnp.bfloat16)
-    small = jax.ShapeDtypeStruct((rows, width), jnp.bfloat16)
-    state = jax.ShapeDtypeStruct((rows, width), jnp.float32)
+
+    def array(*shape, dtype=jnp.bfloat16):
+        return jax.ShapeDtypeStruct(shape, dtype)
 
     def pairs_of(total):
         return [pltpu.VMEM((total, width), jnp.bfloat16)] * 2
 
+    def exchange(matching):
+        apart = 1 << (matching * levels // match_total)
+        return lax.ppermute(features, "dom", [(i, i ^ apart) for i in range(peers)])
+
+    before = lax.ppermute(features, "dom", [(i, (i + 1) % peers) for i in range(peers)])
+    by_1, by_2, by_3 = (exchange(m) for m in range(1, match_total))
+    after = lax.ppermute(features, "dom", [(i, (i - 1) % peers) for i in range(peers)])
     far_blocks, far_count = jnp.transpose(expander_blocks, (1, 2, 0)), jnp.transpose(expander_count)
     tables = (local_blocks, local_count, far_blocks, far_count)
     inputs = (features, w_query, w_key, w_value, w_out, *tables)
+    state = (array(rows, width, dtype=jnp.float32),) * 3
     x, w_key, w_value, w_out, queries, bias, times, *states = pl.pallas_call(
         own_kernel,
         out_shape=(
-            small, wide, wide, wide, small,
-            jax.ShapeDtypeStruct((match_total + 2, groups, rows), jnp.float32),
-            jax.ShapeDtypeStruct((groups, rows), jnp.float32),
-            state, state, state,
+            array(rows, width), *[array(width, width)] * 3, array(rows, width),
+            array(match_total + 2, groups, rows, dtype=jnp.float32), array(groups, rows, dtype=jnp.float32),
+            *state,
         ),
         in_specs=[ANY] * len(inputs),
         out_specs=(VMEM,) * 10,
@@ -233,24 +219,20 @@
         compiler_params=params,
         name="own",
     )(*(pltpu.with_memory_space_constraint(a, pltpu.HBM) for a in inputs))
-    states = pl.pallas_call(
-        middle_kernel,
-        out_shape=(state,) * 3,
-        in_specs=[VMEM] * 11,
-        out_specs=(VMEM,) * 3,
-        scratch_shapes=pairs_of(3 * rows),
+    arrived = []
+    for one in (before, by_1, by_2, by_3, after):
+        one, queries = lax.optimization_barrier((one, queries))
+        arrived.append(one)
+    before, by_1, by_2, by_3, after = arrived
+    return pl.pallas_call(
+        rest_kernel,
+        out_shape=array(rows, width, dtype=features.dtype),
+        in_specs=[VMEM] * 15,
+        out_specs=VMEM,
+        scratch_shapes=pairs_of(4 * rows + block_rows),
         compiler_params=params,
-        name="middle",
-    )(by_core, by_1, by_2, w_key, w_value, queries, bias, times, *states)
-    return pl.pallas_call(
-        last_kernel,
-        out_shape=jax.ShapeDtypeStruct((rows, width), features.dtype),
-        in_specs=[VMEM] * 11,
-        out_specs=VMEM,
-        scratch_shapes=pairs_of(rows + rows // groups),
-        compiler_params=params,
-        name="last",
-    )(x, by_3, ring, w_key, w_value, w_out, queries, bias, *states)
+        name="rest",
+    )(x, before, by_1, by_2, by_3, after, w_key, w_value, w_out, queries, bias, times, *states)
 
 
 def solution(mesh):

time: 17.1 us -> 16.3 us (0.953)
  waiting for transfers between devices: 1.65 us -> 0.38 us
  starting transfers between devices: 7.7 us -> 8.79 us
  Pallas kernels: 7.58 us -> 6.89 us
    ppermute x5, waiting for transfers between devices: 1.65 us -> 0.38 us  [the longest x1 0.37 us: shards(): lax.ppermute(features, 'dom', [(i, (i - 1) % peers) for i in range(peers)])]
    ppermute x5, starting transfers between devices: 7.7 us -> 8.79 us  [the longest x3 5.61 us: exchange(): return lax.ppermute(features, 'dom', [(i, i ^ apart) for i in range(peers)])]
    pallas_call x3 -> x2, Pallas kernels: 7.58 us -> 6.89 us  [the longest x1 4.43 us: shards(): pl.pallas_call(rest_kernel, out_shape=array(rows, width, dtype=features.d...]
  transfers between devices with their start and end apart: 5 -> 5, of which waited for: 1 -> 1; matrix products, arithmetic and copies ran while one was open for 0% -> 0% of each run, Pallas kernels for 29% -> 15%
where the time goes in v6:
time: 16.3 us; the launch traced here: 16.1 us
  starting transfers between devices  8.79 us (54%)
  Pallas kernels  6.89 us (42%)
  waiting for transfers between devices  0.38 us (2%)
    ppermute x3, starting transfers between devices, exchange(): return lax.ppermute(features, 'dom', [(i, i ^ apart) for i in range(peers)])  5.61 us
    pallas_call x1, Pallas kernels, shards(): pl.pallas_call(rest_kernel, out_shape=array(rows, width, dtype=features.d...  4.43 us
    ppermute x1, starting transfers between devices, shards(): lax.ppermute(features, 'dom', [(i, (i - 1) % peers) for i in range(peers)])  2.73 us
    pallas_call x1, Pallas kernels, shards(): pl.pallas_call(own_kernel, out_shape=(array(rows, width), *[array(width,...  2.47 us
    ppermute x1, starting transfers between devices, shards(): lax.ppermute(features, 'dom', [(i, (i + 1) % peers) for i in range(peers)])  0.45 us
    ppermute x1, waiting for transfers between devices, shards(): lax.ppermute(features, 'dom', [(i, (i - 1) % peers) for i in range(peers)])  0.37 us
  transfers between devices with their start and end apart: 5, of which 1 were waited for; matrix products, arithmetic and copies ran while one was open for 0% of the time, Pallas kernels for 15%

profile of v6, /device:TPU:0, one launch (start us, length us, event | category | flops | bytes accessed | tf_op | source)
XLA Modules:
  0.0 16.1 jit_solution(15982157813756022273)
XLA Ops:
  0.0 0.5 %collective-permute-start = (bf16[256,256]{1,0:T(8,128)(2,1)}, bf16[256,256]{1,0:T(8,128)(2,1)S(1)}, u32[]{:S(2)}, u32[]{:S(2)}) collective-permute-start(bf16[256,256]{1,0:T(8,128)(2,1)} %features.1), channel_id=1, source_target_pairs={{0,1},{1,2},{2,3},{3,4},{4,5},{5,6},{6,7},{7,8},{8,9},{9,10},{10,1... | collective-permute-start | bytes 393224 | tf_op jit(solution)/shard_map/ppermute | solution.py:197
  0.5 2.5 %collective-permute-start.1 = (bf16[256,256]{1,0:T(8,128)(2,1)}, bf16[256,256]{1,0:T(8,128)(2,1)S(1)}, u32[]{:S(2)}, u32[]{:S(2)}) collective-permute-start(bf16[256,256]{1,0:T(8,128)(2,1)} %features.1), channel_id=1, source_target_pairs={{0,2},{1,3},{2,0},{3,1},{4,6},{5,7},{6,4},{7,5},{8,10},{9,11},{10,... | collective-permute-start | bytes 393224 | tf_op jit(solution)/shard_map/ppermute | solution.py:195
  3.0 1.5 %collective-permute-start.2 = (bf16[256,256]{1,0:T(8,128)(2,1)}, bf16[256,256]{1,0:T(8,128)(2,1)S(1)}, u32[]{:S(2)}, u32[]{:S(2)}) collective-permute-start(bf16[256,256]{1,0:T(8,128)(2,1)} %features.1), channel_id=1, source_target_pairs={{0,4},{1,5},{2,6},{3,7},{4,0},{5,1},{6,2},{7,3},{8,12},{9,13},{10,... | collective-permute-start | bytes 393224 | tf_op jit(solution)/shard_map/ppermute | solution.py:195
  4.5 1.6 %collective-permute-start.3 = (bf16[256,256]{1,0:T(8,128)(2,1)}, bf16[256,256]{1,0:T(8,128)(2,1)S(1)}, u32[]{:S(2)}, u32[]{:S(2)}) collective-permute-start(bf16[256,256]{1,0:T(8,128)(2,1)} %features.1), channel_id=1, source_target_pairs={{0,8},{1,9},{2,10},{3,11},{4,12},{5,13},{6,14},{7,15},{8,0},{9,1},... | collective-permute-start | bytes 393224 | tf_op jit(solution)/shard_map/ppermute | solution.py:195
  6.1 2.7 %collective-permute-start.4 = (bf16[256,256]{1,0:T(8,128)(2,1)}, bf16[256,256]{1,0:T(8,128)(2,1)S(1)}, u32[]{:S(2)}, u32[]{:S(2)}) collective-permute-start(bf16[256,256]{1,0:T(8,128)(2,1)} %features.1), channel_id=1, source_target_pairs={{0,31},{1,0},{2,1},{3,2},{4,3},{5,4},{6,5},{7,6},{8,7},{9,8},{10,9... | collective-permute-start | bytes 393224 | tf_op jit(solution)/shard_map/ppermute | solution.py:199
  8.8 2.5 %own.1 = (bf16[256,256]{1,0:T(8,128)(2,1)S(1)}, bf16[256,256]{1,0:T(8,128)(2,1)S(1)}, bf16[256,256]{1,0:T(8,128)(2,1)S(1)}, bf16[256,256]{1,0:T(8,128)(2,1)S(1)}...) custom-call(bf16[256,256]{1,0:T(8,128)(2,1)} %features.1, ...), custom_call_target="tpu_custom_call" | custom-call | tf_op jit(solution)/shard_map/own/pallas_call | solution.py:204
  11.3 0.0 collective-permute-done.before
  11.3 0.0 collective-permute-done.1.by_1
  11.3 0.0 collective-permute-done.2.by_2
  11.3 0.0 collective-permute-done.3.by_3
  11.3 0.4 %collective-permute-done.4.after = bf16[256,256]{1,0:T(8,128)(2,1)S(1)} collective-permute-done((bf16[256,256]{1,0:T(8,128)(2,1)}, bf16[256,256]{1,0:T(8,128)(2,1)S(1)}, u32[]{:S(2)}, u32[]{:S(2)}) %collective-permute-start.4) | collective-permute-done | bytes 131104 | tf_op jit(solution)/shard_map/ppermute | solution.py:199
  11.7 4.4 %rest.1 = bf16[256,256]{1,0:T(8,128)(2,1)} custom-call(bf16[256,256]{1,0:T(8,128)(2,1)S(1)} %get-tuple-element.25.features, bf16[256,256]{1,0:T(8,128)(2,1)S(1)} %collective-permute-done.before, bf16[256,256]{1,0:T(8,128)(2,1)S(1)} %collective-permute-done.1.by_1, bf16[256,256]{1,0:T(8,128)(2,1)S(1)} %collective-permute-done.2.by_2, ...), custom_call_target="tpu_custom_call" | custom-call | tf_op jit(solution)/shard_map/rest/pallas_call | solution.py:227
Async XLA Ops:
  0.0 11.3 %collective-permute-start = (bf16[256,256]{1,0:T(8,128)(2,1)}, bf16[256,256]{1,0:T(8,128)(2,1)S(1)}, u32[]{:S(2)}, u32[]{:S(2)}) collective-permute-start(bf16[256,256]{1,0:T(8,128)(2,1)} %features.1), channel_id=1, source_target_pairs={{0,1},{1,2},{2,3},{3,4},{4,5},{5,6},{6,7},{7,8},{8,9},{9,10},{10,1... | collective-permute-start | bytes 393224 | tf_op jit(solution)/shard_map/ppermute | solution.py:197
  0.5 10.8 %collective-permute-start.1 = (bf16[256,256]{1,0:T(8,128)(2,1)}, bf16[256,256]{1,0:T(8,128)(2,1)S(1)}, u32[]{:S(2)}, u32[]{:S(2)}) collective-permute-start(bf16[256,256]{1,0:T(8,128)(2,1)} %features.1), channel_id=1, source_target_pairs={{0,2},{1,3},{2,0},{3,1},{4,6},{5,7},{6,4},{7,5},{8,10},{9,11},{10,... | collective-permute-start | bytes 393224 | tf_op jit(solution)/shard_map/ppermute | solution.py:195
  3.0 8.3 %collective-permute-start.2 = (bf16[256,256]{1,0:T(8,128)(2,1)}, bf16[256,256]{1,0:T(8,128)(2,1)S(1)}, u32[]{:S(2)}, u32[]{:S(2)}) collective-permute-start(bf16[256,256]{1,0:T(8,128)(2,1)} %features.1), channel_id=1, source_target_pairs={{0,4},{1,5},{2,6},{3,7},{4,0},{5,1},{6,2},{7,3},{8,12},{9,13},{10,... | collective-permute-start | bytes 393224 | tf_op jit(solution)/shard_map/ppermute | solution.py:195
  4.5 6.8 %collective-permute-start.3 = (bf16[256,256]{1,0:T(8,128)(2,1)}, bf16[256,256]{1,0:T(8,128)(2,1)S(1)}, u32[]{:S(2)}, u32[]{:S(2)}) collective-permute-start(bf16[256,256]{1,0:T(8,128)(2,1)} %features.1), channel_id=1, source_target_pairs={{0,8},{1,9},{2,10},{3,11},{4,12},{5,13},{6,14},{7,15},{8,0},{9,1},... | collective-permute-start | bytes 393224 | tf_op jit(solution)/shard_map/ppermute | solution.py:195
  6.1 5.6 %collective-permute-start.4 = (bf16[256,256]{1,0:T(8,128)(2,1)}, bf16[256,256]{1,0:T(8,128)(2,1)S(1)}, u32[]{:S(2)}, u32[]{:S(2)}) collective-permute-start(bf16[256,256]{1,0:T(8,128)(2,1)} %features.1), channel_id=1, source_target_pairs={{0,31},{1,0},{2,1},{3,2},{4,3},{5,4},{6,5},{7,6},{8,7},{9,8},{10,9... | collective-permute-start | bytes 393224 | tf_op jit(solution)/shard_map/ppermute | solution.py:199

commit v7 on v6

v7 whole, which is shorter than its diff:
```python
import jax
import jax.numpy as jnp
from jax import lax
from jax.experimental import pallas as pl
from jax.experimental.pallas import tpu as pltpu
from jax.sharding import PartitionSpec as P

HEADS = 8
EPSILON = 1e-06
LOW = -1e30

FIRST = ('own', 'core', 'x')
MIDDLE = ('ring',)
LAST = ('z', 'y')
BIAS_ROW = {"own": 0, "core": 1, "x": 2, "y": 3, "z": 4, "ring": 5}

VMEM = pl.BlockSpec(memory_space=pltpu.VMEM)
ANY = pl.BlockSpec(memory_space=pl.ANY)

def matmul(a, b):
    return jnp.dot(a, b, preferred_element_type=jnp.float32)


def matmul_nt(a, b):
    return lax.dot_general(a, b, (((1,), (1,)), ((), ())), preferred_element_type=jnp.float32)


def used(blocks, count, position, most):
    total = jnp.int32(0)
    for j in range(most):
        total = total + ((blocks(j) == position) & (j < count)).astype(jnp.int32)
    return total


def along_keys(values, block_rows):
    return jnp.concatenate([jnp.full((1, block_rows), v, jnp.float32) for v in values], axis=1)


def attend(queries, parts, groups):
    rows, width = queries.shape
    lanes = width // 2
    count = HEADS // 2
    heads = lax.broadcasted_iota(jnp.int32, (1, lanes), 1) // (lanes // count)
    zero = jnp.zeros((), queries.dtype)

    def by_group(array):
        return array.reshape(count, groups, rows // groups, array.shape[-1])

    cuts = [slice(0, lanes), slice(lanes, width)]
    masked = [
        jnp.concatenate([jnp.where(heads == h, queries[:, cut], zero) for h in range(count)], axis=0) for cut in cuts
    ]
    scores, tops, sums = [[], []], [None, None], [None, None]
    for keys, _, bias, _ in parts:
        for f, cut in enumerate(cuts):
            part = by_group(matmul_nt(masked[f], keys()[:, cut])) + bias()[None, :, None, :]
            part = part.reshape(count * rows, part.shape[-1])
            scores[f].append(part)
            top = jnp.max(part, axis=1, keepdims=True)
            tops[f] = top if tops[f] is None else jnp.maximum(tops[f], top)
    for i, (_, values, _, times) in enumerate(parts):
        for f, cut in enumerate(cuts):
            weights = jnp.exp(scores[f][i] - tops[f])
            if times is not None:
                weights = (by_group(weights) * times()[None, :, None, :]).reshape(weights.shape)
            weights = weights.astype(jnp.bfloat16)
            right = values()[:, cut]
            right = jnp.concatenate([right, jnp.ones_like(right)], axis=1)
            sums[f] = matmul(weights, right) if sums[f] is None else sums[f] + matmul(weights, right)
    state = [[], [], []]
    for f in range(2):
        top = out = total = None
        for h in range(count):
            block = sums[f][h * rows : (h + 1) * rows]
            one = jnp.broadcast_to(tops[f][h * rows : (h + 1) * rows], (rows, lanes)), block[:, :lanes], block[:, lanes:]
            if h == 0:
                top, out, total = one
            else:
                top, out, total = (jnp.where(heads == h, new, old) for new, old in zip(one, (top, out, total)))
        for array, half in zip(state, (top, out, total)):
            array.append(half)
    return tuple(jnp.concatenate(halves, axis=1) for halves in state)


def merge(one, other):
    top = jnp.maximum(one[0], other[0])
    left, right = jnp.exp(one[0] - top), jnp.exp(other[0] - top)
    return top, left * one[1] + right * other[1], left * one[2] + right * other[2]


def project(features, w_key, w_value, keys, values, start):
    rows = pl.ds(start, features.shape[0])
    keys[rows, :] = matmul(features, w_key[...]).astype(keys.dtype)
    values[rows, :] = matmul(features, w_value[...]).astype(values.dtype)


def parts_of(kinds, refs, w_key, w_value, bias, times, keys, values):
    rows = refs[0].shape[0]
    groups = times.shape[0]
    block_rows = rows // groups
    parts = []
    start = 0
    for kind, ref in zip(kinds, refs):
        count = block_rows if kind == "ring" else rows
        if kind == "ring":
            is_odd = lax.rem(lax.axis_index("dom"), 2) == 1
            first = pl.multiple_of(jnp.where(is_odd, 0, rows - block_rows), block_rows)
            arrival = ref[pl.ds(first, block_rows), :]
        else:
            arrival = ref[...]
        project(arrival, w_key, w_value, keys, values, start)
        where = pl.ds(start, count)
        row = BIAS_ROW[kind]
        parts.append((
            lambda where=where: keys[where, :],
            lambda where=where: values[where, :],
            lambda row=row, count=count: bias[row, :, :count],
            (lambda: times[...]) if kind == "core" else None,
        ))
        start += count
    return parts


def first_kernel(
    features, w_query, w_key, w_value, w_out, local_blocks, local_count, expander_blocks, expander_count, *refs
):
    arrivals, refs = refs[: len(FIRST) - 1], refs[len(FIRST) - 1 :]
    (
        x, key_copy, value_copy, out_copy, queries, bias, times, tops, outs, sums,
        query_copy, keys, values, blocks, count, far_blocks, far_count, sems,
    ) = refs
    pairs = (
        (features, x), (w_query, query_copy), (w_key, key_copy), (w_value, value_copy), (local_blocks, blocks),
        (local_count, count), (expander_blocks, far_blocks), (expander_count, far_count), (w_out, out_copy),
    )
    copies = [pltpu.make_async_copy(a, b, sems.at[i]) for i, (a, b) in enumerate(pairs)]
    for copy in copies:
        copy.start()
    groups, most = blocks.shape
    most_far, matchings = far_blocks.shape[1:]
    rows, width = x.shape
    block_rows = rows // groups
    size = width // HEADS
    is_odd = lax.rem(lax.axis_index("dom"), 2) == 1
    for copy in copies[4:8]:
        copy.wait()
    for g in range(groups):
        near = [used(lambda j: blocks[g, j], count[g], position, most) for position in range(groups + 2)]
        takes = [near[1:-1]]
        for m in range(matchings):
            takes.append(
                [used(lambda j: far_blocks[g, j, m], far_count[g, m], b, most_far) for b in range(groups)]
            )
        takes[1][0] = takes[1][0] + jnp.where(is_odd, 0, near[-1])
        takes[1][-1] = takes[1][-1] + jnp.where(is_odd, near[0], 0)
        takes.append([jnp.where(is_odd, near[-1], near[0])] * groups)
        for p, take in enumerate(takes):
            bias[p, g : g + 1, :] = along_keys([jnp.where(t > 0, 0.0, LOW) for t in take], block_rows)
        times[g : g + 1, :] = along_keys([t.astype(jnp.float32) for t in takes[1]], block_rows)
    for copy in copies[:4]:
        copy.wait()
    q = (matmul(x[...], query_copy[...]) * (float(size) ** -0.5)).astype(jnp.bfloat16)
    queries[...] = q
    parts = parts_of(FIRST, (x, *arrivals), key_copy, value_copy, bias, times, keys, values)
    tops[...], outs[...], sums[...] = attend(q, parts, groups)
    copies[8].wait()


def middle_kernel(*refs):
    arrivals, refs = refs[: len(MIDDLE)], refs[len(MIDDLE) :]
    w_key, w_value, queries, bias, times, tops, outs, sums, new_tops, new_outs, new_sums, keys, values = refs
    parts = parts_of(MIDDLE, arrivals, w_key, w_value, bias, times, keys, values)
    state = attend(queries[...], parts, times.shape[0])
    new_tops[...], new_outs[...], new_sums[...] = merge((tops[...], outs[...], sums[...]), state)


def last_kernel(*refs):
    arrivals, refs = refs[: len(LAST)], refs[len(LAST) :]
    w_key, w_value, queries, bias, times, tops, outs, sums, features, w_out, result, keys, values = refs
    parts = parts_of(LAST, arrivals, w_key, w_value, bias, times, keys, values)
    state = attend(queries[...], parts, times.shape[0])
    _, out, total = merge((tops[...], outs[...], sums[...]), state)
    context = (out / total).astype(jnp.bfloat16)
    mixed = matmul(context, w_out[...])
    normed = mixed * lax.rsqrt(jnp.mean(mixed * mixed, axis=1, keepdims=True) + EPSILON)
    result[...] = (features[...].astype(jnp.float32) + normed).astype(result.dtype)


def shards(
    features,
    w_query,
    w_key,
    w_value,
    w_out,
    local_blocks,
    local_count,
    expander_blocks,
    expander_count,
):
    rows, width = features.shape
    groups = local_blocks.shape[0]
    block_rows = rows // groups
    peers = lax.axis_size("dom")
    levels = peers.bit_length() - 1
    match_total = expander_blocks.shape[0]
    params = pltpu.CompilerParams(vmem_limit_bytes=48 * 2**20)

    def array(*shape, dtype=jnp.bfloat16):
        return jax.ShapeDtypeStruct(shape, dtype)

    def pairs_of(total):
        return [pltpu.VMEM((total, width), jnp.bfloat16)] * 2

    def exchange(matching):
        apart = 1 << (matching * levels // match_total)
        return lax.ppermute(features, "dom", [(i, i ^ apart) for i in range(peers)])

    arrived = {
        "core": exchange(0),
        "x": exchange(1),
        "y": exchange(2),
        "z": exchange(3),
        "ring": lax.ppermute(
            features, "dom", [(i, (i + 1) % peers if i % 2 else (i - 1) % peers) for i in range(peers)]
        ),
    }

    def in_order(kinds, after):
        gathered = []
        for kind in kinds:
            one, after = lax.optimization_barrier((arrived[kind], after))
            gathered.append(one)
        return gathered, after

    far_blocks, far_count = jnp.transpose(expander_blocks, (1, 2, 0)), jnp.transpose(expander_count)
    state = (array(rows, width, dtype=jnp.float32),) * 3
    tables = (local_blocks, local_count, far_blocks, far_count)
    inputs = (features, w_query, w_key, w_value, w_out, *tables)
    near, _ = in_order(FIRST[1:], features)
    x, w_key, w_value, w_out, queries, bias, times, *states = pl.pallas_call(
        first_kernel,
        out_shape=(
            array(rows, width), *[array(width, width)] * 3, array(rows, width),
            array(match_total + 2, groups, rows, dtype=jnp.float32), array(groups, rows, dtype=jnp.float32),
            *state,
        ),
        in_specs=[ANY] * len(inputs) + [VMEM] * len(near),
        out_specs=(VMEM,) * 10,
        scratch_shapes=[
            pltpu.VMEM((width, width), jnp.bfloat16),
            *pairs_of(len(FIRST) * rows),
            *(pltpu.SMEM(t.shape, jnp.int32) for t in tables),
            pltpu.SemaphoreType.DMA((len(inputs),)),
        ],
        compiler_params=params,
        name="first",
    )(*(pltpu.with_memory_space_constraint(a, pltpu.HBM) for a in inputs), *near)
    near, queries = in_order(MIDDLE, queries)
    states = pl.pallas_call(
        middle_kernel,
        out_shape=state,
        in_specs=[VMEM] * (len(near) + 8),
        out_specs=(VMEM,) * 3,
        scratch_shapes=pairs_of(len(MIDDLE) * rows),
        compiler_params=params,
        name="middle",
    )(*near, w_key, w_value, queries, bias, times, *states)
    near, states = in_order(LAST, states)
    return pl.pallas_call(
        last_kernel,
        out_shape=array(rows, width, dtype=features.dtype),
        in_specs=[VMEM] * (len(near) + 10),
        out_specs=VMEM,
        scratch_shapes=pairs_of(len(LAST) * rows),
        compiler_params=params,
        name="last",
    )(*near, w_key, w_value, queries, bias, times, *states, x, w_out)


def solution(mesh):
    in_specs = (
        P("dom", None),
        P(),
        P(),
        P(),
        P(),
        P("dom", None),
        P("dom"),
        P(None, "dom", None),
        P(None, "dom"),
    )
    out_specs = P("dom", None)
    return jax.shard_map(shards, mesh=mesh, in_specs=in_specs, out_specs=out_specs, check_vma=False)
```

time: 16.3 us -> 15.5 us (0.951)
  starting transfers between devices: 8.79 us -> 7.31 us
  waiting for transfers between devices: 0.38 us -> 0.93 us
  Pallas kernels: 6.89 us -> 7.08 us
    ppermute x3 -> x4, starting transfers between devices: 5.61 us -> 2.95 us  [exchange(): return lax.ppermute(features, 'dom', [(i, i ^ apart) for i in range(peers)])]
    ppermute x2 -> x1, starting transfers between devices: 3.18 us -> 4.36 us  [shards(): lax.ppermute(features, 'dom', [(i, (i + 1) % peers if i % 2 else (i - 1)...]
    ppermute x3 -> x4, waiting for transfers between devices: 0.01 us -> 0.65 us  [exchange(): return lax.ppermute(features, 'dom', [(i, i ^ apart) for i in range(peers)])]
    pallas_call x2 -> x3, Pallas kernels: 6.89 us -> 7.08 us  [the longest x1 3.53 us: shards(): pl.pallas_call(first_kernel, out_shape=(array(rows, width), *[array(width...]
    ppermute x2 -> x1, waiting for transfers between devices: 0.37 us -> 0.28 us  [shards(): lax.ppermute(features, 'dom', [(i, (i + 1) % peers if i % 2 else (i - 1)...]
  transfers between devices with their start and end apart: 5 -> 5, of which waited for: 1 -> 4; matrix products, arithmetic and copies ran while one was open for 0% -> 0% of each run, Pallas kernels for 15% -> 29%
where the time goes in v7:
time: 15.5 us; the launch traced here: 15.3 us
  starting transfers between devices  7.31 us (47%)
  Pallas kernels  7.08 us (46%)
  waiting for transfers between devices  0.93 us (6%)
    ppermute x1, starting transfers between devices, shards(): lax.ppermute(features, 'dom', [(i, (i + 1) % peers if i % 2 else (i - 1)...  4.36 us
    pallas_call x1, Pallas kernels, shards(): pl.pallas_call(first_kernel, out_shape=(array(rows, width), *[array(width...  3.53 us
    ppermute x4, starting transfers between devices, exchange(): return lax.ppermute(features, 'dom', [(i, i ^ apart) for i in range(peers)])  2.95 us
    pallas_call x1, Pallas kernels, shards(): pl.pallas_call(last_kernel, out_shape=array(rows, width, dtype=features.d...  2.65 us
    pallas_call x1, Pallas kernels, shards(): pl.pallas_call(middle_kernel, out_shape=state, in_specs=[VMEM] * (len(nea...  0.91 us
    ppermute x4, waiting for transfers between devices, exchange(): return lax.ppermute(features, 'dom', [(i, i ^ apart) for i in range(peers)])  0.65 us
  transfers between devices with their start and end apart: 5, of which 4 were waited for; matrix products, arithmetic and copies ran while one was open for 0% of the time, Pallas kernels for 29%

profile of v7, /device:TPU:0, one launch (start us, length us, event | category | flops | bytes accessed | tf_op | source)
XLA Modules:
  0.0 15.3 jit_solution(3746082205516968720)
XLA Ops:
  0.0 0.5 %collective-permute-start.2 = (bf16[256,256]{1,0:T(8,128)(2,1)}, bf16[256,256]{1,0:T(8,128)(2,1)S(1)}, u32[]{:S(2)}, u32[]{:S(2)}) collective-permute-start(bf16[256,256]{1,0:T(8,128)(2,1)} %features.1), channel_id=1, source_target_pairs={{0,1},{1,0},{2,3},{3,2},{4,5},{5,4},{6,7},{7,6},{8,9},{9,8},{10,11... | collective-permute-start | bytes 393224 | tf_op jit(solution)/shard_map/ppermute | solution.py:216
  0.5 2.5 %collective-permute-start.3 = (bf16[256,256]{1,0:T(8,128)(2,1)}, bf16[256,256]{1,0:T(8,128)(2,1)S(1)}, u32[]{:S(2)}, u32[]{:S(2)}) collective-permute-start(bf16[256,256]{1,0:T(8,128)(2,1)} %features.1), channel_id=1, source_target_pairs={{0,2},{1,3},{2,0},{3,1},{4,6},{5,7},{6,4},{7,5},{8,10},{9,11},{10,... | collective-permute-start | bytes 393224 | tf_op jit(solution)/shard_map/ppermute | solution.py:216
  2.9 4.4 %collective-permute-start.1 = (bf16[256,256]{1,0:T(8,128)(2,1)}, bf16[256,256]{1,0:T(8,128)(2,1)S(1)}, u32[]{:S(2)}, u32[]{:S(2)}) collective-permute-start(bf16[256,256]{1,0:T(8,128)(2,1)} %features.1), channel_id=1, source_target_pairs={{0,31},{1,2},{2,1},{3,4},{4,3},{5,6},{6,5},{7,8},{8,7},{9,10},{10,... | collective-permute-start | bytes 393224 | tf_op jit(solution)/shard_map/ppermute | solution.py:223
  7.3 0.0 collective-permute-start
  7.3 0.0 collective-permute-start.4
  7.3 0.0 collective-permute-done.2.refs_0_
  7.3 0.2 %collective-permute-done.3.refs_1_ = bf16[256,256]{1,0:T(8,128)(2,1)S(1)} collective-permute-done((bf16[256,256]{1,0:T(8,128)(2,1)}, bf16[256,256]{1,0:T(8,128)(2,1)S(1)}, u32[]{:S(2)}, u32[]{:S(2)}) %collective-permute-start.3) | collective-permute-done | bytes 131104 | tf_op jit(solution)/shard_map/ppermute | solution.py:216
  7.5 3.5 %first.1 = (bf16[256,256]{1,0:T(8,128)(2,1)S(1)}, bf16[256,256]{1,0:T(8,128)(2,1)S(1)}, bf16[256,256]{1,0:T(8,128)(2,1)S(1)}, bf16[256,256]{1,0:T(8,128)(2,1)S(1...) custom-call(bf16[256,256]{1,0:T(8,128)(2,1)} %features.1, ...), custom_call_target="tpu_custom_call" | custom-call | tf_op jit(solution)/shard_map/first/pallas_call | solution.py:240
  11.0 0.3 %collective-permute-done.1.refs_0_ = bf16[256,256]{1,0:T(8,128)(2,1)S(1)} collective-permute-done((bf16[256,256]{1,0:T(8,128)(2,1)}, bf16[256,256]{1,0:T(8,128)(2,1)S(1)}, u32[]{:S(2)}, u32[]{:S(2)}) %collective-permute-start.1) | collective-permute-done | bytes 131104 | tf_op jit(solution)/shard_map/ppermute | solution.py:223
  11.3 0.9 %middle.1 = (f32[256,256]{1,0:T(8,128)S(1)}, f32[256,256]{1,0:T(8,128)S(1)}, f32[256,256]{1,0:T(8,128)S(1)}) custom-call(bf16[256,256]{1,0:T(8,128)(2,1)S(1)} %collective-permute-done.1.refs_0_, bf16[256,256]{1,0:T(8,128)(2,1)S(1)} %get-tuple-element.32.refs_1_.refs_2_, bf16[256,256]{1,0:T(8,128)(2,1)S(1)} %get-tuple-element.33.refs_2_.refs_3_, ...), custom_call_target="tpu_custom_call" | custom-call | tf_op jit(solution)/shard_map/middle/pallas_call | solution.py:259
  12.2 0.2 %collective-permute-done.refs_0_ = bf16[256,256]{1,0:T(8,128)(2,1)S(1)} collective-permute-done((bf16[256,256]{1,0:T(8,128)(2,1)}, bf16[256,256]{1,0:T(8,128)(2,1)S(1)}, u32[]{:S(2)}, u32[]{:S(2)}) %collective-permute-start) | collective-permute-done | bytes 131104 | tf_op jit(solution)/shard_map/ppermute | solution.py:216
  12.5 0.2 %collective-permute-done.4.refs_1_ = bf16[256,256]{1,0:T(8,128)(2,1)S(1)} collective-permute-done((bf16[256,256]{1,0:T(8,128)(2,1)}, bf16[256,256]{1,0:T(8,128)(2,1)S(1)}, u32[]{:S(2)}, u32[]{:S(2)}) %collective-permute-start.4) | collective-permute-done | bytes 131104 | tf_op jit(solution)/shard_map/ppermute | solution.py:216
  12.7 2.6 %last.1 = bf16[256,256]{1,0:T(8,128)(2,1)} custom-call(bf16[256,256]{1,0:T(8,128)(2,1)S(1)} %collective-permute-done.refs_0_, bf16[256,256]{1,0:T(8,128)(2,1)S(1)} %collective-permute-done.4.refs_1_, bf16[256,256]{1,0:T(8,128)(2,1)S(1)} %get-tuple-element.32.refs_1_.refs_2_, bf16[256,256]{1,0:T(8,128)(2,1)S(1)} %get-tuple-element.33.refs_2_.refs_3_, ...), custom_call_target="tpu_custom_call" | custom-call | tf_op jit(solution)/shard_map/last/pallas_call | solution.py:269
Async XLA Ops:
  0.0 7.3 %collective-permute-start.2 = (bf16[256,256]{1,0:T(8,128)(2,1)}, bf16[256,256]{1,0:T(8,128)(2,1)S(1)}, u32[]{:S(2)}, u32[]{:S(2)}) collective-permute-start(bf16[256,256]{1,0:T(8,128)(2,1)} %features.1), channel_id=1, source_target_pairs={{0,1},{1,0},{2,3},{3,2},{4,5},{5,4},{6,7},{7,6},{8,9},{9,8},{10,11... | collective-permute-start | bytes 393224 | tf_op jit(solution)/shard_map/ppermute | solution.py:216
  0.5 7.0 %collective-permute-start.3 = (bf16[256,256]{1,0:T(8,128)(2,1)}, bf16[256,256]{1,0:T(8,128)(2,1)S(1)}, u32[]{:S(2)}, u32[]{:S(2)}) collective-permute-start(bf16[256,256]{1,0:T(8,128)(2,1)} %features.1), channel_id=1, source_target_pairs={{0,2},{1,3},{2,0},{3,1},{4,6},{5,7},{6,4},{7,5},{8,10},{9,11},{10,... | collective-permute-start | bytes 393224 | tf_op jit(solution)/shard_map/ppermute | solution.py:216
  2.9 8.4 %collective-permute-start.1 = (bf16[256,256]{1,0:T(8,128)(2,1)}, bf16[256,256]{1,0:T(8,128)(2,1)S(1)}, u32[]{:S(2)}, u32[]{:S(2)}) collective-permute-start(bf16[256,256]{1,0:T(8,128)(2,1)} %features.1), channel_id=1, source_target_pairs={{0,31},{1,2},{2,1},{3,4},{4,3},{5,6},{6,5},{7,8},{8,7},{9,10},{10,... | collective-permute-start | bytes 393224 | tf_op jit(solution)/shard_map/ppermute | solution.py:223
  7.3 5.2 %collective-permute-start = (bf16[256,256]{1,0:T(8,128)(2,1)}, bf16[256,256]{1,0:T(8,128)(2,1)S(1)}, u32[]{:S(2)}, u32[]{:S(2)}) collective-permute-start(bf16[256,256]{1,0:T(8,128)(2,1)} %features.1), channel_id=1, source_target_pairs={{0,8},{1,9},{2,10},{3,11},{4,12},{5,13},{6,14},{7,15},{8,0},{9,1},... | collective-permute-start | bytes 393224 | tf_op jit(solution)/shard_map/ppermute | solution.py:216
  7.3 5.4 %collective-permute-start.4 = (bf16[256,256]{1,0:T(8,128)(2,1)}, bf16[256,256]{1,0:T(8,128)(2,1)S(1)}, u32[]{:S(2)}, u32[]{:S(2)}) collective-permute-start(bf16[256,256]{1,0:T(8,128)(2,1)} %features.1), channel_id=1, source_target_pairs={{0,4},{1,5},{2,6},{3,7},{4,0},{5,1},{6,2},{7,3},{8,12},{9,13},{10,... | collective-permute-start | bytes 393224 | tf_op jit(solution)/shard_map/ppermute | solution.py:216

commit v8 on v7

--- a/solution.py
+++ b/solution.py
@@ -1,3 +1,5 @@
+import functools
+
 import jax
 import jax.numpy as jnp
 from jax import lax
@@ -9,9 +11,9 @@
 EPSILON = 1e-06
 LOW = -1e30
 
-FIRST = ('own', 'core', 'x')
-MIDDLE = ('ring',)
-LAST = ('z', 'y')
+FIRST = ('own',)
+MIDDLE = (('core', 'y'), ('ring',))
+LAST = ('x', 'z')
 BIAS_ROW = {"own": 0, "core": 1, "x": 2, "y": 3, "z": 4, "ring": 5}
 
 VMEM = pl.BlockSpec(memory_space=pltpu.VMEM)
@@ -51,15 +53,15 @@
         jnp.concatenate([jnp.where(heads == h, queries[:, cut], zero) for h in range(count)], axis=0) for cut in cuts
     ]
     scores, tops, sums = [[], []], [None, None], [None, None]
-    for keys, _, bias, _ in parts:
-        for f, cut in enumerate(cuts):
+    for f, cut in enumerate(cuts):
+        for keys, _, bias, _ in parts:
             part = by_group(matmul_nt(masked[f], keys()[:, cut])) + bias()[None, :, None, :]
             part = part.reshape(count * rows, part.shape[-1])
             scores[f].append(part)
             top = jnp.max(part, axis=1, keepdims=True)
             tops[f] = top if tops[f] is None else jnp.maximum(tops[f], top)
-    for i, (_, values, _, times) in enumerate(parts):
-        for f, cut in enumerate(cuts):
+    for f, cut in enumerate(cuts):
+        for i, (_, values, _, times) in enumerate(parts):
             weights = jnp.exp(scores[f][i] - tops[f])
             if times is not None:
                 weights = (by_group(weights) * times()[None, :, None, :]).reshape(weights.shape)
@@ -166,10 +168,10 @@
     copies[8].wait()
 
 
-def middle_kernel(*refs):
-    arrivals, refs = refs[: len(MIDDLE)], refs[len(MIDDLE) :]
+def middle_kernel(kinds, *refs):
+    arrivals, refs = refs[: len(kinds)], refs[len(kinds) :]
     w_key, w_value, queries, bias, times, tops, outs, sums, new_tops, new_outs, new_sums, keys, values = refs
-    parts = parts_of(MIDDLE, arrivals, w_key, w_value, bias, times, keys, values)
+    parts = parts_of(kinds, arrivals, w_key, w_value, bias, times, keys, values)
     state = attend(queries[...], parts, times.shape[0])
     new_tops[...], new_outs[...], new_sums[...] = merge((tops[...], outs[...], sums[...]), state)
 
@@ -255,16 +257,17 @@
         compiler_params=params,
         name="first",
     )(*(pltpu.with_memory_space_constraint(a, pltpu.HBM) for a in inputs), *near)
-    near, queries = in_order(MIDDLE, queries)
-    states = pl.pallas_call(
-        middle_kernel,
-        out_shape=state,
-        in_specs=[VMEM] * (len(near) + 8),
-        out_specs=(VMEM,) * 3,
-        scratch_shapes=pairs_of(len(MIDDLE) * rows),
-        compiler_params=params,
-        name="middle",
-    )(*near, w_key, w_value, queries, bias, times, *states)
+    for kinds in MIDDLE:
+        near, states = in_order(kinds, states)
+        states = pl.pallas_call(
+            functools.partial(middle_kernel, kinds),
+            out_shape=state,
+            in_specs=[VMEM] * (len(near) + 8),
+            out_specs=(VMEM,) * 3,
+            scratch_shapes=pairs_of(len(kinds) * rows),
+            compiler_params=params,
+            name="_".join(kinds),
+        )(*near, w_key, w_value, queries, bias, times, *states)
     near, states = in_order(LAST, states)
     return pl.pallas_call(
         last_kernel,

time: 15.5 us -> 15.2 us (0.981)
  waiting for transfers between devices: 0.93 us -> 0.1 us
  Pallas kernels: 7.08 us -> 7.6 us
    pallas_call x1 -> x2, Pallas kernels: 0.91 us -> 2.72 us  [shards(): pl.pallas_call(functools.partial(middle_kernel, kinds), out_shape=state,...]
    pallas_call x1, Pallas kernels: 3.53 us -> 2.3 us  [shards(): pl.pallas_call(first_kernel, out_shape=(array(rows, width), *[array(width...]
    ppermute x4, waiting for transfers between devices: 0.65 us -> 0.1 us  [exchange(): return lax.ppermute(features, 'dom', [(i, i ^ apart) for i in range(peers)])]
    ppermute x1, waiting for transfers between devices: 0.28 us -> 0.01 us  [shards(): lax.ppermute(features, 'dom', [(i, (i + 1) % peers if i % 2 else (i - 1)...]
  transfers between devices with their start and end apart: 5 -> 5, of which waited for: 4 -> 1; matrix products, arithmetic and copies ran while one was open for 0% -> 0% of each run, Pallas kernels for 29% -> 34%
where the time goes in v8:
time: 15.2 us; the launch traced here: 15 us
  Pallas kernels  7.6 us (50%)
  starting transfers between devices  7.28 us (48%)
    ppermute x1, starting transfers between devices, shards(): lax.ppermute(features, 'dom', [(i, (i + 1) % peers if i % 2 else (i - 1)...  4.3 us
    ppermute x4, starting transfers between devices, exchange(): return lax.ppermute(features, 'dom', [(i, i ^ apart) for i in range(peers)])  2.97 us
    pallas_call x2, Pallas kernels, shards(): pl.pallas_call(functools.partial(middle_kernel, kinds), out_shape=state,...  2.72 us
    pallas_call x1, Pallas kernels, shards(): pl.pallas_call(last_kernel, out_shape=array(rows, width, dtype=features.d...  2.58 us
    pallas_call x1, Pallas kernels, shards(): pl.pallas_call(first_kernel, out_shape=(array(rows, width), *[array(width...  2.3 us
  transfers between devices with their start and end apart: 5, of which 1 were waited for; matrix products, arithmetic and copies ran while one was open for 0% of the time, Pallas kernels for 34%

profile of v8, /device:TPU:0, one launch (start us, length us, event | category | flops | bytes accessed | tf_op | source)
XLA Modules:
  0.0 15.0 jit_solution(10431714156515916002)
XLA Ops:
  0.0 0.5 %collective-permute-start.2 = (bf16[256,256]{1,0:T(8,128)(2,1)}, bf16[256,256]{1,0:T(8,128)(2,1)S(1)}, u32[]{:S(2)}, u32[]{:S(2)}) collective-permute-start(bf16[256,256]{1,0:T(8,128)(2,1)} %features.1), channel_id=1, source_target_pairs={{0,1},{1,0},{2,3},{3,2},{4,5},{5,4},{6,7},{7,6},{8,9},{9,8},{10,11... | collective-permute-start | bytes 393224 | tf_op jit(solution)/shard_map/ppermute | solution.py:218
  0.5 2.5 %collective-permute-start.3 = (bf16[256,256]{1,0:T(8,128)(2,1)}, bf16[256,256]{1,0:T(8,128)(2,1)S(1)}, u32[]{:S(2)}, u32[]{:S(2)}) collective-permute-start(bf16[256,256]{1,0:T(8,128)(2,1)} %features.1), channel_id=1, source_target_pairs={{0,4},{1,5},{2,6},{3,7},{4,0},{5,1},{6,2},{7,3},{8,12},{9,13},{10,... | collective-permute-start | bytes 393224 | tf_op jit(solution)/shard_map/ppermute | solution.py:218
  3.0 4.3 %collective-permute-start.1 = (bf16[256,256]{1,0:T(8,128)(2,1)}, bf16[256,256]{1,0:T(8,128)(2,1)S(1)}, u32[]{:S(2)}, u32[]{:S(2)}) collective-permute-start(bf16[256,256]{1,0:T(8,128)(2,1)} %features.1), channel_id=1, source_target_pairs={{0,31},{1,2},{2,1},{3,4},{4,3},{5,6},{6,5},{7,8},{8,7},{9,10},{10,... | collective-permute-start | bytes 393224 | tf_op jit(solution)/shard_map/ppermute | solution.py:225
  7.3 0.0 collective-permute-start
  7.3 0.0 collective-permute-start.4
  7.3 2.3 %first.1 = (bf16[256,256]{1,0:T(8,128)(2,1)S(1)}, bf16[256,256]{1,0:T(8,128)(2,1)S(1)}, bf16[256,256]{1,0:T(8,128)(2,1)S(1)}, bf16[256,256]{1,0:T(8,128)(2,1)S(1...) custom-call(bf16[256,256]{1,0:T(8,128)(2,1)} %features.1, ...), custom_call_target="tpu_custom_call" | custom-call | tf_op jit(solution)/shard_map/first/pallas_call | solution.py:242
  9.6 0.0 collective-permute-done.2.refs_0_
  9.6 0.0 collective-permute-done.3.refs_1_
  9.6 1.8 %core_y.1 = (f32[256,256]{1,0:T(8,128)S(1)}, f32[256,256]{1,0:T(8,128)S(1)}, f32[256,256]{1,0:T(8,128)S(1)}) custom-call(bf16[256,256]{1,0:T(8,128)(2,1)S(1)} %collective-permute-done.2.refs_0_, bf16[256,256]{1,0:T(8,128)(2,1)S(1)} %collective-permute-done.3.refs_1_, bf16[256,256]{1,0:T(8,128)(2,1)S(1)} %get-tuple-element.49.refs_2_.refs_1_, ...), custom_call_target="tpu_custom_call" | custom-call | tf_op jit(solution)/shard_map/core_y/pallas_call | solution.py:262
  11.4 0.0 collective-permute-done.1.refs_0_
  11.4 0.9 %ring.1 = (f32[256,256]{1,0:T(8,128)S(1)}, f32[256,256]{1,0:T(8,128)S(1)}, f32[256,256]{1,0:T(8,128)S(1)}) custom-call(bf16[256,256]{1,0:T(8,128)(2,1)S(1)} %collective-permute-done.1.refs_0_, bf16[256,256]{1,0:T(8,128)(2,1)S(1)} %get-tuple-element.49.refs_2_.refs_1_, bf16[256,256]{1,0:T(8,128)(2,1)S(1)} %get-tuple-element.50.refs_3_.refs_2_, ...), custom_call_target="tpu_custom_call" | custom-call | tf_op jit(solution)/shard_map/ring/pallas_call | solution.py:262
  12.4 0.1 collective-permute-done.refs_0_
  12.5 0.0 collective-permute-done.4.refs_1_
  12.5 2.6 %last.1 = bf16[256,256]{1,0:T(8,128)(2,1)} custom-call(bf16[256,256]{1,0:T(8,128)(2,1)S(1)} %collective-permute-done.refs_0_, bf16[256,256]{1,0:T(8,128)(2,1)S(1)} %collective-permute-done.4.refs_1_, bf16[256,256]{1,0:T(8,128)(2,1)S(1)} %get-tuple-element.49.refs_2_.refs_1_, bf16[256,256]{1,0:T(8,128)(2,1)S(1)} %get-tuple-element.50.refs_3_.refs_2_, ...), custom_call_target="tpu_custom_call" | custom-call | tf_op jit(solution)/shard_map/last/pallas_call | solution.py:272
Async XLA Ops:
  0.0 9.6 %collective-permute-start.2 = (bf16[256,256]{1,0:T(8,128)(2,1)}, bf16[256,256]{1,0:T(8,128)(2,1)S(1)}, u32[]{:S(2)}, u32[]{:S(2)}) collective-permute-start(bf16[256,256]{1,0:T(8,128)(2,1)} %features.1), channel_id=1, source_target_pairs={{0,1},{1,0},{2,3},{3,2},{4,5},{5,4},{6,7},{7,6},{8,9},{9,8},{10,11... | collective-permute-start | bytes 393224 | tf_op jit(solution)/shard_map/ppermute | solution.py:218
  0.5 9.2 %collective-permute-start.3 = (bf16[256,256]{1,0:T(8,128)(2,1)}, bf16[256,256]{1,0:T(8,128)(2,1)S(1)}, u32[]{:S(2)}, u32[]{:S(2)}) collective-permute-start(bf16[256,256]{1,0:T(8,128)(2,1)} %features.1), channel_id=1, source_target_pairs={{0,4},{1,5},{2,6},{3,7},{4,0},{5,1},{6,2},{7,3},{8,12},{9,13},{10,... | collective-permute-start | bytes 393224 | tf_op jit(solution)/shard_map/ppermute | solution.py:218
  3.0 8.5 %collective-permute-start.1 = (bf16[256,256]{1,0:T(8,128)(2,1)}, bf16[256,256]{1,0:T(8,128)(2,1)S(1)}, u32[]{:S(2)}, u32[]{:S(2)}) collective-permute-start(bf16[256,256]{1,0:T(8,128)(2,1)} %features.1), channel_id=1, source_target_pairs={{0,31},{1,2},{2,1},{3,4},{4,3},{5,6},{6,5},{7,8},{8,7},{9,10},{10,... | collective-permute-start | bytes 393224 | tf_op jit(solution)/shard_map/ppermute | solution.py:225
  7.3 5.2 %collective-permute-start = (bf16[256,256]{1,0:T(8,128)(2,1)}, bf16[256,256]{1,0:T(8,128)(2,1)S(1)}, u32[]{:S(2)}, u32[]{:S(2)}) collective-permute-start(bf16[256,256]{1,0:T(8,128)(2,1)} %features.1), channel_id=1, source_target_pairs={{0,2},{1,3},{2,0},{3,1},{4,6},{5,7},{6,4},{7,5},{8,10},{9,11},{10,... | collective-permute-start | bytes 393224 | tf_op jit(solution)/shard_map/ppermute | solution.py:218
  7.3 5.2 %collective-permute-start.4 = (bf16[256,256]{1,0:T(8,128)(2,1)}, bf16[256,256]{1,0:T(8,128)(2,1)S(1)}, u32[]{:S(2)}, u32[]{:S(2)}) collective-permute-start(bf16[256,256]{1,0:T(8,128)(2,1)} %features.1), channel_id=1, source_target_pairs={{0,8},{1,9},{2,10},{3,11},{4,12},{5,13},{6,14},{7,15},{8,0},{9,1},... | collective-permute-start | bytes 393224 | tf_op jit(solution)/shard_map/ppermute | solution.py:218

commit v9 on v8

--- a/solution.py
+++ b/solution.py
@@ -11,9 +11,9 @@
 EPSILON = 1e-06
 LOW = -1e30
 
-FIRST = ('own',)
-MIDDLE = (('core', 'y'), ('ring',))
-LAST = ('x', 'z')
+FIRST = ("own", "core")
+MIDDLE = (("ring", "y"),)
+LAST = ("z", "x")
 BIAS_ROW = {"own": 0, "core": 1, "x": 2, "y": 3, "z": 4, "ring": 5}
 
 VMEM = pl.BlockSpec(memory_space=pltpu.VMEM)
@@ -96,18 +96,24 @@
     values[rows, :] = matmul(features, w_value[...]).astype(values.dtype)
 
 
-def parts_of(kinds, refs, w_key, w_value, bias, times, keys, values):
+def parts_of(kinds, refs, w_key, w_value, bias, times, keys, values, swapped=()):
     rows = refs[0].shape[0]
     groups = times.shape[0]
     block_rows = rows // groups
     parts = []
     start = 0
+    me = lax.axis_index("dom")
+    is_swapped = functools.reduce(lambda one, device: one | (me == device), swapped, me < 0)
+    named = dict(zip(kinds, refs))
     for kind, ref in zip(kinds, refs):
         count = block_rows if kind == "ring" else rows
         if kind == "ring":
-            is_odd = lax.rem(lax.axis_index("dom"), 2) == 1
+            is_odd = lax.rem(me, 2) == 1
             first = pl.multiple_of(jnp.where(is_odd, 0, rows - block_rows), block_rows)
-            arrival = ref[pl.ds(first, block_rows), :]
+            where = pl.ds(first, block_rows)
+            arrival = jnp.where(is_swapped, named["y"][where, :], ref[where, :])
+        elif kind == "y":
+            arrival = jnp.where(is_swapped, named["ring"][...], ref[...])
         else:
             arrival = ref[...]
         project(arrival, w_key, w_value, keys, values, start)
@@ -168,10 +174,10 @@
     copies[8].wait()
 
 
-def middle_kernel(kinds, *refs):
+def middle_kernel(kinds, swapped, *refs):
     arrivals, refs = refs[: len(kinds)], refs[len(kinds) :]
     w_key, w_value, queries, bias, times, tops, outs, sums, new_tops, new_outs, new_sums, keys, values = refs
-    parts = parts_of(kinds, arrivals, w_key, w_value, bias, times, keys, values)
+    parts = parts_of(kinds, arrivals, w_key, w_value, bias, times, keys, values, swapped)
     state = attend(queries[...], parts, times.shape[0])
     new_tops[...], new_outs[...], new_sums[...] = merge((tops[...], outs[...], sums[...]), state)
 
@@ -217,15 +223,23 @@
         apart = 1 << (matching * levels // match_total)
         return lax.ppermute(features, "dom", [(i, i ^ apart) for i in range(peers)])
 
+    ring_of = [(i + 1) % peers if i % 2 else (i - 1) % peers for i in range(peers)]
+    far_of = [i ^ (1 << (2 * levels // match_total)) for i in range(peers)]
+    swapped = []
+    device, end = 0, ring_of[0]
+    while end not in swapped:
+        ring_of[device], far_of[device] = far_of[device], ring_of[device]
+        target = ring_of[device]
+        swapped.append(target)
+        device = next((i for i in range(peers) if ring_of[i] == target and i != device), None)
     arrived = {
         "core": exchange(0),
         "x": exchange(1),
-        "y": exchange(2),
+        "y": lax.ppermute(features, "dom", list(enumerate(far_of))),
         "z": exchange(3),
-        "ring": lax.ppermute(
-            features, "dom", [(i, (i + 1) % peers if i % 2 else (i - 1) % peers) for i in range(peers)]
-        ),
+        "ring": lax.ppermute(features, "dom", list(enumerate(ring_of))),
     }
+    swapped = tuple(swapped)
 
     def in_order(kinds, after):
         gathered = []
@@ -260,7 +274,7 @@
     for kinds in MIDDLE:
         near, states = in_order(kinds, states)
         states = pl.pallas_call(
-            functools.partial(middle_kernel, kinds),
+            functools.partial(middle_kernel, kinds, swapped),
             out_shape=state,
             in_specs=[VMEM] * (len(near) + 8),
             out_specs=(VMEM,) * 3,

time: 15.2 us -> 15 us (0.987)
  waiting for transfers between devices: 0.1 us -> 0.57 us
  Pallas kernels: 7.6 us -> 7.16 us
  starting transfers between devices: 7.28 us -> 7.05 us
    ppermute x4 -> x3, starting transfers between devices: 2.97 us -> 0.46 us  [exchange(): return lax.ppermute(features, 'dom', [(i, i ^ apart) for i in range(peers)])]
    ppermute x1 -> x2, starting transfers between devices: 4.3 us -> 6.6 us  [the longest x1 4.08 us: shards(): lax.ppermute(features, 'dom', list(enumerate(far_of)))]
    pallas_call x2 -> x1, Pallas kernels: 2.72 us -> 1.61 us  [shards(): pl.pallas_call(functools.partial(middle_kernel, kinds, swapped), out_shap...]
    pallas_call x1, Pallas kernels: 2.3 us -> 2.97 us  [shards(): pl.pallas_call(first_kernel, out_shape=(array(rows, width), *[array(width...]
    ppermute x4 -> x3, waiting for transfers between devices: 0.1 us -> 0.53 us  [exchange(): return lax.ppermute(features, 'dom', [(i, i ^ apart) for i in range(peers)])]
  transfers between devices with their start and end apart: 5 -> 5, of which waited for: 1 -> 1; matrix products, arithmetic and copies ran while one was open for 0% -> 0% of each run, Pallas kernels for 34% -> 31%
where the time goes in v9:
time: 15 us; the launch traced here: 14.8 us
  Pallas kernels  7.16 us (48%)
  starting transfers between devices  7.05 us (47%)
  waiting for transfers between devices  0.57 us (4%)
    ppermute x1, starting transfers between devices, shards(): lax.ppermute(features, 'dom', list(enumerate(far_of)))  4.08 us
    pallas_call x1, Pallas kernels, shards(): pl.pallas_call(first_kernel, out_shape=(array(rows, width), *[array(width...  2.97 us
    pallas_call x1, Pallas kernels, shards(): pl.pallas_call(last_kernel, out_shape=array(rows, width, dtype=features.d...  2.58 us
    ppermute x1, starting transfers between devices, shards(): lax.ppermute(features, 'dom', list(enumerate(ring_of)))  2.52 us
    pallas_call x1, Pallas kernels, shards(): pl.pallas_call(functools.partial(middle_kernel, kinds, swapped), out_shap...  1.61 us
    ppermute x3, waiting for transfers between devices, exchange(): return lax.ppermute(features, 'dom', [(i, i ^ apart) for i in range(peers)])  0.53 us
    ppermute x3, starting transfers between devices, exchange(): return lax.ppermute(features, 'dom', [(i, i ^ apart) for i in range(peers)])  0.46 us
  transfers between devices with their start and end apart: 5, of which 1 were waited for; matrix products, arithmetic and copies ran while one was open for 0% of the time, Pallas kernels for 31%

profile of v9, /device:TPU:0, one launch (start us, length us, event | category | flops | bytes accessed | tf_op | source)
XLA Modules:
  0.0 14.8 jit_solution(2263697750791484050)
XLA Ops:
  0.0 0.5 %collective-permute-start.2 = (bf16[256,256]{1,0:T(8,128)(2,1)}, bf16[256,256]{1,0:T(8,128)(2,1)S(1)}, u32[]{:S(2)}, u32[]{:S(2)}) collective-permute-start(bf16[256,256]{1,0:T(8,128)(2,1)} %features.1), channel_id=1, source_target_pairs={{0,1},{1,0},{2,3},{3,2},{4,5},{5,4},{6,7},{7,6},{8,9},{9,8},{10,11... | collective-permute-start | bytes 393224 | tf_op jit(solution)/shard_map/ppermute | solution.py:224
  0.5 2.5 %collective-permute-start.1 = (bf16[256,256]{1,0:T(8,128)(2,1)}, bf16[256,256]{1,0:T(8,128)(2,1)S(1)}, u32[]{:S(2)}, u32[]{:S(2)}) collective-permute-start(bf16[256,256]{1,0:T(8,128)(2,1)} %features.1), channel_id=1, source_target_pairs={{0,4},{1,2},{2,1},{3,7},{4,3},{5,6},{6,5},{7,8},{8,12},{9,10},{10,... | collective-permute-start | bytes 393224 | tf_op jit(solution)/shard_map/ppermute | solution.py:240
  3.0 4.1 %collective-permute-start.3 = (bf16[256,256]{1,0:T(8,128)(2,1)}, bf16[256,256]{1,0:T(8,128)(2,1)S(1)}, u32[]{:S(2)}, u32[]{:S(2)}) collective-permute-start(bf16[256,256]{1,0:T(8,128)(2,1)} %features.1), channel_id=1, source_target_pairs={{0,31},{1,5},{2,6},{3,4},{4,0},{5,1},{6,2},{7,3},{8,7},{9,13},{10,... | collective-permute-start | bytes 393224 | tf_op jit(solution)/shard_map/ppermute | solution.py:238
  7.1 0.0 collective-permute-start
  7.1 0.0 collective-permute-start.4
  7.1 0.0 collective-permute-done.2.refs_0_
  7.1 3.0 %first.1 = (bf16[256,256]{1,0:T(8,128)(2,1)S(1)}, bf16[256,256]{1,0:T(8,128)(2,1)S(1)}, bf16[256,256]{1,0:T(8,128)(2,1)S(1)}, bf16[256,256]{1,0:T(8,128)(2,1)S(1...) custom-call(bf16[256,256]{1,0:T(8,128)(2,1)} %features.1, ...), custom_call_target="tpu_custom_call" | custom-call | tf_op jit(solution)/shard_map/first/pallas_call | solution.py:256
  10.0 0.0 collective-permute-done.1.refs_0_
  10.1 0.0 collective-permute-done.3.refs_1_
  10.1 1.6 %ring_y.1 = (f32[256,256]{1,0:T(8,128)S(1)}, f32[256,256]{1,0:T(8,128)S(1)}, f32[256,256]{1,0:T(8,128)S(1)}) custom-call(bf16[256,256]{1,0:T(8,128)(2,1)S(1)} %collective-permute-done.1.refs_0_, bf16[256,256]{1,0:T(8,128)(2,1)S(1)} %collective-permute-done.3.refs_1_, bf16[256,256]{1,0:T(8,128)(2,1)S(1)} %get-tuple-element.44.refs_2_, ...), custom_call_target="tpu_custom_call" | custom-call | tf_op jit(solution)/shard_map/ring_y/pallas_call | solution.py:276
  11.7 0.5 %collective-permute-done.refs_0_ = bf16[256,256]{1,0:T(8,128)(2,1)S(1)} collective-permute-done((bf16[256,256]{1,0:T(8,128)(2,1)}, bf16[256,256]{1,0:T(8,128)(2,1)S(1)}, u32[]{:S(2)}, u32[]{:S(2)}) %collective-permute-start) | collective-permute-done | bytes 131104 | tf_op jit(solution)/shard_map/ppermute | solution.py:224
  12.2 0.0 collective-permute-done.4.refs_1_
  12.2 2.6 %last.1 = bf16[256,256]{1,0:T(8,128)(2,1)} custom-call(bf16[256,256]{1,0:T(8,128)(2,1)S(1)} %collective-permute-done.refs_0_, bf16[256,256]{1,0:T(8,128)(2,1)S(1)} %collective-permute-done.4.refs_1_, bf16[256,256]{1,0:T(8,128)(2,1)S(1)} %get-tuple-element.44.refs_2_, bf16[256,256]{1,0:T(8,128)(2,1)S(1)} %get-tuple-element.45.refs_3_, ...), custom_call_target="tpu_custom_call" | custom-call | tf_op jit(solution)/shard_map/last/pallas_call | solution.py:286
Async XLA Ops:
  0.0 7.1 %collective-permute-start.2 = (bf16[256,256]{1,0:T(8,128)(2,1)}, bf16[256,256]{1,0:T(8,128)(2,1)S(1)}, u32[]{:S(2)}, u32[]{:S(2)}) collective-permute-start(bf16[256,256]{1,0:T(8,128)(2,1)} %features.1), channel_id=1, source_target_pairs={{0,1},{1,0},{2,3},{3,2},{4,5},{5,4},{6,7},{7,6},{8,9},{9,8},{10,11... | collective-permute-start | bytes 393224 | tf_op jit(solution)/shard_map/ppermute | solution.py:224
  0.5 9.6 %collective-permute-start.1 = (bf16[256,256]{1,0:T(8,128)(2,1)}, bf16[256,256]{1,0:T(8,128)(2,1)S(1)}, u32[]{:S(2)}, u32[]{:S(2)}) collective-permute-start(bf16[256,256]{1,0:T(8,128)(2,1)} %features.1), channel_id=1, source_target_pairs={{0,4},{1,2},{2,1},{3,7},{4,3},{5,6},{6,5},{7,8},{8,12},{9,10},{10,... | collective-permute-start | bytes 393224 | tf_op jit(solution)/shard_map/ppermute | solution.py:240
  3.0 7.1 %collective-permute-start.3 = (bf16[256,256]{1,0:T(8,128)(2,1)}, bf16[256,256]{1,0:T(8,128)(2,1)S(1)}, u32[]{:S(2)}, u32[]{:S(2)}) collective-permute-start(bf16[256,256]{1,0:T(8,128)(2,1)} %features.1), channel_id=1, source_target_pairs={{0,31},{1,5},{2,6},{3,4},{4,0},{5,1},{6,2},{7,3},{8,7},{9,13},{10,... | collective-permute-start | bytes 393224 | tf_op jit(solution)/shard_map/ppermute | solution.py:238
  7.1 5.2 %collective-permute-start = (bf16[256,256]{1,0:T(8,128)(2,1)}, bf16[256,256]{1,0:T(8,128)(2,1)S(1)}, u32[]{:S(2)}, u32[]{:S(2)}) collective-permute-start(bf16[256,256]{1,0:T(8,128)(2,1)} %features.1), channel_id=1, source_target_pairs={{0,8},{1,9},{2,10},{3,11},{4,12},{5,13},{6,14},{7,15},{8,0},{9,1},... | collective-permute-start | bytes 393224 | tf_op jit(solution)/shard_map/ppermute | solution.py:224
  7.1 5.2 %collective-permute-start.4 = (bf16[256,256]{1,0:T(8,128)(2,1)}, bf16[256,256]{1,0:T(8,128)(2,1)S(1)}, u32[]{:S(2)}, u32[]{:S(2)}) collective-permute-start(bf16[256,256]{1,0:T(8,128)(2,1)} %features.1), channel_id=1, source_target_pairs={{0,2},{1,3},{2,0},{3,1},{4,6},{5,7},{6,4},{7,5},{8,10},{9,11},{10,... | collective-permute-start | bytes 393224 | tf_op jit(solution)/shard_map/ppermute | solution.py:224

commit v10 on v9

--- a/solution.py
+++ b/solution.py
@@ -15,6 +15,7 @@
 MIDDLE = (("ring", "y"),)
 LAST = ("z", "x")
 BIAS_ROW = {"own": 0, "core": 1, "x": 2, "y": 3, "z": 4, "ring": 5}
+TIMES_ROW = {"core": 0, "x": 1}
 
 VMEM = pl.BlockSpec(memory_space=pltpu.VMEM)
 ANY = pl.BlockSpec(memory_space=pl.ANY)
@@ -98,7 +99,7 @@
 
 def parts_of(kinds, refs, w_key, w_value, bias, times, keys, values, swapped=()):
     rows = refs[0].shape[0]
-    groups = times.shape[0]
+    groups = times.shape[1]
     block_rows = rows // groups
     parts = []
     start = 0
@@ -118,15 +119,23 @@
             arrival = ref[...]
         project(arrival, w_key, w_value, keys, values, start)
         where = pl.ds(start, count)
-        row = BIAS_ROW[kind]
+        row, repeats = BIAS_ROW[kind], TIMES_ROW.get(kind)
         parts.append((
             lambda where=where: keys[where, :],
             lambda where=where: values[where, :],
             lambda row=row, count=count: bias[row, :, :count],
-            (lambda: times[...]) if kind == "core" else None,
+            None if repeats is None else lambda repeats=repeats: times[repeats],
         ))
         start += count
     return parts
+
+
+def matching_apart(peers, matching, match_total):
+    return 1 << (matching * (peers.bit_length() - 1) // match_total)
+
+
+def moved_targets(peers, match_total):
+    return (peers - 2, (peers - 1) ^ matching_apart(peers, 1, match_total))
 
 
 def first_kernel(
@@ -149,7 +158,9 @@
     rows, width = x.shape
     block_rows = rows // groups
     size = width // HEADS
-    is_odd = lax.rem(lax.axis_index("dom"), 2) == 1
+    me, peers = lax.axis_index("dom"), lax.axis_size("dom")
+    is_odd = lax.rem(me, 2) == 1
+    is_moved = functools.reduce(lambda one, device: one | (me == device), moved_targets(peers, matchings), me < 0)
     for copy in copies[4:8]:
         copy.wait()
     for g in range(groups):
@@ -162,9 +173,14 @@
         takes[1][0] = takes[1][0] + jnp.where(is_odd, 0, near[-1])
         takes[1][-1] = takes[1][-1] + jnp.where(is_odd, near[0], 0)
         takes.append([jnp.where(is_odd, near[-1], near[0])] * groups)
+        takes[1:3] = (
+            [jnp.where(is_moved, other, one) for one, other in zip(*pair)]
+            for pair in ((takes[1], takes[2]), (takes[2], takes[1]))
+        )
         for p, take in enumerate(takes):
             bias[p, g : g + 1, :] = along_keys([jnp.where(t > 0, 0.0, LOW) for t in take], block_rows)
-        times[g : g + 1, :] = along_keys([t.astype(jnp.float32) for t in takes[1]], block_rows)
+        for i in range(2):
+            times[i, g : g + 1, :] = along_keys([t.astype(jnp.float32) for t in takes[1 + i]], block_rows)
     for copy in copies[:4]:
         copy.wait()
     q = (matmul(x[...], query_copy[...]) * (float(size) ** -0.5)).astype(jnp.bfloat16)
@@ -178,7 +194,7 @@
     arrivals, refs = refs[: len(kinds)], refs[len(kinds) :]
     w_key, w_value, queries, bias, times, tops, outs, sums, new_tops, new_outs, new_sums, keys, values = refs
     parts = parts_of(kinds, arrivals, w_key, w_value, bias, times, keys, values, swapped)
-    state = attend(queries[...], parts, times.shape[0])
+    state = attend(queries[...], parts, times.shape[1])
     new_tops[...], new_outs[...], new_sums[...] = merge((tops[...], outs[...], sums[...]), state)
 
 
@@ -186,7 +202,7 @@
     arrivals, refs = refs[: len(LAST)], refs[len(LAST) :]
     w_key, w_value, queries, bias, times, tops, outs, sums, features, w_out, result, keys, values = refs
     parts = parts_of(LAST, arrivals, w_key, w_value, bias, times, keys, values)
-    state = attend(queries[...], parts, times.shape[0])
+    state = attend(queries[...], parts, times.shape[1])
     _, out, total = merge((tops[...], outs[...], sums[...]), state)
     context = (out / total).astype(jnp.bfloat16)
     mixed = matmul(context, w_out[...])
@@ -209,7 +225,6 @@
     groups = local_blocks.shape[0]
     block_rows = rows // groups
     peers = lax.axis_size("dom")
-    levels = peers.bit_length() - 1
     match_total = expander_blocks.shape[0]
     params = pltpu.CompilerParams(vmem_limit_bytes=48 * 2**20)
 
@@ -220,11 +235,11 @@
         return [pltpu.VMEM((total, width), jnp.bfloat16)] * 2
 
     def exchange(matching):
-        apart = 1 << (matching * levels // match_total)
+        apart = matching_apart(peers, matching, match_total)
         return lax.ppermute(features, "dom", [(i, i ^ apart) for i in range(peers)])
 
     ring_of = [(i + 1) % peers if i % 2 else (i - 1) % peers for i in range(peers)]
-    far_of = [i ^ (1 << (2 * levels // match_total)) for i in range(peers)]
+    far_of = [i ^ matching_apart(peers, 2, match_total) for i in range(peers)]
     swapped = []
     device, end = 0, ring_of[0]
     while end not in swapped:
@@ -232,9 +247,13 @@
         target = ring_of[device]
         swapped.append(target)
         device = next((i for i in range(peers) if ring_of[i] == target and i != device), None)
+    near = matching_apart(peers, 1, match_total)
+    core_of, near_of = [i ^ 1 for i in range(peers)], [i ^ near for i in range(peers)]
+    for device in (peers - 1, (peers - 1) ^ near ^ 1):
+        core_of[device], near_of[device] = near_of[device], core_of[device]
     arrived = {
-        "core": exchange(0),
-        "x": exchange(1),
+        "core": lax.ppermute(features, "dom", list(enumerate(core_of))),
+        "x": lax.ppermute(features, "dom", list(enumerate(near_of))),
         "y": lax.ppermute(features, "dom", list(enumerate(far_of))),
         "z": exchange(3),
         "ring": lax.ppermute(features, "dom", list(enumerate(ring_of))),
@@ -257,7 +276,7 @@
         first_kernel,
         out_shape=(
             array(rows, width), *[array(width, width)] * 3, array(rows, width),
-            array(match_total + 2, groups, rows, dtype=jnp.float32), array(groups, rows, dtype=jnp.float32),
+            array(match_total + 2, groups, rows, dtype=jnp.float32), array(2, groups, rows, dtype=jnp.float32),
             *state,
         ),
         in_specs=[ANY] * len(inputs) + [VMEM] * len(near),

time: 15 us -> 14.6 us (0.973)
  starting transfers between devices: 7.05 us -> 6.68 us
    ppermute x0 -> x2, starting transfers between devices: none -> 0.5 us  [the longest x1 0.45 us: shards(): lax.ppermute(features, 'dom', list(enumerate(core_of)))]
    ppermute x3 -> x1, starting transfers between devices: 0.46 us -> 0.01 us  [exchange(): return lax.ppermute(features, 'dom', [(i, i ^ apart) for i in range(peers)])]
    ppermute x3 -> x1, waiting for transfers between devices: 0.53 us -> 0.11 us  [exchange(): return lax.ppermute(features, 'dom', [(i, i ^ apart) for i in range(peers)])]
    ppermute x1, starting transfers between devices: 4.08 us -> 3.66 us  [shards(): lax.ppermute(features, 'dom', list(enumerate(far_of)))]
    ppermute x1, waiting for transfers between devices: 0.01 us -> 0.3 us  [shards(): lax.ppermute(features, 'dom', list(enumerate(far_of)))]
  transfers between devices with their start and end apart: 5 -> 5, of which waited for: 1 -> 3; matrix products, arithmetic and copies ran while one was open for 0% -> 0% of each run, Pallas kernels for 31% -> 32%
where the time goes in v10:
time: 14.6 us; the launch traced here: 14.4 us
  Pallas kernels  7.2 us (49%)
  starting transfers between devices  6.68 us (46%)
  waiting for transfers between devices  0.53 us (4%)
    ppermute x1, starting transfers between devices, shards(): lax.ppermute(features, 'dom', list(enumerate(far_of)))  3.66 us
    pallas_call x1, Pallas kernels, shards(): pl.pallas_call(first_kernel, out_shape=(array(rows, width), *[array(width...  2.96 us
    pallas_call x1, Pallas kernels, shards(): pl.pallas_call(last_kernel, out_shape=array(rows, width, dtype=features.d...  2.62 us
    ppermute x1, starting transfers between devices, shards(): lax.ppermute(features, 'dom', list(enumerate(ring_of)))  2.52 us
    pallas_call x1, Pallas kernels, shards(): pl.pallas_call(functools.partial(middle_kernel, kinds, swapped), out_shap...  1.62 us
    ppermute x1, starting transfers between devices, shards(): lax.ppermute(features, 'dom', list(enumerate(core_of)))  0.45 us
    ppermute x1, waiting for transfers between devices, shards(): lax.ppermute(features, 'dom', list(enumerate(far_of)))  0.3 us
  transfers between devices with their start and end apart: 5, of which 3 were waited for; matrix products, arithmetic and copies ran while one was open for 0% of the time, Pallas kernels for 32%

profile of v10, /device:TPU:0, one launch (start us, length us, event | category | flops | bytes accessed | tf_op | source)
XLA Modules:
  0.0 14.4 jit_solution(8795982724108410733)
XLA Ops:
  0.0 0.5 %collective-permute-start.2 = (bf16[256,256]{1,0:T(8,128)(2,1)}, bf16[256,256]{1,0:T(8,128)(2,1)S(1)}, u32[]{:S(2)}, u32[]{:S(2)}) collective-permute-start(bf16[256,256]{1,0:T(8,128)(2,1)} %features.1), channel_id=1, source_target_pairs={{0,1},{1,0},{2,3},{3,2},{4,5},{5,4},{6,7},{7,6},{8,9},{9,8},{10,11... | collective-permute-start | bytes 393224 | tf_op jit(solution)/shard_map/ppermute | solution.py:255
  0.5 2.5 %collective-permute-start.1 = (bf16[256,256]{1,0:T(8,128)(2,1)}, bf16[256,256]{1,0:T(8,128)(2,1)S(1)}, u32[]{:S(2)}, u32[]{:S(2)}) collective-permute-start(bf16[256,256]{1,0:T(8,128)(2,1)} %features.1), channel_id=1, source_target_pairs={{0,4},{1,2},{2,1},{3,7},{4,3},{5,6},{6,5},{7,8},{8,12},{9,10},{10,... | collective-permute-start | bytes 393224 | tf_op jit(solution)/shard_map/ppermute | solution.py:259
  3.0 3.7 %collective-permute-start.3 = (bf16[256,256]{1,0:T(8,128)(2,1)}, bf16[256,256]{1,0:T(8,128)(2,1)S(1)}, u32[]{:S(2)}, u32[]{:S(2)}) collective-permute-start(bf16[256,256]{1,0:T(8,128)(2,1)} %features.1), channel_id=1, source_target_pairs={{0,31},{1,5},{2,6},{3,4},{4,0},{5,1},{6,2},{7,3},{8,7},{9,13},{10,... | collective-permute-start | bytes 393224 | tf_op jit(solution)/shard_map/ppermute | solution.py:257
  6.6 0.0 collective-permute-start
  6.6 0.1 collective-permute-start.4
  6.7 0.0 collective-permute-done.2.refs_0_
  6.7 3.0 %first.1 = (bf16[256,256]{1,0:T(8,128)(2,1)S(1)}, bf16[256,256]{1,0:T(8,128)(2,1)S(1)}, bf16[256,256]{1,0:T(8,128)(2,1)S(1)}, bf16[256,256]{1,0:T(8,128)(2,1)S(1...) custom-call(bf16[256,256]{1,0:T(8,128)(2,1)} %features.1, ...), custom_call_target="tpu_custom_call" | custom-call | tf_op jit(solution)/shard_map/first/pallas_call | solution.py:275
  9.7 0.1 collective-permute-done.1.refs_0_
  9.8 0.3 %collective-permute-done.3.refs_1_ = bf16[256,256]{1,0:T(8,128)(2,1)S(1)} collective-permute-done((bf16[256,256]{1,0:T(8,128)(2,1)}, bf16[256,256]{1,0:T(8,128)(2,1)S(1)}, u32[]{:S(2)}, u32[]{:S(2)}) %collective-permute-start.3) | collective-permute-done | bytes 131104 | tf_op jit(solution)/shard_map/ppermute | solution.py:257
  10.1 1.6 %ring_y.1 = (f32[256,256]{1,0:T(8,128)S(1)}, f32[256,256]{1,0:T(8,128)S(1)}, f32[256,256]{1,0:T(8,128)S(1)}) custom-call(bf16[256,256]{1,0:T(8,128)(2,1)S(1)} %collective-permute-done.1.refs_0_, bf16[256,256]{1,0:T(8,128)(2,1)S(1)} %collective-permute-done.3.refs_1_, bf16[256,256]{1,0:T(8,128)(2,1)S(1)} %get-tuple-element.44.refs_2_, ...), custom_call_target="tpu_custom_call" | custom-call | tf_op jit(solution)/shard_map/ring_y/pallas_call | solution.py:295
  11.7 0.1 collective-permute-done.refs_0_
  11.8 0.0 collective-permute-done.4.refs_1_
  11.8 2.6 %last.1 = bf16[256,256]{1,0:T(8,128)(2,1)} custom-call(bf16[256,256]{1,0:T(8,128)(2,1)S(1)} %collective-permute-done.refs_0_, bf16[256,256]{1,0:T(8,128)(2,1)S(1)} %collective-permute-done.4.refs_1_, bf16[256,256]{1,0:T(8,128)(2,1)S(1)} %get-tuple-element.44.refs_2_, bf16[256,256]{1,0:T(8,128)(2,1)S(1)} %get-tuple-element.45.refs_3_, ...), custom_call_target="tpu_custom_call" | custom-call | tf_op jit(solution)/shard_map/last/pallas_call | solution.py:305
Async XLA Ops:
  0.0 6.7 %collective-permute-start.2 = (bf16[256,256]{1,0:T(8,128)(2,1)}, bf16[256,256]{1,0:T(8,128)(2,1)S(1)}, u32[]{:S(2)}, u32[]{:S(2)}) collective-permute-start(bf16[256,256]{1,0:T(8,128)(2,1)} %features.1), channel_id=1, source_target_pairs={{0,1},{1,0},{2,3},{3,2},{4,5},{5,4},{6,7},{7,6},{8,9},{9,8},{10,11... | collective-permute-start | bytes 393224 | tf_op jit(solution)/shard_map/ppermute | solution.py:255
  0.5 9.3 %collective-permute-start.1 = (bf16[256,256]{1,0:T(8,128)(2,1)}, bf16[256,256]{1,0:T(8,128)(2,1)S(1)}, u32[]{:S(2)}, u32[]{:S(2)}) collective-permute-start(bf16[256,256]{1,0:T(8,128)(2,1)} %features.1), channel_id=1, source_target_pairs={{0,4},{1,2},{2,1},{3,7},{4,3},{5,6},{6,5},{7,8},{8,12},{9,10},{10,... | collective-permute-start | bytes 393224 | tf_op jit(solution)/shard_map/ppermute | solution.py:259
  3.0 7.1 %collective-permute-start.3 = (bf16[256,256]{1,0:T(8,128)(2,1)}, bf16[256,256]{1,0:T(8,128)(2,1)S(1)}, u32[]{:S(2)}, u32[]{:S(2)}) collective-permute-start(bf16[256,256]{1,0:T(8,128)(2,1)} %features.1), channel_id=1, source_target_pairs={{0,31},{1,5},{2,6},{3,4},{4,0},{5,1},{6,2},{7,3},{8,7},{9,13},{10,... | collective-permute-start | bytes 393224 | tf_op jit(solution)/shard_map/ppermute | solution.py:257
  6.6 5.2 %collective-permute-start = (bf16[256,256]{1,0:T(8,128)(2,1)}, bf16[256,256]{1,0:T(8,128)(2,1)S(1)}, u32[]{:S(2)}, u32[]{:S(2)}) collective-permute-start(bf16[256,256]{1,0:T(8,128)(2,1)} %features.1), channel_id=1, source_target_pairs={{0,8},{1,9},{2,10},{3,11},{4,12},{5,13},{6,14},{7,15},{8,0},{9,1},... | collective-permute-start | bytes 393224 | tf_op jit(solution)/shard_map/ppermute | solution.py:239
  6.6 5.2 %collective-permute-start.4 = (bf16[256,256]{1,0:T(8,128)(2,1)}, bf16[256,256]{1,0:T(8,128)(2,1)S(1)}, u32[]{:S(2)}, u32[]{:S(2)}) collective-permute-start(bf16[256,256]{1,0:T(8,128)(2,1)} %features.1), channel_id=1, source_target_pairs={{0,2},{1,3},{2,0},{3,1},{4,6},{5,7},{6,4},{7,5},{8,10},{9,11},{10,... | collective-permute-start | bytes 393224 | tf_op jit(solution)/shard_map/ppermute | solution.py:256

commit v11 on v10

--- a/solution.py
+++ b/solution.py
@@ -50,19 +50,24 @@
         return array.reshape(count, groups, rows // groups, array.shape[-1])
 
     cuts = [slice(0, lanes), slice(lanes, width)]
+    row_group = lax.broadcasted_iota(jnp.int32, (rows, lanes), 0) // (rows // groups)
+    chooses = (row_group == lax.broadcasted_iota(jnp.int32, (rows, lanes), 1)).astype(queries.dtype)
     masked = [
-        jnp.concatenate([jnp.where(heads == h, queries[:, cut], zero) for h in range(count)], axis=0) for cut in cuts
+        jnp.concatenate(
+            [jnp.concatenate([jnp.where(heads == h, queries[:, cut], zero), chooses], axis=1) for h in range(count)],
+            axis=0,
+        )
+        for cut in cuts
     ]
     scores, tops, sums = [[], []], [None, None], [None, None]
-    for f, cut in enumerate(cuts):
-        for keys, _, bias, _ in parts:
-            part = by_group(matmul_nt(masked[f], keys()[:, cut])) + bias()[None, :, None, :]
-            part = part.reshape(count * rows, part.shape[-1])
+    for f in range(2):
+        for keys, _, _ in parts:
+            part = matmul_nt(masked[f], keys(f))
             scores[f].append(part)
             top = jnp.max(part, axis=1, keepdims=True)
             tops[f] = top if tops[f] is None else jnp.maximum(tops[f], top)
     for f, cut in enumerate(cuts):
-        for i, (_, values, _, times) in enumerate(parts):
+        for i, (_, values, times) in enumerate(parts):
             weights = jnp.exp(scores[f][i] - tops[f])
             if times is not None:
                 weights = (by_group(weights) * times()[None, :, None, :]).reshape(weights.shape)
@@ -93,7 +98,10 @@
 
 def project(features, w_key, w_value, keys, values, start):
     rows = pl.ds(start, features.shape[0])
-    keys[rows, :] = matmul(features, w_key[...]).astype(keys.dtype)
+    lanes = keys.shape[1] // 4
+    made = matmul(features, w_key[...]).astype(keys.dtype)
+    keys[rows, pl.ds(0, lanes)] = made[:, :lanes]
+    keys[rows, pl.ds(2 * lanes, lanes)] = made[:, lanes:]
     values[rows, :] = matmul(features, w_value[...]).astype(values.dtype)
 
 
@@ -117,13 +125,21 @@
             arrival = jnp.where(is_swapped, named["ring"][...], ref[...])
         else:
             arrival = ref[...]
+        row, repeats = BIAS_ROW[kind], TIMES_ROW.get(kind)
         project(arrival, w_key, w_value, keys, values, start)
+        lanes = keys.shape[1] // 4
+        lane = lax.broadcasted_iota(jnp.int32, (1, lanes), 1)
+        for b in range(count // block_rows):
+            mask = jnp.zeros((1, lanes), jnp.float32)
+            for g in range(groups):
+                mask = jnp.where(lane == g, bias[row, g : g + 1, b * block_rows : b * block_rows + 1], mask)
+            mask = jnp.broadcast_to(mask.astype(keys.dtype), (block_rows, lanes))
+            for f in range(2):
+                keys[pl.ds(start + b * block_rows, block_rows), pl.ds((2 * f + 1) * lanes, lanes)] = mask
         where = pl.ds(start, count)
-        row, repeats = BIAS_ROW[kind], TIMES_ROW.get(kind)
         parts.append((
-            lambda where=where: keys[where, :],
+            lambda f, where=where: keys[where, pl.ds(f * keys.shape[1] // 2, keys.shape[1] // 2)],
             lambda where=where: values[where, :],
-            lambda row=row, count=count: bias[row, :, :count],
             None if repeats is None else lambda repeats=repeats: times[repeats],
         ))
         start += count
@@ -232,7 +248,7 @@
         return jax.ShapeDtypeStruct(shape, dtype)
 
     def pairs_of(total):
-        return [pltpu.VMEM((total, width), jnp.bfloat16)] * 2
+        return [pltpu.VMEM((total, 2 * width), jnp.bfloat16), pltpu.VMEM((total, width), jnp.bfloat16)]
 
     def exchange(matching):
         apart = matching_apart(peers, matching, match_total)

time: 14.6 us -> 14.6 us (level)
  no operation moved by 1% of the time
where the time goes in v11:
time: 14.6 us; the launch traced here: 14.5 us
  Pallas kernels  7.26 us (50%)
  starting transfers between devices  6.68 us (46%)
  waiting for transfers between devices  0.52 us (4%)
    ppermute x1, starting transfers between devices, shards(): lax.ppermute(features, 'dom', list(enumerate(far_of)))  3.66 us
    pallas_call x1, Pallas kernels, shards(): pl.pallas_call(first_kernel, out_shape=(array(rows, width), *[array(width...  2.92 us
    pallas_call x1, Pallas kernels, shards(): pl.pallas_call(last_kernel, out_shape=array(rows, width, dtype=features.d...  2.67 us
    ppermute x1, starting transfers between devices, shards(): lax.ppermute(features, 'dom', list(enumerate(ring_of)))  2.52 us
    pallas_call x1, Pallas kernels, shards(): pl.pallas_call(functools.partial(middle_kernel, kinds, swapped), out_shap...  1.67 us
    ppermute x1, starting transfers between devices, shards(): lax.ppermute(features, 'dom', list(enumerate(core_of)))  0.45 us
    ppermute x1, waiting for transfers between devices, shards(): lax.ppermute(features, 'dom', list(enumerate(far_of)))  0.3 us
  transfers between devices with their start and end apart: 5, of which 3 were waited for; matrix products, arithmetic and copies ran while one was open for 0% of the time, Pallas kernels for 32%

profile of v11, /device:TPU:0, one launch (start us, length us, event | category | flops | bytes accessed | tf_op | source)
XLA Modules:
  0.0 14.5 jit_solution(13510543794799110345)
XLA Ops:
  0.0 0.5 %collective-permute-start.2 = (bf16[256,256]{1,0:T(8,128)(2,1)}, bf16[256,256]{1,0:T(8,128)(2,1)S(1)}, u32[]{:S(2)}, u32[]{:S(2)}) collective-permute-start(bf16[256,256]{1,0:T(8,128)(2,1)} %features.1), channel_id=1, source_target_pairs={{0,1},{1,0},{2,3},{3,2},{4,5},{5,4},{6,7},{7,6},{8,9},{9,8},{10,11... | collective-permute-start | bytes 393224 | tf_op jit(solution)/shard_map/ppermute | solution.py:271
  0.5 2.5 %collective-permute-start.1 = (bf16[256,256]{1,0:T(8,128)(2,1)}, bf16[256,256]{1,0:T(8,128)(2,1)S(1)}, u32[]{:S(2)}, u32[]{:S(2)}) collective-permute-start(bf16[256,256]{1,0:T(8,128)(2,1)} %features.1), channel_id=1, source_target_pairs={{0,4},{1,2},{2,1},{3,7},{4,3},{5,6},{6,5},{7,8},{8,12},{9,10},{10,... | collective-permute-start | bytes 393224 | tf_op jit(solution)/shard_map/ppermute | solution.py:275
  3.0 3.7 %collective-permute-start.3 = (bf16[256,256]{1,0:T(8,128)(2,1)}, bf16[256,256]{1,0:T(8,128)(2,1)S(1)}, u32[]{:S(2)}, u32[]{:S(2)}) collective-permute-start(bf16[256,256]{1,0:T(8,128)(2,1)} %features.1), channel_id=1, source_target_pairs={{0,31},{1,5},{2,6},{3,4},{4,0},{5,1},{6,2},{7,3},{8,7},{9,13},{10,... | collective-permute-start | bytes 393224 | tf_op jit(solution)/shard_map/ppermute | solution.py:273
  6.6 0.0 collective-permute-start
  6.6 0.1 collective-permute-start.4
  6.7 0.0 collective-permute-done.2.refs_0_
  6.7 2.9 %first.1 = (bf16[256,256]{1,0:T(8,128)(2,1)S(1)}, bf16[256,256]{1,0:T(8,128)(2,1)S(1)}, bf16[256,256]{1,0:T(8,128)(2,1)S(1)}, bf16[256,256]{1,0:T(8,128)(2,1)S(1...) custom-call(bf16[256,256]{1,0:T(8,128)(2,1)} %features.1, ...), custom_call_target="tpu_custom_call" | custom-call | tf_op jit(solution)/shard_map/first/pallas_call | solution.py:291
  9.6 0.2 %collective-permute-done.1.refs_0_ = bf16[256,256]{1,0:T(8,128)(2,1)S(1)} collective-permute-done((bf16[256,256]{1,0:T(8,128)(2,1)}, bf16[256,256]{1,0:T(8,128)(2,1)S(1)}, u32[]{:S(2)}, u32[]{:S(2)}) %collective-permute-start.1) | collective-permute-done | bytes 131104 | tf_op jit(solution)/shard_map/ppermute | solution.py:275
  9.8 0.3 %collective-permute-done.3.refs_1_ = bf16[256,256]{1,0:T(8,128)(2,1)S(1)} collective-permute-done((bf16[256,256]{1,0:T(8,128)(2,1)}, bf16[256,256]{1,0:T(8,128)(2,1)S(1)}, u32[]{:S(2)}, u32[]{:S(2)}) %collective-permute-start.3) | collective-permute-done | bytes 131104 | tf_op jit(solution)/shard_map/ppermute | solution.py:273
  10.1 1.7 %ring_y.1 = (f32[256,256]{1,0:T(8,128)S(1)}, f32[256,256]{1,0:T(8,128)S(1)}, f32[256,256]{1,0:T(8,128)S(1)}) custom-call(bf16[256,256]{1,0:T(8,128)(2,1)S(1)} %collective-permute-done.1.refs_0_, bf16[256,256]{1,0:T(8,128)(2,1)S(1)} %collective-permute-done.3.refs_1_, bf16[256,256]{1,0:T(8,128)(2,1)S(1)} %get-tuple-element.44.refs_2_, ...), custom_call_target="tpu_custom_call" | custom-call | tf_op jit(solution)/shard_map/ring_y/pallas_call | solution.py:311
  11.8 0.1 collective-permute-done.refs_0_
  11.8 0.0 collective-permute-done.4.refs_1_
  11.8 2.7 %last.1 = bf16[256,256]{1,0:T(8,128)(2,1)} custom-call(bf16[256,256]{1,0:T(8,128)(2,1)S(1)} %collective-permute-done.refs_0_, bf16[256,256]{1,0:T(8,128)(2,1)S(1)} %collective-permute-done.4.refs_1_, bf16[256,256]{1,0:T(8,128)(2,1)S(1)} %get-tuple-element.44.refs_2_, bf16[256,256]{1,0:T(8,128)(2,1)S(1)} %get-tuple-element.45.refs_3_, ...), custom_call_target="tpu_custom_call" | custom-call | tf_op jit(solution)/shard_map/last/pallas_call | solution.py:321
Async XLA Ops:
  0.0 6.7 %collective-permute-start.2 = (bf16[256,256]{1,0:T(8,128)(2,1)}, bf16[256,256]{1,0:T(8,128)(2,1)S(1)}, u32[]{:S(2)}, u32[]{:S(2)}) collective-permute-start(bf16[256,256]{1,0:T(8,128)(2,1)} %features.1), channel_id=1, source_target_pairs={{0,1},{1,0},{2,3},{3,2},{4,5},{5,4},{6,7},{7,6},{8,9},{9,8},{10,11... | collective-permute-start | bytes 393224 | tf_op jit(solution)/shard_map/ppermute | solution.py:271
  0.5 9.3 %collective-permute-start.1 = (bf16[256,256]{1,0:T(8,128)(2,1)}, bf16[256,256]{1,0:T(8,128)(2,1)S(1)}, u32[]{:S(2)}, u32[]{:S(2)}) collective-permute-start(bf16[256,256]{1,0:T(8,128)(2,1)} %features.1), channel_id=1, source_target_pairs={{0,4},{1,2},{2,1},{3,7},{4,3},{5,6},{6,5},{7,8},{8,12},{9,10},{10,... | collective-permute-start | bytes 393224 | tf_op jit(solution)/shard_map/ppermute | solution.py:275
  3.0 7.1 %collective-permute-start.3 = (bf16[256,256]{1,0:T(8,128)(2,1)}, bf16[256,256]{1,0:T(8,128)(2,1)S(1)}, u32[]{:S(2)}, u32[]{:S(2)}) collective-permute-start(bf16[256,256]{1,0:T(8,128)(2,1)} %features.1), channel_id=1, source_target_pairs={{0,31},{1,5},{2,6},{3,4},{4,0},{5,1},{6,2},{7,3},{8,7},{9,13},{10,... | collective-permute-start | bytes 393224 | tf_op jit(solution)/shard_map/ppermute | solution.py:273
  6.6 5.2 %collective-permute-start = (bf16[256,256]{1,0:T(8,128)(2,1)}, bf16[256,256]{1,0:T(8,128)(2,1)S(1)}, u32[]{:S(2)}, u32[]{:S(2)}) collective-permute-start(bf16[256,256]{1,0:T(8,128)(2,1)} %features.1), channel_id=1, source_target_pairs={{0,8},{1,9},{2,10},{3,11},{4,12},{5,13},{6,14},{7,15},{8,0},{9,1},... | collective-permute-start | bytes 393224 | tf_op jit(solution)/shard_map/ppermute | solution.py:255
  6.6 5.2 %collective-permute-start.4 = (bf16[256,256]{1,0:T(8,128)(2,1)}, bf16[256,256]{1,0:T(8,128)(2,1)S(1)}, u32[]{:S(2)}, u32[]{:S(2)}) collective-permute-start(bf16[256,256]{1,0:T(8,128)(2,1)} %features.1), channel_id=1, source_target_pairs={{0,2},{1,3},{2,0},{3,1},{4,6},{5,7},{6,4},{7,5},{8,10},{9,11},{10,... | collective-permute-start | bytes 393224 | tf_op jit(solution)/shard_map/ppermute | solution.py:272
